TPU v7x, 128 devices: a whole 4x4x4 slice. The times are simulated.
128 devices in a mesh: chan: 8 (over z_hi, y), bl: 16 (over x, z_lo, core).
Axes of the slice: x: 4, y: 4, z: 4 (z_hi: 2, z_lo: 2; z = z_hi * 2 + z_lo), core: 2. Of those that a mesh axis runs over, the one named last changes fastest.
Arguments:
- coherency: bfloat16 [8, 32, 8, 16384], P('chan', None, None, 'bl'), may hold values from -1.5 to 1.5
- visibilities: float32 [8, 8, 16384], P('chan', None, 'bl'), may hold values from -6 to 6
- station_pairs: int32 [2, 16384], P(None, 'bl'), may hold values from 0 to 511, as said below
- gains: float32 [8, 32, 8, 512], P('chan', None, None, 'bl'), may hold values from -4 to 4
- duals: float32 [8, 32, 8, 512], P('chan', None, None, 'bl'), may hold values from -5 to 5
- poly: float32 [32, 8, 4, 512], P(None, None, None, 'bl'), may hold values from -4 to 4
- penalty: float32 [32], replicated, may hold values from 2 to 20
Outputs:
- gains_out: float32 [8, 32, 8, 512], P('chan', None, None, 'bl')
- duals_out: float32 [8, 32, 8, 512], P('chan', None, None, 'bl')
- poly_out: float32 [32, 8, 4, 512], P(None, None, None, 'bl')
Inputs may be any that keep to these rules, and one draw needn't show every extreme that they name: `station_pairs`: each row names two different stations; station 0 and station 512 - 1 appear in every draw.
All inputs are finite; a program needn't handle non-finite values.
Results may differ from a plain program's by a relative error of at most 0.00045.
Values sent between devices are 32-bit elements; how exact they have to be, the bound alone decides.
No kernel may reach another device: no remote copies, remote signals or barrier semaphores. Data moves between devices by JAX's collectives and lax.ppermute only.
A program may use at most 64 MiB of HBM per device.

v0:
```python
import jax
import jax.numpy as jnp
from jax import lax
from jax.sharding import PartitionSpec as P

GN_STEPS = 2
ADMM_ITERS = 2


def complex_product(left, right):
    real_parts = []
    imag_parts = []
    for row in (0, 1):
        for col in (0, 1):
            lr0 = left[..., 2 * row, :]
            lr1 = left[..., 2 * row + 1, :]
            li0 = left[..., 4 + 2 * row, :]
            li1 = left[..., 5 + 2 * row, :]
            rr0 = right[..., col, :]
            rr1 = right[..., 2 + col, :]
            ri0 = right[..., 4 + col, :]
            ri1 = right[..., 6 + col, :]
            real_parts.append(lr0 * rr0 - li0 * ri0 + lr1 * rr1 - li1 * ri1)
            imag_parts.append(lr0 * ri0 + li0 * rr0 + lr1 * ri1 + li1 * rr1)
    return jnp.stack(real_parts + imag_parts, axis=-2)


def conj_transpose(matrix):
    order = [0, 2, 1, 3]
    real_parts = [matrix[..., i, :] for i in order]
    imag_parts = [-matrix[..., 4 + i, :] for i in order]
    return jnp.stack(real_parts + imag_parts, axis=-2)


def hermitian_square(matrix):
    full = complex_product(matrix, conj_transpose(matrix))
    return jnp.stack([full[..., 0, :], full[..., 3, :], full[..., 1, :], full[..., 5, :]], axis=-2)


def basis_table(count):
    place = (2.0 * jnp.arange(count, dtype=jnp.float32) + 1.0) / count - 1.0
    return jnp.stack(
        [
            jnp.ones_like(place),
            place,
            1.5 * place * place - 0.5,
            2.5 * place * place * place - 1.5 * place,
        ],
        axis=1,
    )


def channel_sums(gain_one, coh_one, vis_one, first, second, stations):
    gain_first = jnp.take(gain_one, first, axis=2)
    gain_second = jnp.take(gain_one, second, axis=2)
    z_first = complex_product(coh_one, conj_transpose(gain_second))
    model = complex_product(gain_first, z_first)
    resid = vis_one - jnp.sum(model, axis=0)
    per_dir = resid[None] + model
    z_second = complex_product(conj_transpose(coh_one), conj_transpose(gain_first))
    numer_first = complex_product(per_dir, conj_transpose(z_first))
    numer_second = complex_product(conj_transpose(per_dir), conj_transpose(z_second))
    side_first = jnp.concatenate([numer_first, hermitian_square(z_first)], axis=1)
    side_second = jnp.concatenate([numer_second, hermitian_square(z_second)], axis=1)
    stacked = jnp.concatenate([side_first, side_second], axis=2)
    dir_count = stacked.shape[0]
    sum_count = stacked.shape[1]
    flat_rows = stacked.reshape(dir_count * sum_count, stacked.shape[2])
    index = jnp.concatenate([first, second])
    summed = jax.ops.segment_sum(flat_rows.T, index, num_segments=stations)
    return summed.T.reshape(dir_count, sum_count, stations)


def all_channels(gain_full, coherency, visibilities, first, second):
    stations = gain_full.shape[3]

    def one_channel(items):
        gain_one, coh_one, vis_one = items
        return channel_sums(gain_one, coh_one.astype(jnp.float32), vis_one, first, second, stations)

    return lax.map(one_channel, (gain_full, coherency, visibilities))


def gain_update(gain_now, sums, target, penalty):
    half_rho = 0.5 * penalty[None, :, None]
    diag_first = sums[:, :, 8, :] + half_rho
    diag_second = sums[:, :, 9, :] + half_rho
    off_real = sums[:, :, 10, :]
    off_imag = sums[:, :, 11, :]
    determinant = diag_first * diag_second - off_real * off_real - off_imag * off_imag
    zeros = jnp.zeros_like(diag_first)
    inverse = (
        jnp.stack(
            [diag_second, -off_real, -off_real, diag_first, zeros, -off_imag, off_imag, zeros],
            axis=2,
        )
        / determinant[:, :, None, :]
    )
    solved = complex_product(sums[:, :, :8, :] + target, inverse)
    return 0.5 * (gain_now + solved)


def poly_solve(chol, total):
    shape = total.shape
    moved = jnp.moveaxis(total, 2, 0).reshape(shape[2], -1)
    half = lax.linalg.triangular_solve(chol, moved, left_side=True, lower=True)
    whole = lax.linalg.triangular_solve(chol, half, left_side=True, lower=True, transpose_a=True)
    return jnp.moveaxis(whole.reshape(shape[2], shape[0], shape[1], shape[3]), 0, 2)


def local(coherency, visibilities, station_pairs, gains, duals, poly, penalty):
    local_count = gains.shape[3]
    chan_local = gains.shape[0]
    table_all = basis_table(chan_local * lax.axis_size("chan"))
    gram = jnp.dot(table_all.T, table_all, precision=lax.Precision.HIGHEST)
    chol = jnp.linalg.cholesky(gram)
    table = lax.dynamic_slice_in_dim(table_all, lax.axis_index("chan") * chan_local, chan_local, 0)
    offset = lax.axis_index("bl") * local_count
    rho_four = penalty[None, :, None, None]
    first = station_pairs[0]
    second = station_pairs[1]
    local_gains = gains
    full_gains = lax.all_gather(gains, "bl", axis=3, tiled=True)
    for outer in range(ADMM_ITERS):
        fitted = jnp.einsum("ft,kctn->fkcn", table, poly, precision=lax.Precision.HIGHEST)
        target = 0.5 * rho_four * fitted - 0.5 * duals
        target_full = lax.all_gather(target, "bl", axis=3, tiled=True)
        for inner in range(GN_STEPS):
            partial_sums = all_channels(full_gains, coherency, visibilities, first, second)
            sums = lax.psum(partial_sums, "bl")
            full_gains = gain_update(full_gains, sums, target_full, penalty)
        local_gains = lax.dynamic_slice_in_dim(full_gains, offset, local_count, 3)
        moments = jnp.einsum(
            "ft,fkcn->kctn", table, duals + rho_four * local_gains, precision=lax.Precision.HIGHEST
        )
        total = lax.psum(moments, "chan")
        poly = poly_solve(chol, total)
        fitted = jnp.einsum("ft,kctn->fkcn", table, poly, precision=lax.Precision.HIGHEST)
        duals = duals + rho_four * (local_gains - fitted)
    return (local_gains, duals, poly)


def solution(mesh):
    in_specs = (
        P("chan", None, None, "bl"),
        P("chan", None, "bl"),
        P(None, "bl"),
        P("chan", None, None, "bl"),
        P("chan", None, None, "bl"),
        P(None, None, None, "bl"),
        P(),
    )
    out_specs = (
        P("chan", None, None, "bl"),
        P("chan", None, None, "bl"),
        P(None, None, None, "bl"),
    )
    return jax.shard_map(local, mesh=mesh, in_specs=in_specs, out_specs=out_specs, check_vma=False)
```

profile of v0, /device:TPU:1, one launch (start us, length us, event | category | flops | bytes accessed | tf_op | source)
XLA Modules:
  0.0 1019.4 jit_solution(7257423283331238146)
XLA Ops:
  9.7 32.2 %all_gather.9 = f32[1,32,8,512]{1,2,0,3:T(8,128)} all-gather(f32[1,32,8,32]{1,2,0,3:T(8,128)S(1)} %copy.1405), channel_id=1, replica_groups=mesh['chan'=8,'bl'=16] {'bl'}, dimensions={3}, use_global_device_ids=true | all-gather | bytes 557056 | tf_op jit(solution)/shard_map/all_gather | solution.py:123
  41.9 9.7 gather_fusion
  51.6 3.6 copy.1406
  55.3 9.7 gather_fusion.1
  65.0 3.7 copy.1408
  76.3 1.8 copy.1410
  78.1 2.0 reduce_sum.48
  80.0 1.8 copy.1469
  81.8 2.0 fusion.3
  83.8 1.8 copy.1411
  89.9 3.9 copy.1412
  93.8 4.7 reshape.1380
  98.5 3.5 copy.1413
  102.0 13.3 %scatter_custom_fusion = f32[512,384]{1,0:T(8,128)S(1)} fusion(s32[2048]{0:T(1024)} %pad_add_fusion, f32[2048,384]{1,0:T(8,128)} %copy.1413, f32[]{:T(128)} %constant.123.clone.1), kind=kCustom, calls=%fused_computation.55 | custom fusion | flops 786432 | bytes 786944 | tf_op jit(solution)/shard_map/while/body/eval_jaxpr/scatter-add | solution.py:70
  117.1 2.4 copy.1417
  120.9 37.8 %all_gather.10 = f32[1,32,8,512]{1,2,0,3:T(8,128)} all-gather(f32[1,32,8,32]{1,2,0,3:T(8,128)S(1)} %copy.1415), channel_id=1, replica_groups=mesh['chan'=8,'bl'=16] {'bl'}, dimensions={3}, use_global_device_ids=true | all-gather | bytes 557056 | tf_op jit(solution)/shard_map/all_gather | solution.py:127
  158.6 2.4 copy.1416
  161.0 78.7 %all-reduce.7.cloned.1.call-done = f32[1,32,12,512]{3,2,1,0:T(8,128)} async-done(((f32[1,32,12,512]{3,2,1,0:T(8,128)}), f32[1,32,12,512]{3,2,1,0:T(8,128)}) %all-reduce.7.cloned.1.call-update) | async-done | bytes 786448 | tf_op jit(solution)/shard_map/psum | solution.py:130
  239.8 2.1 fusion.278
  247.1 2.0 copy.1418
  249.1 9.8 gather_fusion.2
  258.9 9.7 gather_fusion.3
  268.6 3.6 copy.1419
  273.6 3.6 copy.1421
  286.9 2.0 fusion.2
  293.7 3.9 copy.1425
  297.6 4.7 reshape.1382
  302.3 3.5 copy.1426
  305.8 24.6 %scatter_custom_fusion.1 = f32[512,384]{1,0:T(8,128)S(1)} fusion(s32[2048]{0:T(1024)} %pad_add_fusion, f32[2048,384]{1,0:T(8,128)} %copy.1426, f32[]{:T(128)} %constant.123.clone.1), kind=kCustom, calls=%fused_computation.53 | custom fusion | flops 786432 | bytes 786944 | tf_op jit(solution)/shard_map/while/body/eval_jaxpr/scatter-add | solution.py:70
  334.7 117.6 %all-reduce.9.cloned.1.call-done = f32[1,32,12,512]{3,2,1,0:T(8,128)} async-done(((f32[1,32,12,512]{3,2,1,0:T(8,128)}), f32[1,32,12,512]{3,2,1,0:T(8,128)}) %all-reduce.9.cloned.1.call-update) | async-done | bytes 786448 | tf_op jit(solution)/shard_map/psum | solution.py:130
  452.3 2.1 fusion.277
  459.4 1.6 stack.266
  461.1 2.0 copy.1429
  463.2 9.8 gather_fusion.4
  473.0 9.7 gather_fusion.5
  482.7 3.6 copy.1430
  487.7 4.0 copy.1432
  499.0 1.4 reduce_sum.52
  502.7 1.4 broadcast_add_fusion.1
  507.7 2.0 reshape.1385
  516.2 3.9 copy.1436
  520.1 4.9 reshape.1383
  524.9 3.5 copy.1437
  528.5 13.3 %scatter_custom_fusion.2 = f32[512,384]{1,0:T(8,128)S(1)} fusion(s32[2048]{0:T(1024)} %pad_add_fusion, f32[2048,384]{1,0:T(8,128)} %copy.1437, f32[]{:T(128)} %constant.123.clone.1), kind=kCustom, calls=%fused_computation.51 | custom fusion | flops 786432 | bytes 786944 | tf_op jit(solution)/shard_map/while/body/eval_jaxpr/scatter-add | solution.py:70
  543.2 46.1 %all-reduce.13.cloned.1.call-done = f32[4,8192]{1,0:T(4,128)} async-done(((f32[4,8192]{1,0:T(4,128)}), f32[4,8192]{1,0:T(4,128)}) %all-reduce.13.cloned.1.call-update) | async-done | bytes 131088 | tf_op jit(solution)/shard_map/psum | solution.py:136
  592.8 41.8 %all_gather.11 = f32[1,32,8,512]{1,2,0,3:T(8,128)} all-gather(f32[1,32,8,32]{1,2,0,3:T(8,128)S(1)} %copy.1442), channel_id=1, replica_groups=mesh['chan'=8,'bl'=16] {'bl'}, dimensions={3}, use_global_device_ids=true | all-gather | bytes 557056 | tf_op jit(solution)/shard_map/all_gather | solution.py:127
  634.6 2.4 copy.1443
  637.1 78.7 %all-reduce.11.cloned.1.call-done = f32[1,32,12,512]{3,2,1,0:T(8,128)} async-done(((f32[1,32,12,512]{3,2,1,0:T(8,128)}), f32[1,32,12,512]{3,2,1,0:T(8,128)}) %all-reduce.11.cloned.1.call-update) | async-done | bytes 786448 | tf_op jit(solution)/shard_map/psum | solution.py:130
  715.8 2.1 fusion.276
  724.4 1.6 stack.269
  726.2 2.0 copy.1444
  728.2 9.8 gather_fusion.6
  738.0 9.7 gather_fusion.7
  747.7 3.6 copy.1445
  752.7 3.6 copy.1447
  765.9 2.0 fusion
  772.8 3.9 copy.1451
  776.7 4.7 reshape.1387
  781.3 3.5 copy.1452
  784.9 13.5 %scatter_custom_fusion.3 = f32[512,384]{1,0:T(8,128)S(1)} fusion(s32[2048]{0:T(1024)} %pad_add_fusion, f32[2048,384]{1,0:T(8,128)} %copy.1452, f32[]{:T(128)} %constant.123.clone.1), kind=kCustom, calls=%fused_computation.49 | custom fusion | flops 786432 | bytes 786944 | tf_op jit(solution)/shard_map/while/body/eval_jaxpr/scatter-add | solution.py:70
  799.8 120.5 %all-reduce.15.cloned.1.call-done = f32[1,32,12,512]{3,2,1,0:T(8,128)} async-done(((f32[1,32,12,512]{3,2,1,0:T(8,128)}), f32[1,32,12,512]{3,2,1,0:T(8,128)}) %all-reduce.15.cloned.1.call-update) | async-done | bytes 786448 | tf_op jit(solution)/shard_map/psum | solution.py:130
  920.3 2.2 fusion.275
  928.7 79.6 %all-reduce.17.cloned.1.call-done = f32[4,8192]{1,0:T(4,128)} async-done(((f32[4,8192]{1,0:T(4,128)}), f32[4,8192]{1,0:T(4,128)}) %all-reduce.17.cloned.1.call-update) | async-done | bytes 131088 | tf_op jit(solution)/shard_map/psum | solution.py:136
  1008.3 1.4 fusion.260
  (340 shorter events, 105.1 us)
Async XLA Ops:
  7.2 112.5 %copy-start = (f32[32,8,4,32]{3,2,1,0:T(4,128)S(1)}, f32[32,8,4,32]{3,2,1,0:T(4,128)}, u32[]{:S(2)}) copy-start(f32[32,8,4,32]{3,2,1,0:T(4,128)} %param.18) | copy-start | bytes 393220
  7.2 232.6 %all-reduce.7.cloned.1.call-start = ((), (), s32[]{:S(2)}) async-start(), calls=%async_computation | async-start | bytes 2097152 | tf_op jit(solution)/shard_map/psum | solution.py:130
  8.6 60.4 %copy-start.36 = (pred[1024]{0:T(1024)(128)(4,1)}, pred[1024]{0:T(1024)(128)(4,1)S(1)}, u32[]{:S(2)}) copy-start(pred[1024]{0:T(1024)(128)(4,1)S(1)} %compare_and_fusion.1) | copy-start | bytes 3076
  8.7 268.6 %copy-start.33 = (pred[1024]{0:T(1024)(128)(4,1)}, pred[1024]{0:T(1024)(128)(4,1)S(1)}, u32[]{:S(2)}) copy-start(pred[1024]{0:T(1024)(128)(4,1)S(1)} %compare_and_fusion) | copy-start | bytes 3076
  65.0 3.7 copy-start.31
  68.7 1.2 copy-start.21
  68.7 1.5 copy-start.22
  72.0 3.6 copy-start.5
  87.1 0.9 copy-start.6
  116.7 2.8 copy-start.43
  116.7 335.6 %all-reduce.9.cloned.1.call-start = ((), (), s32[]{:S(2)}) async-start(), calls=%async_computation.1 | async-start | bytes 2097152 | tf_op jit(solution)/shard_map/psum | solution.py:130
  117.1 3.6 copy-start.27
  119.5 127.5 %copy-start.17 = (f32[1,32,8,512]{3,2,1,0:T(8,128)}, f32[1,32,8,512]{3,2,1,0:T(8,128)S(1)}, u32[]{:S(2)}) copy-start(f32[1,32,8,512]{3,2,1,0:T(8,128)S(1)} %copy.1417) | copy-start | bytes 1572868
  119.5 332.8 %copy-start.40 = (f32[32]{0:T(128)}, f32[32]{0:T(128)S(1)}, u32[]{:S(2)}) copy-start(f32[32]{0:T(128)S(1)} %broadcast_multiply_fusion) | copy-start | bytes 388
  161.0 82.9 %copy-start.13 = (f32[1,32,8,512]{3,2,1,0:T(8,128)}, f32[1,32,8,512]{3,2,1,0:T(8,128)S(1)}, u32[]{:S(2)}) copy-start(f32[1,32,8,512]{3,2,1,0:T(8,128)S(1)} %copy.1416) | copy-start | bytes 1572868
  241.9 212.6 %copy-start.11 = (f32[1,32,1,512]{3,2,1,0:T(1,128)}, f32[1,32,1,512]{3,2,1,0:T(1,128)S(1)}, u32[]{:S(2)}) copy-start(f32[1,32,1,512]{3,2,1,0:T(1,128)S(1)} %stack.261) | copy-start | bytes 196612
  247.0 2.1 copy-start.19
  268.6 3.6 copy-start.37
  331.8 123.6 %copy-start.14 = (f32[1,32,8,512]{3,2,1,0:T(8,128)S(1)}, f32[1,32,8,512]{3,2,1,0:T(8,128)}, u32[]{:S(2)}) copy-start(f32[1,32,8,512]{3,2,1,0:T(8,128)} %copy-done.13) | copy-start | bytes 1572868
  331.8 257.5 %all-reduce.13.cloned.1.call-start = ((), (), s32[]{:S(2)}) async-start(), calls=%async_computation.3 | async-start | bytes 262144 | tf_op jit(solution)/shard_map/psum | solution.py:136
  458.1 2.8 copy-start.18
  458.1 2.8 copy-start.20
  461.1 11.9 %copy-start.8 = (f32[1,32,8,512]{3,2,1,0:T(8,128)}, f32[1,32,8,512]{3,2,1,0:T(8,128)S(1)}, u32[]{:S(2)}) copy-start(f32[1,32,8,512]{3,2,1,0:T(8,128)S(1)} %add_multiply_fusion.1) | copy-start | bytes 1572868
  482.7 3.6 copy-start.38
  487.6 10.6 %copy-start.2 = (f32[32,8,1024]{2,0,1:T(8,128)}, f32[32,8,1024]{2,0,1:T(8,128)S(1)}, u32[]{:S(2)}) copy-start(f32[32,8,1024]{2,0,1:T(8,128)S(1)} %select_bitcast_fusion.3) | copy-start | bytes 3145732
  487.7 4.0 copy-start.34
  499.0 1.6 copy-start.7
  502.7 2.1 copy-start.3
  504.8 0.9 copy-start.28
  504.8 0.9 copy-start.44
  504.8 2.0 copy-start.47
  509.7 206.1 %all-reduce.11.cloned.1.call-start = ((), (), s32[]{:S(2)}) async-start(), calls=%async_computation.2 | async-start | bytes 2097152 | tf_op jit(solution)/shard_map/psum | solution.py:130
  511.2 2.2 copy-start.4
  511.2 2.2 copy-start.26
  513.3 0.9 copy-start.10
  513.3 1.5 copy-start.25
  543.1 49.3 %copy-start.9 = (f32[1,32,8,512]{3,2,1,0:T(8,128)S(1)}, f32[1,32,8,512]{3,2,1,0:T(8,128)}, u32[]{:S(2)}) copy-start(f32[1,32,8,512]{3,2,1,0:T(8,128)} %copy-done.8) | copy-start | bytes 1572868
  543.1 49.3 %copy-start.29 = (f32[1,32,8,32]{3,2,1,0:T(8,128)S(1)}, f32[1,32,8,32]{3,2,1,0:T(8,128)}, u32[]{:S(2)}) copy-start(f32[1,32,8,32]{3,2,1,0:T(8,128)} %param.17) | copy-start | bytes 98308
  543.1 49.3 %copy-start.41 = (f32[32]{0:T(128)S(1)}, f32[32]{0:T(128)}, u32[]{:S(2)}) copy-start(f32[32]{0:T(128)} %copy-done.40) | copy-start | bytes 388
  543.2 49.3 %copy-start.45 = (f32[32]{0:T(128)S(1)}, f32[32]{0:T(128)}, u32[]{:S(2)}) copy-start(f32[32]{0:T(128)} %param.19) | copy-start | bytes 388
  543.2 377.1 %all-reduce.15.cloned.1.call-start = ((), (), s32[]{:S(2)}) async-start(), calls=%async_computation.4 | async-start | bytes 2097152 | tf_op jit(solution)/shard_map/psum | solution.py:130
  634.6 83.3 %copy-start.12 = (f32[1,32,1,512]{3,2,1,0:T(1,128)S(1)}, f32[1,32,1,512]{3,2,1,0:T(1,128)}, u32[]{:S(2)}) copy-start(f32[1,32,1,512]{3,2,1,0:T(1,128)} %copy-done.11) | copy-start | bytes 196612
  637.1 83.3 %copy-start.15 = (f32[1,32,8,512]{3,2,1,0:T(8,128)}, f32[1,32,8,512]{3,2,1,0:T(8,128)S(1)}, u32[]{:S(2)}) copy-start(f32[1,32,8,512]{3,2,1,0:T(8,128)S(1)} %copy.1443) | copy-start | bytes 1572868
  726.1 11.9 %copy-start.23 = (f32[1,32,8,512]{3,2,1,0:T(8,128)}, f32[1,32,8,512]{3,2,1,0:T(8,128)S(1)}, u32[]{:S(2)}) copy-start(f32[1,32,8,512]{3,2,1,0:T(8,128)S(1)} %add_multiply_fusion) | copy-start | bytes 1572868
  747.7 3.6 copy-start.39
  752.7 3.7 copy-start.35
  798.6 121.7 %copy-start.42 = (f32[32]{0:T(128)S(1)}, f32[32]{0:T(128)}, u32[]{:S(2)}) copy-start(f32[32]{0:T(128)} %copy-done.40) | copy-start | bytes 388
  799.8 123.6 %copy-start.16 = (f32[1,32,8,512]{3,2,1,0:T(8,128)S(1)}, f32[1,32,8,512]{3,2,1,0:T(8,128)}, u32[]{:S(2)}) copy-start(f32[1,32,8,512]{3,2,1,0:T(8,128)} %copy-done.15) | copy-start | bytes 1572868
  799.8 208.6 %all-reduce.17.cloned.1.call-start = ((), (), s32[]{:S(2)}) async-start(), calls=%async_computation.5 | async-start | bytes 262144 | tf_op jit(solution)/shard_map/psum | solution.py:136
  920.3 3.1 copy-start.30
  924.4 2.1 copy-start.46
  924.4 3.2 copy-start.48
  927.6 84.0 %copy-start.32 = (f32[1,32,8,32]{3,2,1,0:T(8,128)}, f32[1,32,8,32]{3,2,1,0:T(8,128)S(1)}, u32[]{:S(2)}) copy-start(f32[1,32,8,32]{3,2,1,0:T(8,128)S(1)} %get-tuple-element.86) | copy-start | bytes 98308
  1008.3 4.1 copy-start.1
  1010.6 1.8 copy-start.24
Sparse Core Ops, SparseCore 0:
  116.8 122.9 all-reduce.6
  331.9 120.3 all-reduce.8
  509.8 79.4 all-reduce.12
  591.8 123.9 all-reduce.10
  799.9 120.3 all-reduce.14
  928.8 79.4 all-reduce.16
where the time goes:
time: 1030 us; the launch traced here: 1020 us
  waiting for transfers between devices  521 us (51%)
  local copies, waits for them, and re-layouts  204 us (20%)
  other arithmetic  159 us (15%)
  blocking collectives  112 us (11%)
  between operations  16 us (2%)
    psum x4, waiting for transfers between devices, local(): sums = lax.psum(partial_sums, 'bl')  396 us
    psum x2, waiting for transfers between devices, local(): total = lax.psum(moments, 'chan')  126 us
    all_gather x2, blocking collectives, local(): target_full = lax.all_gather(target, 'bl', axis=3, tiled=True)  79.6 us
    scatter-add x4, other arithmetic, channel_sums(): summed = jax.ops.segment_sum(flat_rows.T, index, num_segments=stations)  64.8 us
    gather x8, local copies, waits for them, and re-layouts, channel_sums(): gain_second = jnp.take(gain_one, second, axis=2)  53.8 us
    gather x8, local copies, waits for them, and re-layouts, channel_sums(): gain_first = jnp.take(gain_one, first, axis=2)  53.7 us
    all_gather x1, blocking collectives, local(): full_gains = lax.all_gather(gains, 'bl', axis=3, tiled=True)  32.2 us
    unnamed x108, other arithmetic  32.2 us
  transfers between devices with their start and end apart: 6, of which 6 were waited for; matrix products, arithmetic and copies ran while one was open for 5% of the time, Pallas kernels for 0%

commit v1 on v0

v1 whole, which is shorter than its diff:
```python
import functools

import jax
import jax.numpy as jnp
import numpy as np
from jax import lax
from jax.experimental import pallas as pl
from jax.experimental.pallas import tpu as pltpu
from jax.sharding import Mesh, PartitionSpec as P


CHANNELS = 8
TERMS = 4
ROWS = 1024
BLOCK = 256
STATIONS = 512
F32 = jnp.float32
BF16 = jnp.bfloat16
CORE_SWAP = [(0, 1), (1, 0)]
VMEM_BYTES = 24 * 1024 * 1024


def consensus_tables():
    place = (2.0 * np.arange(CHANNELS) + 1.0) / CHANNELS - 1.0
    basis = np.stack(
        [np.ones_like(place), place, 1.5 * place**2 - 0.5, 2.5 * place**3 - 1.5 * place], axis=1
    )
    solve = np.linalg.solve(basis.T @ basis, basis.T)
    return basis, solve, basis @ solve


def call(kernel, out_shapes, scratch=(), smem=(), n_in=0):
    in_specs = [
        pl.BlockSpec(memory_space=pltpu.SMEM if i in smem else pltpu.VMEM) for i in range(n_in)
    ]
    return pl.pallas_call(
        kernel,
        out_shape=[jax.ShapeDtypeStruct(s, d) for s, d in out_shapes],
        in_specs=in_specs,
        out_specs=[pl.BlockSpec(memory_space=pltpu.VMEM) for _ in out_shapes],
        scratch_shapes=list(scratch),
        compiler_params=pltpu.CompilerParams(vmem_limit_bytes=VMEM_BYTES),
    )


def lanes():
    return lax.broadcasted_iota(jnp.int32, (8, 128), 1)


def split_parts(x):
    high = x.astype(BF16)
    return high, (x - high.astype(F32)).astype(BF16)


def matrix(load):
    return [load(i) for i in range(4)], [load(4 + i) for i in range(4)]


def conj_t(m):
    re, im = m
    return [re[0], re[2], re[1], re[3]], [-im[0], -im[2], -im[1], -im[3]]


def product_nh(a, b):
    (ar, ai), (br, bi) = a, b
    re, im = [], []
    for i in (0, 1):
        for j in (0, 1):
            p, q, u, v = 2 * i, 2 * i + 1, 2 * j, 2 * j + 1
            re.append((ar[p] * br[u] + ai[p] * bi[u]) + (ar[q] * br[v] + ai[q] * bi[v]))
            im.append((ai[p] * br[u] - ar[p] * bi[u]) + (ai[q] * br[v] - ar[q] * bi[v]))
    return re, im


def product_hn(a, b):
    (ar, ai), (br, bi) = a, b
    re, im = [], []
    for i in (0, 1):
        for j in (0, 1):
            p, q, u, v = i, 2 + i, j, 2 + j
            re.append((ar[p] * br[u] + ai[p] * bi[u]) + (ar[q] * br[v] + ai[q] * bi[v]))
            im.append((ar[p] * bi[u] - ai[p] * br[u]) + (ar[q] * bi[v] - ai[q] * br[v]))
    return re, im


def product(a, b):
    (ar, ai), (br, bi) = a, b
    re, im = [], []
    for i in (0, 1):
        for j in (0, 1):
            p, q, u, v = 2 * i, 2 * i + 1, j, 2 + j
            re.append((ar[p] * br[u] - ai[p] * bi[u]) + (ar[q] * br[v] - ai[q] * bi[v]))
            im.append((ar[p] * bi[u] + ai[p] * br[u]) + (ar[q] * bi[v] + ai[q] * br[v]))
    return re, im


def square_nh(a):
    r, i = a
    return [
        (r[0] * r[0] + i[0] * i[0]) + (r[1] * r[1] + i[1] * i[1]),
        (r[2] * r[2] + i[2] * i[2]) + (r[3] * r[3] + i[3] * i[3]),
        (r[0] * r[2] + i[0] * i[2]) + (r[1] * r[3] + i[1] * i[3]),
        (i[0] * r[2] - r[0] * i[2]) + (i[1] * r[3] - r[1] * i[3]),
    ]


def square_hn(a):
    r, i = a
    return [
        (r[0] * r[0] + i[0] * i[0]) + (r[2] * r[2] + i[2] * i[2]),
        (r[1] * r[1] + i[1] * i[1]) + (r[3] * r[3] + i[3] * i[3]),
        (r[0] * r[1] + i[0] * i[1]) + (r[2] * r[3] + i[2] * i[3]),
        (r[0] * i[1] - i[0] * r[1]) + (r[2] * i[3] - i[2] * r[3]),
    ]


def prepare_kernel(
    coh, gains, duals, poly, penalty, tables,
    coh_keep, coh_send, state_keep, state_send, rho_a, rho_f,
    wide, thin,
):
    core = lax.axis_index("core")
    chan = lax.axis_index("chan")
    for t in range(ROWS // 128):
        cols = slice(t * 128, (t + 1) * 128)
        wide[t] = coh[:, :, cols].astype(F32).reshape(256, 128)
        for c in range(8):
            coh_keep[c * 16:(c + 1) * 16, cols] = wide[t, pl.ds(core * 128 + c, 16, stride=8), :]
            coh_send[c * 16:(c + 1) * 16, cols] = wide[t, pl.ds((1 - core) * 128 + c, 16, stride=8), :]
    row = lax.broadcasted_iota(jnp.int32, (8, 128), 0)
    lane = lanes()
    by_dir = jnp.zeros((8, 128), F32)
    half_dir = jnp.zeros((8, 128), F32)
    for q in range(4):
        for s in range(8):
            here = row == s
            by_dir = jnp.where(here & (lane // 32 == q), penalty[q * 8 + s], by_dir)
    for q in range(2):
        for s in range(8):
            here = row == s
            half_dir = jnp.where(here & (lane // 64 == q), penalty[core * 16 + q * 8 + s], half_dir)
    rho_a[...] = half_dir
    rho_f[...] = by_dir

    def pack(which):
        for c in range(8):
            for out, half in ((state_keep, core), (state_send, 1 - core)):
                total = None
                for h in range(2):
                    part = thin[pl.ds((half * 16 + h * 8) * 8 + c, 8, stride=8), :]
                    part = pltpu.roll(part, h * 64 + core * 32, 1)
                    total = part if total is None else total + part
                out[which * 64 + c * 8:which * 64 + (c + 1) * 8, :] = total

    thin[...] = jnp.zeros((256, 128), F32)
    thin[:, 0:32] = gains[...].reshape(256, 32)
    pack(0)
    thin[:, 0:32] = duals[...].reshape(256, 32)
    pack(1)
    fitted = poly[:, :, 0, :] * tables[chan, 0]
    for t in range(1, TERMS):
        fitted = fitted + poly[:, :, t, :] * tables[chan, t]
    thin[:, 0:32] = fitted.reshape(256, 32)
    pack(2)


def first_kernel(state_keep, state_recv, rho_a, gains, duals, target, spread):
    both = state_keep[...] + state_recv[...]
    gains[...] = both[0:64]
    duals[...] = both[64:128]
    for d in range(8):
        spread[d * 64:(d + 1) * 64, :] = both[0:64]
    half_rho = 0.5 * rho_a[...]
    for c in range(8):
        at = c * 8
        target[at:at + 8, :] = half_rho * both[128 + at:136 + at] - 0.5 * both[64 + at:72 + at]


def model_kernel(gathered, coh_own, coh_other, vis, pairs_own, pairs_other, z_ref, w_ref, s_ref, table, near, far):
    lane = lanes()
    low = lane < 64
    for c in range(8):
        for t in range(4):
            a = gathered[(2 * t) * 64 + c * 8:(2 * t) * 64 + c * 8 + 8, :]
            b = gathered[(2 * t + 1) * 64 + c * 8:(2 * t + 1) * 64 + c * 8 + 8, :]
            first = jnp.where(low, a, pltpu.roll(b, 64, 1))
            second = jnp.where(low, pltpu.roll(a, 64, 1), b)
            high, rest = split_parts(jnp.concatenate([first, second], axis=0))
            table[c * 16:(c + 1) * 16, t * 128:(t + 1) * 128] = high
            table[128 + c * 16:128 + (c + 1) * 16, t * 128:(t + 1) * 128] = rest
    station = lax.broadcasted_iota(jnp.int32, (STATIONS, BLOCK), 0)
    for j in range(2 * ROWS // BLOCK):
        own = j < ROWS // BLOCK
        coh = coh_own if own else coh_other
        pairs = pairs_own if own else pairs_other
        col = (j * BLOCK) % ROWS
        for side, dest in ((0, near), (1, far)):
            hot = (station == pairs[side:side + 1, col:col + BLOCK]).astype(F32).astype(BF16)
            both = jnp.dot(table[...], hot, preferred_element_type=F32)
            dest[j % 2] = both[:128] + both[128:]
        for l in range(BLOCK // 128):
            src = col + l * 128
            dst = j * BLOCK + l * 128
            gp = matrix(lambda i: near[j % 2, i * 16:(i + 1) * 16, l * 128:(l + 1) * 128])
            gq = matrix(lambda i: far[j % 2, i * 16:(i + 1) * 16, l * 128:(l + 1) * 128])
            cc = matrix(lambda i: coh[i * 16:(i + 1) * 16, src:src + 128])
            z = product_nh(cc, gq)
            w = product(gp, cc)
            m = product(gp, z)
            for i in range(8):
                z_ref[i * 16:(i + 1) * 16, dst:dst + 128] = z[i // 4][i % 4]
                w_ref[i * 16:(i + 1) * 16, dst:dst + 128] = w[i // 4][i % 4]
                total = -jnp.sum(m[i // 4][i % 4], axis=0, keepdims=True)
                if own:
                    total = total + vis[i:i + 1, src:src + 128]
                s_ref[i:i + 1, dst:dst + 128] = total


def sums_kernel(z_ref, w_ref, s_own, s_other, pairs_own, pairs_other, out, left, acc):
    station = lax.broadcasted_iota(jnp.int32, (STATIONS, BLOCK), 0)
    steps = 2 * ROWS // BLOCK
    for j in range(steps):
        own = j < steps // 2
        pairs = pairs_own if own else pairs_other
        col = (j * BLOCK) % ROWS
        slot = j % 2
        for l in range(BLOCK // 128):
            src = j * BLOCK + l * 128
            swapped = (src + ROWS) % (2 * ROWS)
            r = matrix(lambda i: s_own[i:i + 1, src:src + 128] + s_other[i:i + 1, swapped:swapped + 128])
            z = matrix(lambda i: z_ref[i * 16:(i + 1) * 16, src:src + 128])
            w = matrix(lambda i: w_ref[i * 16:(i + 1) * 16, src:src + 128])
            for side, (num, den) in enumerate(
                ((product_nh(r, z), square_nh(z)), (product_hn(r, w), square_hn(w)))
            ):
                at = side * BLOCK + l * 128
                for i, value in enumerate(num[0] + num[1] + den):
                    high, rest = split_parts(value)
                    left[slot, i * 16:(i + 1) * 16, at:at + 128] = high
                    left[slot, 192 + i * 16:192 + (i + 1) * 16, at:at + 128] = rest
        total = None
        for side in range(2):
            hot = (station == pairs[side:side + 1, col:col + BLOCK]).astype(F32).astype(BF16)
            part = lax.dot_general(
                left[slot, :, side * BLOCK:(side + 1) * BLOCK], hot,
                (((1,), (1,)), ((), ())), preferred_element_type=F32,
            )
            total = part if total is None else total + part
        if j == 0:
            acc[...] = total
        else:
            acc[...] += total
    low = lanes() < 64
    for c in range(12):
        for t in range(4):
            cols = slice(t * 128, (t + 1) * 128)
            at = c * 16
            v0 = acc[at:at + 8, cols] + acc[192 + at:192 + at + 8, cols]
            v1 = acc[at + 8:at + 16, cols] + acc[192 + at + 8:192 + at + 16, cols]
            out[(2 * t) * 96 + c * 8:(2 * t) * 96 + c * 8 + 8, :] = jnp.where(low, v0, pltpu.roll(v1, 64, 1))
            out[(2 * t + 1) * 96 + c * 8:(2 * t + 1) * 96 + c * 8 + 8, :] = jnp.where(low, pltpu.roll(v0, 64, 1), v1)


def updated(received, gains, target, rho):
    sums = []
    for c in range(12):
        parts = [received[d * 96 + c * 8:d * 96 + c * 8 + 8, :] for d in range(8)]
        while len(parts) > 1:
            parts = [parts[i] + parts[i + 1] for i in range(0, len(parts), 2)]
        sums.append(parts[0])
    half_rho = 0.5 * rho
    a, d, br, bi = sums[8] + half_rho, sums[9] + half_rho, sums[10], sums[11]
    scale = 0.5 / (a * d - br * br - bi * bi)
    n = [sums[i] + target[i] - half_rho * gains[i] for i in range(8)]
    result = [None] * 8
    for i in (0, 1):
        r0, r1, i0, i1 = n[2 * i], n[2 * i + 1], n[4 + 2 * i], n[5 + 2 * i]
        result[2 * i] = gains[2 * i] + scale * (r0 * d - (r1 * br + i1 * bi))
        result[4 + 2 * i] = gains[4 + 2 * i] + scale * (i0 * d - (i1 * br - r1 * bi))
        result[2 * i + 1] = gains[2 * i + 1] + scale * (r1 * a - (r0 * br - i0 * bi))
        result[5 + 2 * i] = gains[5 + 2 * i] + scale * (i1 * a - (i0 * br + r0 * bi))
    return result


def comps(ref):
    return [ref[c * 8:(c + 1) * 8, :] for c in range(8)]


def put(ref, values, base=0):
    for c in range(8):
        ref[base + c * 8:base + (c + 1) * 8, :] = values[c]


def update_kernel(received, gains, target, rho_a, gains_new, spread):
    new = updated(received, comps(gains), comps(target), rho_a[...])
    put(gains_new, new)
    for d in range(8):
        put(spread, new, d * 64)


def update_moment_kernel(received, gains, target, duals, rho_a, gains_new, spread, moment):
    rho = rho_a[...]
    new = updated(received, comps(gains), comps(target), rho)
    put(gains_new, new)
    old = comps(duals)
    whole = [old[c] + rho * new[c] for c in range(8)]
    for d in range(8):
        put(spread, new, d * 64)
        put(moment, whole, d * 64)


def fit(tables, row, moments, column):
    result = []
    for c in range(8):
        total = None
        for f in range(CHANNELS):
            part = tables[row, column + f] * moments[f * 64 + c * 8:f * 64 + c * 8 + 8, :]
            total = part if total is None else total + part
        result.append(total)
    return result


def update_consensus_kernel(received, gains, moments, duals, rho_a, tables, gains_new, spread, duals_new, target):
    rho = rho_a[...]
    chan = lax.axis_index("chan")
    old_gains = comps(gains)
    old_duals = comps(duals)
    fitted = fit(tables, chan, moments, 4)
    new_duals = [old_duals[c] + rho * (old_gains[c] - fitted[c]) for c in range(8)]
    aim = [0.5 * (rho * fitted[c] - new_duals[c]) for c in range(8)]
    put(duals_new, new_duals)
    put(target, aim)
    new = updated(received, old_gains, aim, rho)
    put(gains_new, new)
    for d in range(8):
        put(spread, new, d * 64)


def update_last_kernel(received, gains, target, duals, rho_a, keep, send):
    core = lax.axis_index("core")
    new = updated(received, comps(gains), comps(target), rho_a[...])
    old = comps(duals)
    lane = lanes()
    for out, stations in ((keep, core), (send, 1 - core)):
        for base, values in ((0, new), (64, old)):
            for c in range(8):
                total = jnp.zeros((8, 128), F32)
                for h in range(2):
                    here = jnp.where(lane // 32 == 2 * h + stations, values[c], 0.0)
                    total = total + pltpu.roll(here, (64 * core + 32 * stations * 3 + 96 * h) % 128, 1)
                out[base + c * 8:base + (c + 1) * 8, :] = total


def moment_kernel(keep, recv, rho_f, state, moment):
    both = keep[...] + recv[...]
    state[...] = both
    rho = rho_f[...]
    for c in range(8):
        value = both[64 + c * 8:72 + c * 8] + rho * both[c * 8:c * 8 + 8]
        for d in range(8):
            moment[d * 64 + c * 8:d * 64 + (c + 1) * 8, :] = value


def finish_kernel(moments, state, rho_f, tables, gains, duals, poly, thin, deep):
    chan = lax.axis_index("chan")
    rho = rho_f[...]
    fitted = fit(tables, chan, moments, 4)
    for c in range(8):
        value = state[c * 8:(c + 1) * 8, :]
        for q in range(4):
            thin[pl.ds(q * 64 + c, 8, stride=8), :] = pltpu.roll(value, (128 - 32 * q) % 128, 1)
    gains[...] = thin[:, 0:32].reshape(32, 8, 32)
    for c in range(8):
        value = state[64 + c * 8:72 + c * 8, :] + rho * (state[c * 8:(c + 1) * 8, :] - fitted[c])
        for q in range(4):
            thin[pl.ds(q * 64 + c, 8, stride=8), :] = pltpu.roll(value, (128 - 32 * q) % 128, 1)
    duals[...] = thin[:, 0:32].reshape(32, 8, 32)
    for t in range(TERMS):
        part = fit(tables, 8 + t, moments, 4)
        for c in range(8):
            for q in range(4):
                deep[pl.ds((q * 64 + c) * 4 + t, 8, stride=32), :] = pltpu.roll(part[c], (128 - 32 * q) % 128, 1)
    poly[...] = deep[:, 0:32].reshape(32, 8, 4, 32)


def local(coherency, visibilities, station_pairs, gains, duals, poly, penalty):
    basis, solve, hat = consensus_tables()
    constants = np.zeros((12, 12), np.float32)
    constants[:8, :4] = basis
    constants[:8, 4:] = hat
    constants[8:, 4:] = solve
    tables = jnp.asarray(constants)
    coh_keep, coh_send, state_keep, state_send, rho_a, rho_f = call(
        prepare_kernel,
        [((128, ROWS), F32), ((128, ROWS), F32), ((192, 128), F32), ((192, 128), F32), ((8, 128), F32), ((8, 128), F32)],
        [pltpu.VMEM((ROWS // 128, 256, 128), F32), pltpu.VMEM((256, 128), F32)],
        smem=(4, 5), n_in=6,
    )(coherency[0], gains[0], duals[0], poly, penalty, tables)

    def swap(x):
        return lax.ppermute(x, "core", CORE_SWAP)

    def exchange(x, axis):
        return lax.all_to_all(x, axis, 0, 0, tiled=True)

    state_recv = swap(state_send)
    coh_recv = swap(coh_send)
    pairs_recv = swap(station_pairs)
    vis = visibilities[0]
    packed = ((64, 128), F32)
    wide = ((512, 128), F32)
    gain, dual, target, spread = call(first_kernel, [packed, packed, packed, wide], n_in=3)(
        state_keep, state_recv, rho_a
    )

    def sums(spread):
        gathered = exchange(spread, "st")
        z, w, own = call(
            model_kernel,
            [((128, 2 * ROWS), F32), ((128, 2 * ROWS), F32), ((8, 2 * ROWS), F32)],
            [pltpu.VMEM((256, STATIONS), BF16), pltpu.VMEM((2, 128, BLOCK), F32), pltpu.VMEM((2, 128, BLOCK), F32)],
            n_in=6,
        )(gathered, coh_keep, coh_recv, vis, station_pairs, pairs_recv)
        other = swap(own)
        (parts,) = call(
            sums_kernel,
            [((768, 128), F32)],
            [pltpu.VMEM((2, 384, 2 * BLOCK), BF16), pltpu.VMEM((384, STATIONS), F32)],
            n_in=6,
        )(z, w, own, other, station_pairs, pairs_recv)
        return exchange(parts, "st")

    gain, spread = call(update_kernel, [packed, wide], n_in=4)(sums(spread), gain, target, rho_a)
    gain, spread, moment = call(update_moment_kernel, [packed, wide, wide], n_in=5)(
        sums(spread), gain, target, dual, rho_a
    )
    moments = exchange(moment, "chan")
    gain, spread, dual, target = call(
        update_consensus_kernel, [packed, wide, packed, packed], smem=(5,), n_in=6
    )(sums(spread), gain, moments, dual, rho_a, tables)
    keep, send = call(update_last_kernel, [((128, 128), F32), ((128, 128), F32)], n_in=5)(
        sums(spread), gain, target, dual, rho_a
    )
    state, moment = call(moment_kernel, [((128, 128), F32), wide], n_in=3)(keep, swap(send), rho_f)
    moments = exchange(moment, "chan")
    gains_out, duals_out, poly_out = call(
        finish_kernel,
        [((32, 8, 32), F32), ((32, 8, 32), F32), ((32, 8, 4, 32), F32)],
        [pltpu.VMEM((256, 128), F32), pltpu.VMEM((1024, 128), F32)],
        smem=(3,), n_in=4,
    )(moments, state, rho_f, tables)
    return gains_out[None], duals_out[None], poly_out


def solution(mesh):
    chan, bl = mesh.devices.shape
    finer = Mesh(mesh.devices.reshape(chan, bl // 2, 2), ("chan", "st", "core"))
    both = ("st", "core")
    in_specs = (
        P("chan", None, None, both),
        P("chan", None, both),
        P(None, both),
        P("chan", None, None, both),
        P("chan", None, None, both),
        P(None, None, None, both),
        P(),
    )
    out_specs = (
        P("chan", None, None, both),
        P("chan", None, None, both),
        P(None, None, None, both),
    )
    return jax.shard_map(local, mesh=finer, in_specs=in_specs, out_specs=out_specs, check_vma=False)
```

time: 1030 us -> 156 us (0.15)
  waiting for transfers between devices: 521 us -> 11.3 us
  local copies, waits for them, and re-layouts: 204 us -> 5.25 us
  other arithmetic: 159 us -> 0 us
  blocking collectives: 112 us -> 79.7 us
  starting transfers between devices: 0.5 us -> 30.9 us
  Pallas kernels: 0 us -> 27.2 us
  between operations: 16 us -> 0.77 us
    psum x6 -> x0, waiting for transfers between devices: 521 us -> none  [the longest x4 396 us: local(): sums = lax.psum(partial_sums, 'bl')]
    all_gather x3 -> x0, blocking collectives: 112 us -> none  [the longest x2 79.6 us: local(): target_full = lax.all_gather(target, 'bl', axis=3, tiled=True)]
    gather x16 -> x0, local copies, waits for them, and re-layouts: 108 us -> none  [the longest x8 53.8 us: channel_sums(): gain_second = jnp.take(gain_one, second, axis=2)]
    all_to_all x0 -> x8, blocking collectives: none -> 79.7 us  [exchange(): return lax.all_to_all(x, axis, 0, 0, tiled=True)]
    scatter-add x4 -> x0, other arithmetic: 64.8 us -> none  [channel_sums(): summed = jax.ops.segment_sum(flat_rows.T, index, num_segments=stations)]
    unnamed x108 -> x0, other arithmetic: 32.2 us -> none
    add x29 -> x0, other arithmetic: 27.7 us -> none  [the longest x8 12.4 us: channel_sums(): per_dir = resid[None] + model]
    pallas_call x0 -> x16, Pallas kernels: none -> 27.2 us  [the longest x4 11.9 us: sums(): call(sums_kernel, [((768, 128), F32)], [pltpu.VMEM((2, 384, 2 * BLOCK), B...]
  transfers between devices with their start and end apart: 6 -> 10, of which waited for: 6 -> 8; matrix products, arithmetic and copies ran while one was open for 5% -> 0% of each run, Pallas kernels for 0% -> 4%
where the time goes in v1:
time: 156 us; the launch traced here: 155 us
  blocking collectives  79.7 us (51%)
  starting transfers between devices  30.9 us (20%)
  Pallas kernels  27.2 us (17%)
  waiting for transfers between devices  11.3 us (7%)
  local copies, waits for them, and re-layouts  5.25 us (3%)
    all_to_all x8, blocking collectives, exchange(): return lax.all_to_all(x, axis, 0, 0, tiled=True)  79.7 us
    ppermute x8, starting transfers between devices, swap(): return lax.ppermute(x, 'core', CORE_SWAP)  18.1 us
    all_to_all x2, starting transfers between devices, exchange(): return lax.all_to_all(x, axis, 0, 0, tiled=True)  12.8 us
    pallas_call x4, Pallas kernels, sums(): call(sums_kernel, [((768, 128), F32)], [pltpu.VMEM((2, 384, 2 * BLOCK), B...  11.9 us
    pallas_call x4, Pallas kernels, sums(): call(model_kernel, [((128, 2 * ROWS), F32), ((128, 2 * ROWS), F32), ((8,...  9 us
    ppermute x8, waiting for transfers between devices, swap(): return lax.ppermute(x, 'core', CORE_SWAP)  6.93 us
    unnamed x18, local copies, waits for them, and re-layouts  5.25 us
    all_to_all x2, waiting for transfers between devices, exchange(): return lax.all_to_all(x, axis, 0, 0, tiled=True)  4.38 us
  transfers between devices with their start and end apart: 10, of which 8 were waited for; matrix products, arithmetic and copies ran while one was open for 0% of the time, Pallas kernels for 4%

profile of v1, /device:TPU:1, one launch (start us, length us, event | category | flops | bytes accessed | tf_op | source)
XLA Modules:
  0.0 155.1 jit_solution(6947392520927375400)
XLA Ops:
  0.6 0.0 copy-start.8
  0.6 0.6 copy-done.8
  1.3 0.0 copy-start.1
  1.3 1.0 copy-done.1
  2.3 0.0 copy-start.2
  2.3 1.0 copy-done.2
  3.4 0.0 copy-start.4
  3.4 0.9 copy-done.4
  4.3 0.0 copy-start.5
  4.3 0.9 copy-done.5
  5.2 0.0 copy-start.6
  5.2 0.7 copy-done.6
  5.9 1.7 %shard_map.103 = (f32[128,1024]{1,0:T(8,128)S(1)}, f32[128,1024]{1,0:T(8,128)S(1)}, f32[192,128]{1,0:T(8,128)S(1)}, f32[192,128]{1,0:T(8,128)S(1)}, f32[8,128]{1,0:T(8,128)S(1)}, /*index=5*/f32[8,128]{1,0:T(8,128)S(1)}) custom-call(bf16[32,8,1024]{2,1,0:T(8,128)(2,1)S(1)} %bitcast.40, f32[32,8,32]{2,1,0:T(8,128)S(1)} %bitcast.49, f32[32,8,32]{2,1,0:T(8,128)S(1)} %bitcast.50, ...), custom_call_target="tpu_custom_call" | custom-call | tf_op jit(solution)/shard_map/pallas_call | solution.py:393
  7.6 1.5 collective-permute-start.1
  9.1 0.1 collective-permute-start
  9.2 1.6 %collective-permute-done.state_recv = f32[192,128]{1,0:T(8,128)S(1)} collective-permute-done((f32[192,128]{1,0:T(8,128)S(1)}, f32[192,128]{1,0:T(8,128)S(1)}, u32[]{:S(2)}, u32[]{:S(2)}) %collective-permute-start) | collective-permute-done | bytes 98336 | tf_op jit(solution)/shard_map/ppermute | solution.py:401
  10.8 0.7 shard_map.104
  11.5 0.0 copy-start
  11.5 0.0 copy-start.3
  11.5 5.6 %all-to-all-start = ((f32[8,64,128]{2,1,0:T(8,128)}), f32[8,64,128]{2,1,0:T(8,128)S(1)}, u32[]{:S(2)}, u32[]{:S(2)}) async-start(f32[8,64,128]{2,1,0:T(8,128)} %bitcast.3), calls=%async_computation | async-start | bytes 524288 | tf_op jit(solution)/shard_map/all_to_all | solution.py:404
  17.1 0.0 copy-done
  17.1 0.7 collective-permute-start.2
  17.8 0.8 collective-permute-done.2.pairs_other
  18.7 4.4 %all-to-all-done = f32[8,64,128]{2,1,0:T(8,128)S(1)} async-done(((f32[8,64,128]{2,1,0:T(8,128)}), f32[8,64,128]{2,1,0:T(8,128)S(1)}, u32[]{:S(2)}, u32[]{:S(2)}) %all-to-all-start) | async-done | bytes 262176 | tf_op jit(solution)/shard_map/all_to_all | solution.py:404
  23.0 0.0 collective-permute-done.1.coh_other
  23.0 0.0 copy-done.3
  23.0 2.2 %shard_map.105 = (f32[128,2048]{1,0:T(8,128)S(1)}, f32[128,2048]{1,0:T(8,128)S(1)}, f32[8,2048]{1,0:T(8,128)S(1)}) custom-call(f32[512,128]{1,0:T(8,128)S(1)} %bitcast.36, f32[128,1024]{1,0:T(8,128)S(1)} %get-tuple-element.45.coh_own, f32[128,1024]{1,0:T(8,128)S(1)} %collective-permute-done.1.coh_other, f32[8,1024]{1,0:T(8,128)S(1)} %bitcast.41, ...), custom_call_target="tpu_custom_call" | custom-call | tf_op jit(solution)/shard_map/pallas_call | solution.py:418
  25.3 2.1 %collective-permute-start.3 = (f32[8,2048]{1,0:T(8,128)S(1)}, f32[8,2048]{1,0:T(8,128)S(1)}, u32[]{:S(2)}, u32[]{:S(2)}) collective-permute-start(f32[8,2048]{1,0:T(8,128)S(1)} %get-tuple-element.49.s_own), channel_id=1, source_target_pairs={{0,1},{1,0},{2,3},{3,2},{4,5},{5,4},{6,7},{7,6},{8,9},{9,8},{10,11... | collective-permute-start | bytes 196616 | tf_op jit(solution)/shard_map/ppermute | solution.py:401
  27.4 0.9 collective-permute-done.3.s_other
  28.3 3.0 %shard_map.106 = f32[768,128]{1,0:T(8,128)S(1)} custom-call(f32[128,2048]{1,0:T(8,128)S(1)} %get-tuple-element.47.z_ref, f32[128,2048]{1,0:T(8,128)S(1)} %get-tuple-element.48.w_ref, f32[8,2048]{1,0:T(8,128)S(1)} %get-tuple-element.49.s_own, f32[8,2048]{1,0:T(8,128)S(1)} %collective-permute-done.3.s_other, s32[2,1024]{1,0:T(2,128)S(1)} %copy-done, ...), custom_call_target="tpu_custom_call" | custom-call | tf_op jit(solution)/shard_map/pallas_call | solution.py:425
  31.3 10.1 %all_to_all.110 = f32[8,96,128]{2,1,0:T(8,128)S(1)} all-to-all(f32[8,96,128]{2,1,0:T(8,128)S(1)} %bitcast.29), channel_id=1, replica_groups=mesh['chan'=8,'st'=8,'core'=2] {'st'}, dimensions={0} | all-to-all | bytes 786432 | tf_op jit(solution)/shard_map/all_to_all | solution.py:404
  41.4 0.1 shard_map.107
  41.5 8.6 %all_to_all.111 = f32[8,64,128]{2,1,0:T(8,128)S(1)} all-to-all(f32[8,64,128]{2,1,0:T(8,128)S(1)} %bitcast.47), channel_id=1, replica_groups=mesh['chan'=8,'st'=8,'core'=2] {'st'}, dimensions={0} | all-to-all | bytes 524288 | tf_op jit(solution)/shard_map/all_to_all | solution.py:404
  50.1 2.2 %shard_map.108 = (f32[128,2048]{1,0:T(8,128)S(1)}, f32[128,2048]{1,0:T(8,128)S(1)}, f32[8,2048]{1,0:T(8,128)S(1)}) custom-call(f32[512,128]{1,0:T(8,128)S(1)} %bitcast.39, f32[128,1024]{1,0:T(8,128)S(1)} %get-tuple-element.45.coh_own, f32[128,1024]{1,0:T(8,128)S(1)} %collective-permute-done.1.coh_other, f32[8,1024]{1,0:T(8,128)S(1)} %bitcast.42, ...), custom_call_target="tpu_custom_call" | custom-call | tf_op jit(solution)/shard_map/pallas_call | solution.py:418
  52.4 3.1 %collective-permute-start.4 = (f32[8,2048]{1,0:T(8,128)S(1)}, f32[8,2048]{1,0:T(8,128)S(1)}, u32[]{:S(2)}, u32[]{:S(2)}) collective-permute-start(f32[8,2048]{1,0:T(8,128)S(1)} %get-tuple-element.55.s_own), channel_id=1, source_target_pairs={{0,1},{1,0},{2,3},{3,2},{4,5},{5,4},{6,7},{7,6},{8,9},{9,8},{10,11... | collective-permute-start | bytes 196616 | tf_op jit(solution)/shard_map/ppermute | solution.py:401
  55.5 0.9 collective-permute-done.4.s_other
  56.4 3.0 %shard_map.109 = f32[768,128]{1,0:T(8,128)S(1)} custom-call(f32[128,2048]{1,0:T(8,128)S(1)} %get-tuple-element.53.z_ref, f32[128,2048]{1,0:T(8,128)S(1)} %get-tuple-element.54.w_ref, f32[8,2048]{1,0:T(8,128)S(1)} %get-tuple-element.55.s_own, f32[8,2048]{1,0:T(8,128)S(1)} %collective-permute-done.4.s_other, s32[2,1024]{1,0:T(2,128)S(1)} %copy-done, ...), custom_call_target="tpu_custom_call" | custom-call | tf_op jit(solution)/shard_map/pallas_call | solution.py:425
  59.4 10.2 %all_to_all.112 = f32[8,96,128]{2,1,0:T(8,128)S(1)} all-to-all(f32[8,96,128]{2,1,0:T(8,128)S(1)} %bitcast.31), channel_id=1, replica_groups=mesh['chan'=8,'st'=8,'core'=2] {'st'}, dimensions={0} | all-to-all | bytes 786432 | tf_op jit(solution)/shard_map/all_to_all | solution.py:404
  69.6 0.8 shard_map.110
  70.4 8.6 %all_to_all.113 = f32[8,64,128]{2,1,0:T(8,128)S(1)} all-to-all(f32[8,64,128]{2,1,0:T(8,128)S(1)} %bitcast.46), channel_id=1, replica_groups=mesh['chan'=8,'st'=8,'core'=2] {'st'}, dimensions={0} | all-to-all | bytes 524288 | tf_op jit(solution)/shard_map/all_to_all | solution.py:404
  79.0 7.2 %all-to-all-start.6 = ((f32[8,64,128]{2,1,0:T(8,128)}), f32[8,64,128]{2,1,0:T(8,128)S(1)}, u32[]{:S(2)}, u32[]{:S(2)}) async-start(f32[8,64,128]{2,1,0:T(8,128)} %bitcast.16), calls=%async_computation.6 | async-start | bytes 524288 | tf_op jit(solution)/shard_map/all_to_all | solution.py:404
  86.2 2.3 %shard_map.111 = (f32[128,2048]{1,0:T(8,128)S(1)}, f32[128,2048]{1,0:T(8,128)S(1)}, f32[8,2048]{1,0:T(8,128)S(1)}) custom-call(f32[512,128]{1,0:T(8,128)S(1)} %bitcast.37, f32[128,1024]{1,0:T(8,128)S(1)} %get-tuple-element.45.coh_own, f32[128,1024]{1,0:T(8,128)S(1)} %collective-permute-done.1.coh_other, f32[8,1024]{1,0:T(8,128)S(1)} %bitcast.43, ...), custom_call_target="tpu_custom_call" | custom-call | tf_op jit(solution)/shard_map/pallas_call | solution.py:418
  88.5 3.2 %collective-permute-start.5 = (f32[8,2048]{1,0:T(8,128)S(1)}, f32[8,2048]{1,0:T(8,128)S(1)}, u32[]{:S(2)}, u32[]{:S(2)}) collective-permute-start(f32[8,2048]{1,0:T(8,128)S(1)} %get-tuple-element.61.s_own), channel_id=1, source_target_pairs={{0,1},{1,0},{2,3},{3,2},{4,5},{5,4},{6,7},{7,6},{8,9},{9,8},{10,11... | collective-permute-start | bytes 196616 | tf_op jit(solution)/shard_map/ppermute | solution.py:401
  91.7 0.9 collective-permute-done.5.s_other
  92.6 3.0 %shard_map.112 = f32[768,128]{1,0:T(8,128)S(1)} custom-call(f32[128,2048]{1,0:T(8,128)S(1)} %get-tuple-element.59.z_ref, f32[128,2048]{1,0:T(8,128)S(1)} %get-tuple-element.60.w_ref, f32[8,2048]{1,0:T(8,128)S(1)} %get-tuple-element.61.s_own, f32[8,2048]{1,0:T(8,128)S(1)} %collective-permute-done.5.s_other, s32[2,1024]{1,0:T(2,128)S(1)} %copy-done, ...), custom_call_target="tpu_custom_call" | custom-call | tf_op jit(solution)/shard_map/pallas_call | solution.py:425
  95.6 0.0 all-to-all-done.6
  95.6 0.0 copy-start.7
  95.6 9.1 %all_to_all.114 = f32[8,96,128]{2,1,0:T(8,128)S(1)} all-to-all(f32[8,96,128]{2,1,0:T(8,128)S(1)} %bitcast.26), channel_id=1, replica_groups=mesh['chan'=8,'st'=8,'core'=2] {'st'}, dimensions={0} | all-to-all | bytes 786432 | tf_op jit(solution)/shard_map/all_to_all | solution.py:404
  104.7 0.0 copy-done.7
  104.7 0.7 shard_map.113
  105.5 8.5 %all_to_all.115 = f32[8,64,128]{2,1,0:T(8,128)S(1)} all-to-all(f32[8,64,128]{2,1,0:T(8,128)S(1)} %bitcast.45), channel_id=1, replica_groups=mesh['chan'=8,'st'=8,'core'=2] {'st'}, dimensions={0} | all-to-all | bytes 524288 | tf_op jit(solution)/shard_map/all_to_all | solution.py:404
  113.9 2.2 %shard_map.114 = (f32[128,2048]{1,0:T(8,128)S(1)}, f32[128,2048]{1,0:T(8,128)S(1)}, f32[8,2048]{1,0:T(8,128)S(1)}) custom-call(f32[512,128]{1,0:T(8,128)S(1)} %bitcast.38, f32[128,1024]{1,0:T(8,128)S(1)} %get-tuple-element.45.coh_own, f32[128,1024]{1,0:T(8,128)S(1)} %collective-permute-done.1.coh_other, f32[8,1024]{1,0:T(8,128)S(1)} %bitcast.44, ...), custom_call_target="tpu_custom_call" | custom-call | tf_op jit(solution)/shard_map/pallas_call | solution.py:418
  116.2 5.4 %collective-permute-start.6 = (f32[8,2048]{1,0:T(8,128)S(1)}, f32[8,2048]{1,0:T(8,128)S(1)}, u32[]{:S(2)}, u32[]{:S(2)}) collective-permute-start(f32[8,2048]{1,0:T(8,128)S(1)} %get-tuple-element.67.s_own), channel_id=1, source_target_pairs={{0,1},{1,0},{2,3},{3,2},{4,5},{5,4},{6,7},{7,6},{8,9},{9,8},{10,11... | collective-permute-start | bytes 196616 | tf_op jit(solution)/shard_map/ppermute | solution.py:401
  121.6 0.9 collective-permute-done.6.s_other
  122.5 3.0 %shard_map.115 = f32[768,128]{1,0:T(8,128)S(1)} custom-call(f32[128,2048]{1,0:T(8,128)S(1)} %get-tuple-element.65.z_ref, f32[128,2048]{1,0:T(8,128)S(1)} %get-tuple-element.66.w_ref, f32[8,2048]{1,0:T(8,128)S(1)} %get-tuple-element.67.s_own, f32[8,2048]{1,0:T(8,128)S(1)} %collective-permute-done.6.s_other, s32[2,1024]{1,0:T(2,128)S(1)} %copy-done, ...), custom_call_target="tpu_custom_call" | custom-call | tf_op jit(solution)/shard_map/pallas_call | solution.py:425
  125.5 10.2 %all_to_all.116 = f32[8,96,128]{2,1,0:T(8,128)S(1)} all-to-all(f32[8,96,128]{2,1,0:T(8,128)S(1)} %bitcast.28), channel_id=1, replica_groups=mesh['chan'=8,'st'=8,'core'=2] {'st'}, dimensions={0} | all-to-all | bytes 786432 | tf_op jit(solution)/shard_map/all_to_all | solution.py:404
  135.7 0.2 shard_map.116
  135.8 1.9 %collective-permute-start.7 = (f32[128,128]{1,0:T(8,128)S(1)}, f32[128,128]{1,0:T(8,128)S(1)}, u32[]{:S(2)}, u32[]{:S(2)}) collective-permute-start(f32[128,128]{1,0:T(8,128)S(1)} %get-tuple-element.72), channel_id=1, source_target_pairs={{0,1},{1,0},{2,3},{3,2},{4,5},{5,4},{6,7},{7,6},{8,9},{9,8},{10,11... | collective-permute-start | bytes 196616 | tf_op jit(solution)/shard_map/ppermute | solution.py:401
  137.8 0.9 collective-permute-done.7.recv
  138.7 14.3 %all_to_all.117 = f32[8,64,128]{2,1,0:T(8,128)S(1)} all-to-all(f32[8,64,128]{2,1,0:T(8,128)S(1)} %bitcast.48), channel_id=1, replica_groups=mesh['chan'=8,'st'=8,'core'=2] {'chan'}, dimensions={0} | all-to-all | bytes 524288 | tf_op jit(solution)/shard_map/all_to_all | solution.py:404
  153.0 2.0 %shard_map.118 = (f32[32,8,32]{2,1,0:T(8,128)}, f32[32,8,32]{2,1,0:T(8,128)}, f32[32,8,4,32]{3,2,1,0:T(4,128)}) custom-call(f32[512,128]{1,0:T(8,128)S(1)} %bitcast.34, f32[128,128]{1,0:T(8,128)S(1)} %get-tuple-element.75.state, f32[8,128]{1,0:T(8,128)S(1)} %get-tuple-element.73.rho_f, f32[12,12]{1,0:T(8,128)S(1)} %copy-done.7), custom_call_target="tpu_custom_call" | custom-call | tf_op jit(solution)/shard_map/pallas_call | solution.py:446
  (1 shorter events, 0.0 us)
Async XLA Ops:
  0.6 0.7 copy-start.8
  1.3 1.0 copy-start.1
  2.3 1.0 copy-start.2
  3.4 0.9 copy-start.4
  4.3 0.9 copy-start.5
  5.2 0.7 copy-start.6
  7.6 15.4 %collective-permute-start.1 = (f32[128,1024]{1,0:T(8,128)S(1)}, f32[128,1024]{1,0:T(8,128)S(1)}, u32[]{:S(2)}, u32[]{:S(2)}) collective-permute-start(f32[128,1024]{1,0:T(8,128)S(1)} %get-tuple-element.46), channel_id=1, source_target_pairs={{0,1},{1,0},{2,3},{3,2},{4,5},{5,4},{6,7},{7,6},{8,9},{9,8},{10,11... | collective-permute-start | bytes 1572872 | tf_op jit(solution)/shard_map/ppermute | solution.py:401
  9.1 1.7 %collective-permute-start = (f32[192,128]{1,0:T(8,128)S(1)}, f32[192,128]{1,0:T(8,128)S(1)}, u32[]{:S(2)}, u32[]{:S(2)}) collective-permute-start(f32[192,128]{1,0:T(8,128)S(1)} %get-tuple-element.42), channel_id=1, source_target_pairs={{0,1},{1,0},{2,3},{3,2},{4,5},{5,4},{6,7},{7,6},{8,9},{9,8},{10,11... | collective-permute-start | bytes 294920 | tf_op jit(solution)/shard_map/ppermute | solution.py:401
  11.5 5.6 %copy-start = (s32[2,1024]{1,0:T(2,128)S(1)}, s32[2,1024]{1,0:T(2,128)}, u32[]{:S(2)}) copy-start(s32[2,1024]{1,0:T(2,128)} %pairs_own.15) | copy-start | bytes 24580
  11.5 11.5 %copy-start.3 = (f32[1,8,1024]{2,1,0:T(8,128)S(1)}, f32[1,8,1024]{2,1,0:T(8,128)}, u32[]{:S(2)}) copy-start(f32[1,8,1024]{2,1,0:T(8,128)} %param.9) | copy-start | bytes 98308
  11.5 11.5 %all-to-all-start = ((f32[8,64,128]{2,1,0:T(8,128)}), f32[8,64,128]{2,1,0:T(8,128)S(1)}, u32[]{:S(2)}, u32[]{:S(2)}) async-start(f32[8,64,128]{2,1,0:T(8,128)} %bitcast.3), calls=%async_computation | async-start | bytes 524288 | tf_op jit(solution)/shard_map/all_to_all | solution.py:404
  17.1 1.6 %collective-permute-start.2 = (s32[2,1024]{1,0:T(2,128)S(1)}, s32[2,1024]{1,0:T(2,128)S(1)}, u32[]{:S(2)}, u32[]{:S(2)}) collective-permute-start(s32[2,1024]{1,0:T(2,128)S(1)} %copy-done), channel_id=1, source_target_pairs={{0,1},{1,0},{2,3},{3,2},{4,5},{5,4},{6,7},{7,6},{8,9},{9,8},{10,11... | collective-permute-start | bytes 24584 | tf_op jit(solution)/shard_map/ppermute | solution.py:401
  25.3 3.0 %collective-permute-start.3 = (f32[8,2048]{1,0:T(8,128)S(1)}, f32[8,2048]{1,0:T(8,128)S(1)}, u32[]{:S(2)}, u32[]{:S(2)}) collective-permute-start(f32[8,2048]{1,0:T(8,128)S(1)} %get-tuple-element.49.s_own), channel_id=1, source_target_pairs={{0,1},{1,0},{2,3},{3,2},{4,5},{5,4},{6,7},{7,6},{8,9},{9,8},{10,11... | collective-permute-start | bytes 196616 | tf_op jit(solution)/shard_map/ppermute | solution.py:401
  52.4 4.0 %collective-permute-start.4 = (f32[8,2048]{1,0:T(8,128)S(1)}, f32[8,2048]{1,0:T(8,128)S(1)}, u32[]{:S(2)}, u32[]{:S(2)}) collective-permute-start(f32[8,2048]{1,0:T(8,128)S(1)} %get-tuple-element.55.s_own), channel_id=1, source_target_pairs={{0,1},{1,0},{2,3},{3,2},{4,5},{5,4},{6,7},{7,6},{8,9},{9,8},{10,11... | collective-permute-start | bytes 196616 | tf_op jit(solution)/shard_map/ppermute | solution.py:401
  79.0 16.6 %all-to-all-start.6 = ((f32[8,64,128]{2,1,0:T(8,128)}), f32[8,64,128]{2,1,0:T(8,128)S(1)}, u32[]{:S(2)}, u32[]{:S(2)}) async-start(f32[8,64,128]{2,1,0:T(8,128)} %bitcast.16), calls=%async_computation.6 | async-start | bytes 524288 | tf_op jit(solution)/shard_map/all_to_all | solution.py:404
  88.5 4.1 %collective-permute-start.5 = (f32[8,2048]{1,0:T(8,128)S(1)}, f32[8,2048]{1,0:T(8,128)S(1)}, u32[]{:S(2)}, u32[]{:S(2)}) collective-permute-start(f32[8,2048]{1,0:T(8,128)S(1)} %get-tuple-element.61.s_own), channel_id=1, source_target_pairs={{0,1},{1,0},{2,3},{3,2},{4,5},{5,4},{6,7},{7,6},{8,9},{9,8},{10,11... | collective-permute-start | bytes 196616 | tf_op jit(solution)/shard_map/ppermute | solution.py:401
  95.6 9.1 %copy-start.7 = (f32[12,12]{1,0:T(8,128)S(1)}, f32[12,12]{1,0:T(8,128)}, u32[]{:S(2)}) copy-start(f32[12,12]{1,0:T(8,128)} %constant.2.clone.tables) | copy-start | bytes 1732
  116.2 6.3 %collective-permute-start.6 = (f32[8,2048]{1,0:T(8,128)S(1)}, f32[8,2048]{1,0:T(8,128)S(1)}, u32[]{:S(2)}, u32[]{:S(2)}) collective-permute-start(f32[8,2048]{1,0:T(8,128)S(1)} %get-tuple-element.67.s_own), channel_id=1, source_target_pairs={{0,1},{1,0},{2,3},{3,2},{4,5},{5,4},{6,7},{7,6},{8,9},{9,8},{10,11... | collective-permute-start | bytes 196616 | tf_op jit(solution)/shard_map/ppermute | solution.py:401
  135.8 2.8 %collective-permute-start.7 = (f32[128,128]{1,0:T(8,128)S(1)}, f32[128,128]{1,0:T(8,128)S(1)}, u32[]{:S(2)}, u32[]{:S(2)}) collective-permute-start(f32[128,128]{1,0:T(8,128)S(1)} %get-tuple-element.72), channel_id=1, source_target_pairs={{0,1},{1,0},{2,3},{3,2},{4,5},{5,4},{6,7},{7,6},{8,9},{9,8},{10,11... | collective-permute-start | bytes 196616 | tf_op jit(solution)/shard_map/ppermute | solution.py:401

commit v2 on v1

v2 whole, which is shorter than its diff:
```python
import jax
import jax.numpy as jnp
import numpy as np
from jax import lax
from jax.experimental import pallas as pl
from jax.experimental.pallas import tpu as pltpu
from jax.sharding import Mesh, PartitionSpec as P


CHANNELS = 8
TERMS = 4
ROWS = 1024
BLOCK = 256
STATIONS = 512
F32 = jnp.float32
BF16 = jnp.bfloat16
CORE_SWAP = [(0, 1), (1, 0)]
VMEM_BYTES = 24 * 1024 * 1024
WHOLE_BYTES = 60 * 1024 * 1024


def consensus_tables():
    place = (2.0 * np.arange(CHANNELS) + 1.0) / CHANNELS - 1.0
    basis = np.stack(
        [np.ones_like(place), place, 1.5 * place**2 - 0.5, 2.5 * place**3 - 1.5 * place], axis=1
    )
    solve = np.linalg.solve(basis.T @ basis, basis.T)
    return basis, solve, basis @ solve


def call(kernel, out_shapes, scratch=(), smem=(), hbm=(), n_in=0, cost=0, room=VMEM_BYTES):
    spaces = [pltpu.SMEM if i in smem else pl.ANY if i in hbm else pltpu.VMEM for i in range(n_in)]
    in_specs = [pl.BlockSpec(memory_space=space) for space in spaces]
    return pl.pallas_call(
        kernel,
        out_shape=[jax.ShapeDtypeStruct(s, d) for s, d in out_shapes],
        in_specs=in_specs,
        out_specs=[pl.BlockSpec(memory_space=pltpu.VMEM) for _ in out_shapes],
        scratch_shapes=list(scratch),
        compiler_params=pltpu.CompilerParams(vmem_limit_bytes=room),
        cost_estimate=pl.CostEstimate(flops=0, bytes_accessed=cost * 3_000_000 + 1000, transcendentals=0),
    )


def lanes():
    return lax.broadcasted_iota(jnp.int32, (8, 128), 1)


def split_parts(x):
    high = x.astype(BF16)
    return high, (x - high.astype(F32)).astype(BF16)


def matrix(load):
    return [load(i) for i in range(4)], [load(4 + i) for i in range(4)]


def conj_t(m):
    re, im = m
    return [re[0], re[2], re[1], re[3]], [-im[0], -im[2], -im[1], -im[3]]


def product_nh(a, b):
    (ar, ai), (br, bi) = a, b
    re, im = [], []
    for i in (0, 1):
        for j in (0, 1):
            p, q, u, v = 2 * i, 2 * i + 1, 2 * j, 2 * j + 1
            re.append((ar[p] * br[u] + ai[p] * bi[u]) + (ar[q] * br[v] + ai[q] * bi[v]))
            im.append((ai[p] * br[u] - ar[p] * bi[u]) + (ai[q] * br[v] - ar[q] * bi[v]))
    return re, im


def product_hn(a, b):
    (ar, ai), (br, bi) = a, b
    re, im = [], []
    for i in (0, 1):
        for j in (0, 1):
            p, q, u, v = i, 2 + i, j, 2 + j
            re.append((ar[p] * br[u] + ai[p] * bi[u]) + (ar[q] * br[v] + ai[q] * bi[v]))
            im.append((ar[p] * bi[u] - ai[p] * br[u]) + (ar[q] * bi[v] - ai[q] * br[v]))
    return re, im


def product(a, b):
    (ar, ai), (br, bi) = a, b
    re, im = [], []
    for i in (0, 1):
        for j in (0, 1):
            p, q, u, v = 2 * i, 2 * i + 1, j, 2 + j
            re.append((ar[p] * br[u] - ai[p] * bi[u]) + (ar[q] * br[v] - ai[q] * bi[v]))
            im.append((ar[p] * bi[u] + ai[p] * br[u]) + (ar[q] * bi[v] + ai[q] * br[v]))
    return re, im


def square_nh(a):
    r, i = a
    return [
        (r[0] * r[0] + i[0] * i[0]) + (r[1] * r[1] + i[1] * i[1]),
        (r[2] * r[2] + i[2] * i[2]) + (r[3] * r[3] + i[3] * i[3]),
        (r[0] * r[2] + i[0] * i[2]) + (r[1] * r[3] + i[1] * i[3]),
        (i[0] * r[2] - r[0] * i[2]) + (i[1] * r[3] - r[1] * i[3]),
    ]


def square_hn(a):
    r, i = a
    return [
        (r[0] * r[0] + i[0] * i[0]) + (r[2] * r[2] + i[2] * i[2]),
        (r[1] * r[1] + i[1] * i[1]) + (r[3] * r[3] + i[3] * i[3]),
        (r[0] * r[1] + i[0] * i[1]) + (r[2] * r[3] + i[2] * i[3]),
        (r[0] * i[1] - i[0] * r[1]) + (r[2] * i[3] - i[2] * r[3]),
    ]


def spread_kernel(gains, spread, mark, thin):
    thin[...] = jnp.zeros((256, 128), F32)
    mark[...] = jnp.zeros((8, 128), F32)
    thin[:, 0:32] = gains[...].reshape(256, 32)
    for half in range(2):
        for c in range(4):
            total = None
            for im in range(2):
                for h in range(2):
                    part = thin[pl.ds((half * 16 + h * 8) * 8 + im * 4 + c, 8, stride=8), :]
                    if im or h:
                        part = pltpu.roll(part, im * 64 + h * 32, 1)
                    total = part if total is None else total + part
            for d in range(8):
                at = (2 * d + half) * 32 + c * 8
                spread[at:at + 8, :] = total


def prepare_kernel(
    mark, coh_hbm, gains_hbm, duals_hbm, poly_hbm, pairs, penalty, tables,
    coh_keep, state_keep, rho_a, rho_f, send_0, send_1, send_2, send_3,
    coh, gains, duals, poly, wide, thin, sems,
):
    send = (send_0, send_1, send_2, send_3)
    copies = [
        pltpu.make_async_copy(src, dst, sems.at[i])
        for i, (src, dst) in enumerate(((gains_hbm, gains), (duals_hbm, duals), (poly_hbm, poly), (coh_hbm, coh)))
    ]
    for copy in copies:
        copy.start()
    core = lax.axis_index("core")
    chan = lax.axis_index("chan")
    row = lax.broadcasted_iota(jnp.int32, (8, 128), 0)
    lane = lanes()
    by_dir = jnp.zeros((8, 128), F32)
    half_dir = jnp.zeros((8, 128), F32)
    for q in range(4):
        for s in range(8):
            here = row == s
            by_dir = jnp.where(here & (lane // 32 == q), penalty[q * 8 + s], by_dir)
    for q in range(2):
        for s in range(8):
            here = row == s
            half_dir = jnp.where(here & (lane // 64 == q), penalty[core * 16 + q * 8 + s], half_dir)
    rho_a[...] = half_dir
    rho_f[...] = by_dir
    send_3[32:40, :] = jnp.zeros((8, ROWS), F32)
    send_3[32:34, :] = pairs[...].astype(F32)

    def pack(which):
        for c in range(8):
            for keep, half in ((True, core), (False, 1 - core)):
                total = None
                for h in range(2):
                    part = thin[pl.ds((half * 16 + h * 8) * 8 + c, 8, stride=8), :]
                    part = pltpu.roll(part, h * 64 + core * 32, 1)
                    total = part if total is None else total + part
                if keep:
                    state_keep[which * 64 + c * 8:which * 64 + (c + 1) * 8, :] = total
                else:
                    send[which][32:40, c * 128:(c + 1) * 128] = total

    thin[...] = jnp.zeros((256, 128), F32)
    copies[0].wait()
    thin[:, 0:32] = gains[...].reshape(256, 32)
    pack(0)
    copies[1].wait()
    thin[:, 0:32] = duals[...].reshape(256, 32)
    pack(1)
    copies[2].wait()
    fitted = poly[:, :, 0, :] * tables[chan, 0]
    for t in range(1, TERMS):
        fitted = fitted + poly[:, :, t, :] * tables[chan, t]
    thin[:, 0:32] = fitted.reshape(256, 32)
    pack(2)
    copies[3].wait()
    for t in range(ROWS // 128):
        cols = slice(t * 128, (t + 1) * 128)
        wide[t] = coh[:, :, cols].astype(F32).reshape(256, 128)
        for c in range(8):
            coh_keep[c * 16:(c + 1) * 16, cols] = wide[t, pl.ds(core * 128 + c, 16, stride=8), :]
            send[c // 2][(c % 2) * 16:(c % 2) * 16 + 16, cols] = wide[t, pl.ds((1 - core) * 128 + c, 16, stride=8), :]


def one_hot(pairs, side, j):
    index = jnp.broadcast_to(pairs[side:side + 1, j * BLOCK:(j + 1) * BLOCK], (16, BLOCK)).astype(jnp.int16)
    index = jnp.concatenate([index] * (STATIONS // 16), axis=0)
    here = lax.broadcasted_iota(jnp.int16, (STATIONS, BLOCK), 0) == index
    return jnp.where(here, jnp.ones((STATIONS, BLOCK), BF16), jnp.zeros((STATIONS, BLOCK), BF16))


def put_table(table, c, t, first, second):
    high, rest = split_parts(jnp.concatenate([first, second], axis=0))
    table[c * 16:(c + 1) * 16, t * 128:(t + 1) * 128] = high
    table[128 + c * 16:128 + (c + 1) * 16, t * 128:(t + 1) * 128] = rest


def start_table(gathered, table):
    lane = lanes()
    for c in range(8):
        im, row = divmod(c, 4)
        for t in range(4):
            halves = []
            for h in range(2):
                total = None
                for b in range(4):
                    part = gathered[(4 * t + b) * 32 + row * 8:(4 * t + b) * 32 + row * 8 + 8, :]
                    shift = (b * 32 - im * 64 - h * 32) % 128
                    if shift:
                        part = pltpu.roll(part, shift, 1)
                    total = part if total is None else jnp.where(lane // 32 == b, part, total)
                halves.append(total)
            put_table(table, c, t, *halves)


def step_table(gathered, table):
    low = lanes() < 64
    for c in range(8):
        for t in range(4):
            a = gathered[(2 * t) * 64 + c * 8:(2 * t) * 64 + c * 8 + 8, :]
            b = gathered[(2 * t + 1) * 64 + c * 8:(2 * t + 1) * 64 + c * 8 + 8, :]
            first = jnp.where(low, a, pltpu.roll(b, 64, 1))
            second = jnp.where(low, pltpu.roll(a, 64, 1), b)
            put_table(table, c, t, first, second)


def first_model_kernel(
    gathered, coh_own, recv_0, recv_1, recv_2, recv_3, vis, pairs_own, state_keep, rho_a,
    z_ref, w_ref, s_ref, pairs, gains, duals, target, table, near, far,
):
    received = (recv_0, recv_1, recv_2, recv_3)
    pairs[0:2, 0:ROWS] = pairs_own[...]
    pairs[0:2, ROWS:] = recv_3[32:34, :].astype(jnp.int32)
    half_rho = 0.5 * rho_a[...]
    for c in range(8):
        at = c * 8
        state = [
            state_keep[which * 64 + at:which * 64 + at + 8, :]
            + received[which][32:40, c * 128:(c + 1) * 128]
            for which in range(3)
        ]
        gains[at:at + 8, :] = state[0]
        duals[at:at + 8, :] = state[1]
        target[at:at + 8, :] = half_rho * state[2] - 0.5 * state[1]
    start_table(gathered, table)
    model(coh_own, received, vis, pairs, z_ref, w_ref, s_ref, table, near, far)


def model_kernel(
    gathered, coh_own, recv_0, recv_1, recv_2, recv_3, vis, pairs, z_ref, w_ref, s_ref, table, near, far
):
    received = (recv_0, recv_1, recv_2, recv_3)
    step_table(gathered, table)
    model(coh_own, received, vis, pairs, z_ref, w_ref, s_ref, table, near, far)


def model(coh_own, received, vis, pairs, z_ref, w_ref, s_ref, table, near, far):
    for j in range(2 * ROWS // BLOCK):
        own = j < ROWS // BLOCK
        col = (j * BLOCK) % ROWS
        for side, dest in ((0, near), (1, far)):
            both = jnp.dot(table[...], one_hot(pairs, side, j), preferred_element_type=F32)
            dest[j % 2] = both[:128] + both[128:]
        for l in range(BLOCK // 128):
            src = col + l * 128
            dst = j * BLOCK + l * 128
            gp = matrix(lambda i: near[j % 2, i * 16:(i + 1) * 16, l * 128:(l + 1) * 128])
            gq = matrix(lambda i: far[j % 2, i * 16:(i + 1) * 16, l * 128:(l + 1) * 128])
            if own:
                cc = matrix(lambda i: coh_own[i * 16:(i + 1) * 16, src:src + 128])
            else:
                cc = matrix(lambda i: received[i // 2][(i % 2) * 16:(i % 2) * 16 + 16, src:src + 128])
            z = product_nh(cc, gq)
            w = product(gp, cc)
            m = product(gp, z)
            for i in range(8):
                z_ref[i * 16:(i + 1) * 16, dst:dst + 128] = z[i // 4][i % 4]
                w_ref[i * 16:(i + 1) * 16, dst:dst + 128] = w[i // 4][i % 4]
                total = -jnp.sum(m[i // 4][i % 4], axis=0, keepdims=True)
                if own:
                    total = total + vis[i:i + 1, src:src + 128]
                s_ref[i:i + 1, dst:dst + 128] = total


def sums_kernel(z_ref, w_ref, s_own, s_other, pairs, out, left, acc, hot):
    steps = 2 * ROWS // BLOCK
    for j in range(steps):
        for l in range(BLOCK // 128):
            src = j * BLOCK + l * 128
            swapped = (src + ROWS) % (2 * ROWS)
            r = matrix(lambda i: s_own[i:i + 1, src:src + 128] + s_other[i:i + 1, swapped:swapped + 128])
            z = matrix(lambda i: z_ref[i * 16:(i + 1) * 16, src:src + 128])
            w = matrix(lambda i: w_ref[i * 16:(i + 1) * 16, src:src + 128])
            for side, (num, den) in enumerate(
                ((product_nh(r, z), square_nh(z)), (product_hn(r, w), square_hn(w)))
            ):
                at = side * BLOCK + l * 128
                for i, value in enumerate(num[0] + num[1] + den):
                    high, rest = split_parts(value)
                    left[j, i * 16:(i + 1) * 16, at:at + 128] = high
                    left[j, 192 + i * 16:192 + (i + 1) * 16, at:at + 128] = rest
        for side in range(2):
            hot[j, :, side * BLOCK:(side + 1) * BLOCK] = one_hot(pairs, side, j)
        total = lax.dot_general(left[j], hot[j], (((1,), (1,)), ((), ())), preferred_element_type=F32)
        if j == 0:
            acc[...] = total
        else:
            acc[...] += total
    low = lanes() < 64
    for c in range(12):
        for t in range(4):
            cols = slice(t * 128, (t + 1) * 128)
            at = c * 16
            v0 = acc[at:at + 8, cols] + acc[192 + at:192 + at + 8, cols]
            v1 = acc[at + 8:at + 16, cols] + acc[192 + at + 8:192 + at + 16, cols]
            out[(2 * t) * 96 + c * 8:(2 * t) * 96 + c * 8 + 8, :] = jnp.where(low, v0, pltpu.roll(v1, 64, 1))
            out[(2 * t + 1) * 96 + c * 8:(2 * t + 1) * 96 + c * 8 + 8, :] = jnp.where(low, pltpu.roll(v0, 64, 1), v1)


def updated(received, gains, target, rho):
    sums = []
    for c in range(12):
        parts = [received[d * 96 + c * 8:d * 96 + c * 8 + 8, :] for d in range(8)]
        while len(parts) > 1:
            parts = [parts[i] + parts[i + 1] for i in range(0, len(parts), 2)]
        sums.append(parts[0])
    half_rho = 0.5 * rho
    a, d, br, bi = sums[8] + half_rho, sums[9] + half_rho, sums[10], sums[11]
    scale = 0.5 / (a * d - br * br - bi * bi)
    n = [sums[i] + target[i] - half_rho * gains[i] for i in range(8)]
    result = [None] * 8
    for i in (0, 1):
        r0, r1, i0, i1 = n[2 * i], n[2 * i + 1], n[4 + 2 * i], n[5 + 2 * i]
        result[2 * i] = gains[2 * i] + scale * (r0 * d - (r1 * br + i1 * bi))
        result[4 + 2 * i] = gains[4 + 2 * i] + scale * (i0 * d - (i1 * br - r1 * bi))
        result[2 * i + 1] = gains[2 * i + 1] + scale * (r1 * a - (r0 * br - i0 * bi))
        result[5 + 2 * i] = gains[5 + 2 * i] + scale * (i1 * a - (i0 * br + r0 * bi))
    return result


def comps(ref):
    return [ref[c * 8:(c + 1) * 8, :] for c in range(8)]


def put(ref, values, base=0):
    for c in range(8):
        ref[base + c * 8:base + (c + 1) * 8, :] = values[c]


def update_kernel(received, gains, target, rho_a, gains_new, spread):
    new = updated(received, comps(gains), comps(target), rho_a[...])
    put(gains_new, new)
    for d in range(8):
        put(spread, new, d * 64)


def update_moment_kernel(received, gains, target, duals, rho_a, gains_new, spread, moment):
    rho = rho_a[...]
    new = updated(received, comps(gains), comps(target), rho)
    put(gains_new, new)
    old = comps(duals)
    whole = [old[c] + rho * new[c] for c in range(8)]
    for d in range(8):
        put(spread, new, d * 64)
        put(moment, whole, d * 64)


def fit(tables, row, moments, first, stride, count):
    result = []
    for c in range(count):
        total = None
        for f in range(CHANNELS):
            at = f * stride + first + c * 8
            part = tables[row, 4 + f] * moments[at:at + 8, :]
            total = part if total is None else total + part
        result.append(total)
    return result


def update_consensus_kernel(received, gains, moments, duals, rho_a, tables, gains_new, spread, duals_new, target):
    rho = rho_a[...]
    chan = lax.axis_index("chan")
    old_gains = comps(gains)
    old_duals = comps(duals)
    fitted = fit(tables, chan, moments, 0, 64, 8)
    new_duals = [old_duals[c] + rho * (old_gains[c] - fitted[c]) for c in range(8)]
    aim = [0.5 * (rho * fitted[c] - new_duals[c]) for c in range(8)]
    put(duals_new, new_duals)
    put(target, aim)
    new = updated(received, old_gains, aim, rho)
    put(gains_new, new)
    for d in range(8):
        put(spread, new, d * 64)


def update_last_kernel(received, gains, target, duals, rho_a, keep, send, moment):
    core = lax.axis_index("core")
    rho = rho_a[...]
    new = updated(received, comps(gains), comps(target), rho)
    old = comps(duals)
    lane = lanes()
    quarter = lane // 32
    whole = [old[c] + rho * new[c] for c in range(8)]
    for half in range(2):
        for c in range(4):
            total = jnp.zeros((8, 128), F32)
            for im in range(2):
                for h in range(2):
                    here = jnp.where(quarter == 2 * h + half, whole[im * 4 + c], 0.0)
                    shift = (im * 64 - 32 * h - 32 * half) % 128
                    total = total + (pltpu.roll(here, shift, 1) if shift else here)
            for f in range(CHANNELS):
                at = (2 * f + half) * 32 + c * 8
                moment[at:at + 8, :] = total
    for out, stations in ((keep, core), (send, 1 - core)):
        for base, values in ((0, new), (64, old)):
            for c in range(8):
                total = jnp.zeros((8, 128), F32)
                for h in range(2):
                    here = jnp.where(quarter == 2 * h + stations, values[c], 0.0)
                    total = total + pltpu.roll(here, (64 * core + 96 * stations + 96 * h) % 128, 1)
                out[base + c * 8:base + (c + 1) * 8, :] = total


def finish_kernel(moments, keep, recv, rho_f, tables, gains, duals, poly, thin, deep):
    chan = lax.axis_index("chan")
    rho = rho_f[...]
    low = lanes() < 64

    def combine(row):
        parts = [fit(tables, row, moments, half * 32, 64, 4) for half in range(2)]
        real = [jnp.where(low, a, pltpu.roll(b, 64, 1)) for a, b in zip(*parts)]
        imag = [jnp.where(low, pltpu.roll(a, 64, 1), b) for a, b in zip(*parts)]
        return real + imag

    def place(ref, value, first, stride):
        for q in range(4):
            part = pltpu.roll(value, 128 - 32 * q, 1) if q else value
            ref[pl.ds(q * 8 * stride + first, 8, stride=stride), :] = part

    for t in range(TERMS):
        for c, value in enumerate(combine(8 + t)):
            place(deep, value, c * 4 + t, 32)
    poly[...] = deep[:, 0:32].reshape(32, 8, 4, 32)
    fitted = combine(chan)
    now = [keep[c * 8:(c + 1) * 8, :] + recv[c * 8:(c + 1) * 8, :] for c in range(16)]
    for c in range(8):
        place(thin, now[c], c, 8)
    gains[...] = thin[:, 0:32].reshape(32, 8, 32)
    for c in range(8):
        place(thin, now[8 + c] + rho * (now[c] - fitted[c]), c, 8)
    duals[...] = thin[:, 0:32].reshape(32, 8, 32)


def local(coherency, visibilities, station_pairs, gains, duals, poly, penalty):
    basis, solve, hat = consensus_tables()
    constants = np.zeros((12, 12), np.float32)
    constants[:8, :4] = basis
    constants[:8, 4:] = hat
    constants[8:, 4:] = solve
    tables = jnp.asarray(constants)

    def swap(x):
        return lax.ppermute(x, "core", CORE_SWAP)

    def exchange(x, axis):
        return lax.all_to_all(x, axis, 0, 0, tiled=True)

    packed = ((64, 128), F32)
    wide = ((512, 128), F32)
    small = ((8, 128), F32)
    state_in = pltpu.VMEM((32, 8, 32), F32)
    thin = pltpu.VMEM((256, 128), F32)
    spread, mark = call(
        spread_kernel, [wide, small], [thin], n_in=1
    )(gains[0])
    gathered = exchange(spread, ("st", "core"))
    coh_keep, state_keep, rho_a, rho_f, *send = call(
        prepare_kernel,
        [((128, ROWS), F32), ((192, 128), F32), small, small] + [((40, ROWS), F32)] * 4,
        [
            pltpu.VMEM((32, 8, ROWS), BF16), state_in, state_in, pltpu.VMEM((32, 8, TERMS, 32), F32),
            pltpu.VMEM((ROWS // 128, 256, 128), F32), thin, pltpu.SemaphoreType.DMA((4,)),
        ],
        smem=(6, 7), hbm=(0, 1, 2, 3, 4), n_in=8,
    )(mark, coherency[0], gains[0], duals[0], poly, station_pairs, penalty, tables)
    received = [swap(x) for x in send]
    vis = visibilities[0]

    model_outs = [((128, 2 * ROWS), F32), ((128, 2 * ROWS), F32), ((8, 2 * ROWS), F32)]
    model_scratch = [
        pltpu.VMEM((256, STATIONS), BF16), pltpu.VMEM((2, 128, BLOCK), F32), pltpu.VMEM((2, 128, BLOCK), F32)
    ]
    sums_out = ((768, 128), F32)
    blocks = 2 * ROWS // BLOCK
    sums_scratch = [
        pltpu.VMEM((blocks, 384, 2 * BLOCK), BF16),
        pltpu.VMEM((384, STATIONS), F32),
        pltpu.VMEM((blocks, STATIONS, 2 * BLOCK), BF16),
    ]
    z, w, own, pairs, gain, dual, target = call(
        first_model_kernel,
        model_outs + [((2, 2 * ROWS), jnp.int32), packed, packed, packed],
        model_scratch, n_in=10,
    )(gathered, coh_keep, *received, vis, station_pairs, state_keep, rho_a)

    def step_model(spread):
        gathered = exchange(spread, "st")
        return call(model_kernel, model_outs, model_scratch, n_in=8)(
            gathered, coh_keep, *received, vis, pairs
        )

    def step_sums(z, w, own):
        (parts,) = call(sums_kernel, [sums_out], sums_scratch, n_in=5)(z, w, own, swap(own), pairs)
        return exchange(parts, "st")

    gain, spread = call(update_kernel, [packed, wide], n_in=4)(step_sums(z, w, own), gain, target, rho_a)
    gain, spread, moment = call(update_moment_kernel, [packed, wide, wide], n_in=5)(
        step_sums(*step_model(spread)), gain, target, dual, rho_a
    )
    moments = exchange(moment, "chan")
    gain, spread, dual, target = call(
        update_consensus_kernel, [packed, wide, packed, packed], smem=(5,), n_in=6
    )(step_sums(*step_model(spread)), gain, moments, dual, rho_a, tables)
    keep, send, moment = call(update_last_kernel, [((128, 128), F32), ((128, 128), F32), wide], n_in=5)(
        step_sums(*step_model(spread)), gain, target, dual, rho_a
    )
    moments = exchange(moment, ("chan", "core"))
    gains_out, duals_out, poly_out = call(
        finish_kernel,
        [((32, 8, 32), F32), ((32, 8, 32), F32), ((32, 8, 4, 32), F32)],
        [pltpu.VMEM((256, 128), F32), pltpu.VMEM((1024, 128), F32)],
        smem=(4,), n_in=5,
    )(moments, keep, swap(send), rho_f, tables)
    return gains_out[None], duals_out[None], poly_out


def solution(mesh):
    chan, bl = mesh.devices.shape
    finer = Mesh(mesh.devices.reshape(chan, bl // 2, 2), ("chan", "st", "core"))
    both = ("st", "core")
    in_specs = (
        P("chan", None, None, both),
        P("chan", None, both),
        P(None, both),
        P("chan", None, None, both),
        P("chan", None, None, both),
        P(None, None, None, both),
        P(),
    )
    out_specs = (
        P("chan", None, None, both),
        P("chan", None, None, both),
        P(None, None, None, both),
    )
    return jax.shard_map(local, mesh=finer, in_specs=in_specs, out_specs=out_specs, check_vma=False)
```

time: 156 us -> 146 us (0.936)
  blocking collectives: 79.7 us -> 67.6 us
  starting transfers between devices: 30.9 us -> 35.9 us
  Pallas kernels: 27.2 us -> 23.7 us
  waiting for transfers between devices: 11.3 us -> 13.3 us
    all_to_all x8 -> x7, blocking collectives: 79.7 us -> 67.6 us  [exchange(): return lax.all_to_all(x, axis, 0, 0, tiled=True)]
    all_to_all x2 -> x3, starting transfers between devices: 12.8 us -> 21.5 us  [exchange(): return lax.all_to_all(x, axis, 0, 0, tiled=True)]
    ppermute x8 -> x9, starting transfers between devices: 18.1 us -> 14.4 us  [swap(): return lax.ppermute(x, 'core', CORE_SWAP)]
    pallas_call x12 -> x11, Pallas kernels: 23.6 us -> 20 us  [the longest x4 8.04 us: step_sums(): call(sums_kernel, [sums_out], sums_scratch, n_in=5)]
    all_to_all x2 -> x3, waiting for transfers between devices: 4.38 us -> 7.43 us  [exchange(): return lax.all_to_all(x, axis, 0, 0, tiled=True)]
    ppermute x8 -> x9, waiting for transfers between devices: 6.93 us -> 5.87 us  [swap(): return lax.ppermute(x, 'core', CORE_SWAP)]
    unnamed x18 -> x20, local copies, waits for them, and re-layouts: 5.25 us -> 4.24 us
  transfers between devices with their start and end apart: 10 -> 12, of which waited for: 8 -> 10; matrix products, arithmetic and copies ran while one was open for 0% -> 0% of each run, Pallas kernels for 4% -> 4%
where the time goes in v2:
time: 146 us
  blocking collectives  67.6 us (46%)
  starting transfers between devices  35.9 us (25%)
  Pallas kernels  23.7 us (16%)
  waiting for transfers between devices  13.3 us (9%)
  local copies, waits for them, and re-layouts  4.24 us (3%)
    all_to_all x7, blocking collectives, exchange(): return lax.all_to_all(x, axis, 0, 0, tiled=True)  67.6 us
    all_to_all x3, starting transfers between devices, exchange(): return lax.all_to_all(x, axis, 0, 0, tiled=True)  21.5 us
    ppermute x9, starting transfers between devices, swap(): return lax.ppermute(x, 'core', CORE_SWAP)  14.4 us
    pallas_call x4, Pallas kernels, step_sums(): call(sums_kernel, [sums_out], sums_scratch, n_in=5)  8.04 us
    all_to_all x3, waiting for transfers between devices, exchange(): return lax.all_to_all(x, axis, 0, 0, tiled=True)  7.43 us
    ppermute x9, waiting for transfers between devices, swap(): return lax.ppermute(x, 'core', CORE_SWAP)  5.87 us
    pallas_call x3, Pallas kernels, step_model(): call(model_kernel, model_outs, model_scratch, n_in=8)  5.85 us
    unnamed x20, local copies, waits for them, and re-layouts  4.24 us
  transfers between devices with their start and end apart: 12, of which 10 were waited for; matrix products, arithmetic and copies ran while one was open for 0% of the time, Pallas kernels for 4%

profile of v2, /device:TPU:1, one launch (start us, length us, event | category | flops | bytes accessed | tf_op | source)
XLA Modules:
  0.0 145.5 jit_solution(3363075302509078566)
XLA Ops:
  0.6 0.0 copy-start
  0.6 0.0 copy-start.3
  0.7 1.0 copy-done.3
  1.6 0.8 shard_map.103
  2.4 0.0 copy-start.4
  2.4 0.0 copy-start.6
  2.4 7.3 %all-to-all-start = ((f32[16,32,128]{2,1,0:T(8,128)}), f32[16,32,128]{2,1,0:T(8,128)S(1)}, u32[]{:S(2)}, u32[]{:S(2)}) async-start(f32[16,32,128]{2,1,0:T(8,128)} %bitcast.1), calls=%async_computation | async-start | bytes 524288 | tf_op jit(solution)/shard_map/all_to_all | solution.py:482
  9.7 0.0 copy-start.9
  9.7 0.0 copy-done
  9.8 0.0 copy-done.4
  9.8 0.0 copy-done.6
  9.8 0.6 copy-done.9
  10.4 0.0 copy-start.1
  10.4 1.0 copy-done.1
  11.4 0.0 copy-start.5
  11.4 0.9 copy-done.5
  12.3 0.7 copy-done.7
  13.0 2.3 %shard_map.104 = (f32[128,1024]{1,0:T(8,128)S(1)}, f32[192,128]{1,0:T(8,128)S(1)}, f32[8,128]{1,0:T(8,128)S(1)}, f32[8,128]{1,0:T(8,128)S(1)}, f32[40,1024]{1,0:...) custom-call(f32[8,128]{1,0:T(8,128)S(1)} %get-tuple-element.45.mark, ...), custom_call_target="tpu_custom_call" | custom-call | bytes 1000 | tf_op jit(solution)/shard_map/pallas_call | solution.py:493
  15.4 0.0 copy-start.8
  15.4 0.2 collective-permute-start
  15.6 0.4 collective-permute-start.1
  16.0 0.1 collective-permute-start.2
  16.1 0.4 collective-permute-start.3
  16.5 0.4 collective-permute-done.recv_0
  16.9 0.2 collective-permute-done.1.recv_1
  17.1 0.3 collective-permute-done.2.recv_2
  17.4 0.2 collective-permute-done.3.recv_3
  17.6 0.0 all-to-all-done
  17.6 0.0 copy-done.2
  17.6 0.0 copy-done.8
  17.6 2.1 %shard_map.105 = (f32[128,2048]{1,0:T(8,128)S(1)}, f32[128,2048]{1,0:T(8,128)S(1)}, f32[8,2048]{1,0:T(8,128)S(1)}, s32[2,2048]{1,0:T(2,128)S(1)}, f32[64,128]{1,...) custom-call(f32[512,128]{1,0:T(8,128)S(1)} %bitcast.35, f32[128,1024]{1,0:T(8,128)S(1)} %get-tuple-element.46.coh_own, ...), custom_call_target="tpu_custom_call" | custom-call | bytes 1000 | tf_op jit(solution)/shard_map/pallas_call | solution.py:516
  19.7 0.4 collective-permute-start.4
  20.1 1.0 collective-permute-done.4.s_other
  21.0 2.1 %shard_map.106 = f32[768,128]{1,0:T(8,128)S(1)} custom-call(f32[128,2048]{1,0:T(8,128)S(1)} %get-tuple-element.53.z_ref, f32[128,2048]{1,0:T(8,128)S(1)} %get-tuple-element.54.w_ref, f32[8,2048]{1,0:T(8,128)S(1)} %get-tuple-element.55.s_own, f32[8,2048]{1,0:T(8,128)S(1)} %collective-permute-done.4.s_other, s32[2,2048]{1,0:T(2,128)S(1)} %get-tuple-element.56.pairs), custom_call_target="tpu_custom_call" | custom-call | bytes 1000 | tf_op jit(solution)/shard_map/pallas_call | solution.py:529
  23.1 12.7 %all_to_all.110 = f32[8,96,128]{2,1,0:T(8,128)S(1)} all-to-all(f32[8,96,128]{2,1,0:T(8,128)S(1)} %bitcast.29), channel_id=1, replica_groups=mesh['chan'=8,'st'=8,'core'=2] {'st'}, dimensions={0} | all-to-all | bytes 786432 | tf_op jit(solution)/shard_map/all_to_all | solution.py:482
  35.9 0.1 shard_map.107
  35.9 8.6 %all_to_all.111 = f32[8,64,128]{2,1,0:T(8,128)S(1)} all-to-all(f32[8,64,128]{2,1,0:T(8,128)S(1)} %bitcast.49), channel_id=1, replica_groups=mesh['chan'=8,'st'=8,'core'=2] {'st'}, dimensions={0} | all-to-all | bytes 524288 | tf_op jit(solution)/shard_map/all_to_all | solution.py:482
  44.5 2.0 %shard_map.108 = (f32[128,2048]{1,0:T(8,128)S(1)}, f32[128,2048]{1,0:T(8,128)S(1)}, f32[8,2048]{1,0:T(8,128)S(1)}) custom-call(f32[512,128]{1,0:T(8,128)S(1)} %bitcast.39, f32[128,1024]{1,0:T(8,128)S(1)} %get-tuple-element.46.coh_own, f32[40,1024]{1,0:T(8,128)S(1)} %collective-permute-done.recv_0, f32[40,1024]{1,0:T(8,128)S(1)} %collective-permute-done.1.recv_1, ...), custom_call_target="tpu_custom_call" | custom-call | bytes 1000 | tf_op jit(solution)/shard_map/pallas_call | solution.py:524
  46.4 2.9 %collective-permute-start.5 = (f32[8,2048]{1,0:T(8,128)S(1)}, f32[8,2048]{1,0:T(8,128)S(1)}, u32[]{:S(2)}, u32[]{:S(2)}) collective-permute-start(f32[8,2048]{1,0:T(8,128)S(1)} %get-tuple-element.62.s_own), channel_id=1, source_target_pairs={{0,1},{1,0},{2,3},{3,2},{4,5},{5,4},{6,7},{7,6},{8,9},{9,8},{10,11... | collective-permute-start | bytes 196616 | tf_op jit(solution)/shard_map/ppermute | solution.py:479
  49.3 0.9 collective-permute-done.5.s_other
  50.2 2.0 %shard_map.109 = f32[768,128]{1,0:T(8,128)S(1)} custom-call(f32[128,2048]{1,0:T(8,128)S(1)} %get-tuple-element.60.z_ref, f32[128,2048]{1,0:T(8,128)S(1)} %get-tuple-element.61.w_ref, f32[8,2048]{1,0:T(8,128)S(1)} %get-tuple-element.62.s_own, f32[8,2048]{1,0:T(8,128)S(1)} %collective-permute-done.5.s_other, s32[2,2048]{1,0:T(2,128)S(1)} %get-tuple-element.56.pairs), custom_call_target="tpu_custom_call" | custom-call | bytes 1000 | tf_op jit(solution)/shard_map/pallas_call | solution.py:529
  52.2 10.2 %all_to_all.112 = f32[8,96,128]{2,1,0:T(8,128)S(1)} all-to-all(f32[8,96,128]{2,1,0:T(8,128)S(1)} %bitcast.31), channel_id=1, replica_groups=mesh['chan'=8,'st'=8,'core'=2] {'st'}, dimensions={0} | all-to-all | bytes 786432 | tf_op jit(solution)/shard_map/all_to_all | solution.py:482
  62.4 0.8 shard_map.110
  63.2 8.6 %all_to_all.113 = f32[8,64,128]{2,1,0:T(8,128)S(1)} all-to-all(f32[8,64,128]{2,1,0:T(8,128)S(1)} %bitcast.48), channel_id=1, replica_groups=mesh['chan'=8,'st'=8,'core'=2] {'st'}, dimensions={0} | all-to-all | bytes 524288 | tf_op jit(solution)/shard_map/all_to_all | solution.py:482
  71.8 7.2 %all-to-all-start.6 = ((f32[8,64,128]{2,1,0:T(8,128)}), f32[8,64,128]{2,1,0:T(8,128)S(1)}, u32[]{:S(2)}, u32[]{:S(2)}) async-start(f32[8,64,128]{2,1,0:T(8,128)} %bitcast.16), calls=%async_computation.6 | async-start | bytes 524288 | tf_op jit(solution)/shard_map/all_to_all | solution.py:482
  79.0 2.0 %shard_map.111 = (f32[128,2048]{1,0:T(8,128)S(1)}, f32[128,2048]{1,0:T(8,128)S(1)}, f32[8,2048]{1,0:T(8,128)S(1)}) custom-call(f32[512,128]{1,0:T(8,128)S(1)} %bitcast.37, f32[128,1024]{1,0:T(8,128)S(1)} %get-tuple-element.46.coh_own, f32[40,1024]{1,0:T(8,128)S(1)} %collective-permute-done.recv_0, f32[40,1024]{1,0:T(8,128)S(1)} %collective-permute-done.1.recv_1, ...), custom_call_target="tpu_custom_call" | custom-call | bytes 1000 | tf_op jit(solution)/shard_map/pallas_call | solution.py:524
  81.0 3.2 %collective-permute-start.6 = (f32[8,2048]{1,0:T(8,128)S(1)}, f32[8,2048]{1,0:T(8,128)S(1)}, u32[]{:S(2)}, u32[]{:S(2)}) collective-permute-start(f32[8,2048]{1,0:T(8,128)S(1)} %get-tuple-element.68.s_own), channel_id=1, source_target_pairs={{0,1},{1,0},{2,3},{3,2},{4,5},{5,4},{6,7},{7,6},{8,9},{9,8},{10,11... | collective-permute-start | bytes 196616 | tf_op jit(solution)/shard_map/ppermute | solution.py:479
  84.2 0.9 collective-permute-done.6.s_other
  85.1 2.0 %shard_map.112 = f32[768,128]{1,0:T(8,128)S(1)} custom-call(f32[128,2048]{1,0:T(8,128)S(1)} %get-tuple-element.66.z_ref, f32[128,2048]{1,0:T(8,128)S(1)} %get-tuple-element.67.w_ref, f32[8,2048]{1,0:T(8,128)S(1)} %get-tuple-element.68.s_own, f32[8,2048]{1,0:T(8,128)S(1)} %collective-permute-done.6.s_other, s32[2,2048]{1,0:T(2,128)S(1)} %get-tuple-element.56.pairs), custom_call_target="tpu_custom_call" | custom-call | bytes 1000 | tf_op jit(solution)/shard_map/pallas_call | solution.py:529
  87.1 0.0 all-to-all-done.6
  87.1 9.1 %all_to_all.114 = f32[8,96,128]{2,1,0:T(8,128)S(1)} all-to-all(f32[8,96,128]{2,1,0:T(8,128)S(1)} %bitcast.26), channel_id=1, replica_groups=mesh['chan'=8,'st'=8,'core'=2] {'st'}, dimensions={0} | all-to-all | bytes 786432 | tf_op jit(solution)/shard_map/all_to_all | solution.py:482
  96.2 0.7 shard_map.113
  97.0 8.2 %all_to_all.115 = f32[8,64,128]{2,1,0:T(8,128)S(1)} all-to-all(f32[8,64,128]{2,1,0:T(8,128)S(1)} %bitcast.47), channel_id=1, replica_groups=mesh['chan'=8,'st'=8,'core'=2] {'st'}, dimensions={0} | all-to-all | bytes 524288 | tf_op jit(solution)/shard_map/all_to_all | solution.py:482
  105.2 2.0 %shard_map.114 = (f32[128,2048]{1,0:T(8,128)S(1)}, f32[128,2048]{1,0:T(8,128)S(1)}, f32[8,2048]{1,0:T(8,128)S(1)}) custom-call(f32[512,128]{1,0:T(8,128)S(1)} %bitcast.38, f32[128,1024]{1,0:T(8,128)S(1)} %get-tuple-element.46.coh_own, f32[40,1024]{1,0:T(8,128)S(1)} %collective-permute-done.recv_0, f32[40,1024]{1,0:T(8,128)S(1)} %collective-permute-done.1.recv_1, ...), custom_call_target="tpu_custom_call" | custom-call | bytes 1000 | tf_op jit(solution)/shard_map/pallas_call | solution.py:524
  107.1 6.6 %collective-permute-start.7 = (f32[8,2048]{1,0:T(8,128)S(1)}, f32[8,2048]{1,0:T(8,128)S(1)}, u32[]{:S(2)}, u32[]{:S(2)}) collective-permute-start(f32[8,2048]{1,0:T(8,128)S(1)} %get-tuple-element.74.s_own), channel_id=1, source_target_pairs={{0,1},{1,0},{2,3},{3,2},{4,5},{5,4},{6,7},{7,6},{8,9},{9,8},{10,11... | collective-permute-start | bytes 196616 | tf_op jit(solution)/shard_map/ppermute | solution.py:479
  113.8 0.9 collective-permute-done.7.s_other
  114.7 2.0 %shard_map.115 = f32[768,128]{1,0:T(8,128)S(1)} custom-call(f32[128,2048]{1,0:T(8,128)S(1)} %get-tuple-element.72.z_ref, f32[128,2048]{1,0:T(8,128)S(1)} %get-tuple-element.73.w_ref, f32[8,2048]{1,0:T(8,128)S(1)} %get-tuple-element.74.s_own, f32[8,2048]{1,0:T(8,128)S(1)} %collective-permute-done.7.s_other, s32[2,2048]{1,0:T(2,128)S(1)} %get-tuple-element.56.pairs), custom_call_target="tpu_custom_call" | custom-call | bytes 1000 | tf_op jit(solution)/shard_map/pallas_call | solution.py:529
  116.7 10.2 %all_to_all.116 = f32[8,96,128]{2,1,0:T(8,128)S(1)} all-to-all(f32[8,96,128]{2,1,0:T(8,128)S(1)} %bitcast.28), channel_id=1, replica_groups=mesh['chan'=8,'st'=8,'core'=2] {'st'}, dimensions={0} | all-to-all | bytes 786432 | tf_op jit(solution)/shard_map/all_to_all | solution.py:482
  126.9 0.8 shard_map.116
  127.7 7.0 %all-to-all-start.9 = ((f32[16,32,128]{2,1,0:T(8,128)}), f32[16,32,128]{2,1,0:T(8,128)S(1)}, u32[]{:S(2)}, u32[]{:S(2)}) async-start(f32[16,32,128]{2,1,0:T(8,128)} %bitcast.22), calls=%async_computation.9 | async-start | bytes 524288 | tf_op jit(solution)/shard_map/all_to_all | solution.py:482
  134.7 0.2 collective-permute-start.8
  134.8 1.1 collective-permute-done.8.recv
  135.9 7.4 %all-to-all-done.9 = f32[16,32,128]{2,1,0:T(8,128)S(1)} async-done(((f32[16,32,128]{2,1,0:T(8,128)}), f32[16,32,128]{2,1,0:T(8,128)S(1)}, u32[]{:S(2)}, u32[]{:S(2)}) %all-to-all-start.9) | async-done | bytes 262176 | tf_op jit(solution)/shard_map/all_to_all | solution.py:482
  143.3 2.2 %shard_map.117 = (f32[32,8,32]{2,1,0:T(8,128)}, f32[32,8,32]{2,1,0:T(8,128)}, f32[32,8,4,32]{3,2,1,0:T(4,128)}) custom-call(f32[512,128]{1,0:T(8,128)S(1)} %bitcast.34, f32[128,128]{1,0:T(8,128)S(1)} %get-tuple-element.79.keep, f32[128,128]{1,0:T(8,128)S(1)} %collective-permute-done.8.recv, f32[8,128]{1,0:T(8,128)S(1)} %get-tuple-element.81.rho_f, ...), custom_call_target="tpu_custom_call" | custom-call | bytes 1000 | tf_op jit(solution)/shard_map/pallas_call | solution.py:544
  (2 shorter events, 0.0 us)
Async XLA Ops:
  0.6 9.1 %copy-start = (bf16[1,32,8,1024]{3,2,1,0:T(8,128)(2,1)S(1)}, bf16[1,32,8,1024]{3,2,1,0:T(8,128)(2,1)}, u32[]{:S(2)}) copy-start(bf16[1,32,8,1024]{3,2,1,0:T(8,128)(2,1)} %param.8) | copy-start | bytes 1572868
  0.6 1.0 copy-start.3
  2.4 7.3 %copy-start.4 = (f32[1,32,8,32]{3,2,1,0:T(8,128)S(1)}, f32[1,32,8,32]{3,2,1,0:T(8,128)}, u32[]{:S(2)}) copy-start(f32[1,32,8,32]{3,2,1,0:T(8,128)} %param.11) | copy-start | bytes 98308
  2.4 7.3 %copy-start.6 = (f32[12,12]{1,0:T(8,128)S(1)}, f32[12,12]{1,0:T(8,128)}, u32[]{:S(2)}) copy-start(f32[12,12]{1,0:T(8,128)} %constant.2.clone.tables) | copy-start | bytes 1732
  2.4 15.2 %all-to-all-start = ((f32[16,32,128]{2,1,0:T(8,128)}), f32[16,32,128]{2,1,0:T(8,128)S(1)}, u32[]{:S(2)}, u32[]{:S(2)}) async-start(f32[16,32,128]{2,1,0:T(8,128)} %bitcast.1), calls=%async_computation | async-start | bytes 524288 | tf_op jit(solution)/shard_map/all_to_all | solution.py:482
  9.7 0.7 copy-start.9
  10.4 1.0 copy-start.1
  11.4 0.9 copy-start.5
  12.3 0.7 copy-start.7
  13.0 4.6 %copy-start.2 = (f32[1,8,1024]{2,1,0:T(8,128)S(1)}, f32[1,8,1024]{2,1,0:T(8,128)}, u32[]{:S(2)}) copy-start(f32[1,8,1024]{2,1,0:T(8,128)} %param.9) | copy-start | bytes 98308
  15.4 2.2 %copy-start.8 = (s32[2,1024]{1,0:T(2,128)S(1)}, s32[2,1024]{1,0:T(2,128)}, u32[]{:S(2)}) copy-start(s32[2,1024]{1,0:T(2,128)} %pairs_own.1) | copy-start | bytes 24580
  15.4 1.5 %collective-permute-start = (f32[40,1024]{1,0:T(8,128)S(1)}, f32[40,1024]{1,0:T(8,128)S(1)}, u32[]{:S(2)}, u32[]{:S(2)}) collective-permute-start(f32[40,1024]{1,0:T(8,128)S(1)} %get-tuple-element.47), channel_id=1, source_target_pairs={{0,1},{1,0},{2,3},{3,2},{4,5},{5,4},{6,7},{7,6},{8,9},{9,8},{10,11... | collective-permute-start | bytes 491528 | tf_op jit(solution)/shard_map/ppermute | solution.py:479
  15.6 1.5 %collective-permute-start.1 = (f32[40,1024]{1,0:T(8,128)S(1)}, f32[40,1024]{1,0:T(8,128)S(1)}, u32[]{:S(2)}, u32[]{:S(2)}) collective-permute-start(f32[40,1024]{1,0:T(8,128)S(1)} %get-tuple-element.48), channel_id=1, source_target_pairs={{0,1},{1,0},{2,3},{3,2},{4,5},{5,4},{6,7},{7,6},{8,9},{9,8},{10,11... | collective-permute-start | bytes 491528 | tf_op jit(solution)/shard_map/ppermute | solution.py:479
  16.0 1.4 collective-permute-start.2
  16.1 1.5 %collective-permute-start.3 = (f32[40,1024]{1,0:T(8,128)S(1)}, f32[40,1024]{1,0:T(8,128)S(1)}, u32[]{:S(2)}, u32[]{:S(2)}) collective-permute-start(f32[40,1024]{1,0:T(8,128)S(1)} %get-tuple-element.50), channel_id=1, source_target_pairs={{0,1},{1,0},{2,3},{3,2},{4,5},{5,4},{6,7},{7,6},{8,9},{9,8},{10,11... | collective-permute-start | bytes 491528 | tf_op jit(solution)/shard_map/ppermute | solution.py:479
  19.7 1.3 collective-permute-start.4
  46.4 3.8 %collective-permute-start.5 = (f32[8,2048]{1,0:T(8,128)S(1)}, f32[8,2048]{1,0:T(8,128)S(1)}, u32[]{:S(2)}, u32[]{:S(2)}) collective-permute-start(f32[8,2048]{1,0:T(8,128)S(1)} %get-tuple-element.62.s_own), channel_id=1, source_target_pairs={{0,1},{1,0},{2,3},{3,2},{4,5},{5,4},{6,7},{7,6},{8,9},{9,8},{10,11... | collective-permute-start | bytes 196616 | tf_op jit(solution)/shard_map/ppermute | solution.py:479
  71.8 15.3 %all-to-all-start.6 = ((f32[8,64,128]{2,1,0:T(8,128)}), f32[8,64,128]{2,1,0:T(8,128)S(1)}, u32[]{:S(2)}, u32[]{:S(2)}) async-start(f32[8,64,128]{2,1,0:T(8,128)} %bitcast.16), calls=%async_computation.6 | async-start | bytes 524288 | tf_op jit(solution)/shard_map/all_to_all | solution.py:482
  81.0 4.1 %collective-permute-start.6 = (f32[8,2048]{1,0:T(8,128)S(1)}, f32[8,2048]{1,0:T(8,128)S(1)}, u32[]{:S(2)}, u32[]{:S(2)}) collective-permute-start(f32[8,2048]{1,0:T(8,128)S(1)} %get-tuple-element.68.s_own), channel_id=1, source_target_pairs={{0,1},{1,0},{2,3},{3,2},{4,5},{5,4},{6,7},{7,6},{8,9},{9,8},{10,11... | collective-permute-start | bytes 196616 | tf_op jit(solution)/shard_map/ppermute | solution.py:479
  107.1 7.6 %collective-permute-start.7 = (f32[8,2048]{1,0:T(8,128)S(1)}, f32[8,2048]{1,0:T(8,128)S(1)}, u32[]{:S(2)}, u32[]{:S(2)}) collective-permute-start(f32[8,2048]{1,0:T(8,128)S(1)} %get-tuple-element.74.s_own), channel_id=1, source_target_pairs={{0,1},{1,0},{2,3},{3,2},{4,5},{5,4},{6,7},{7,6},{8,9},{9,8},{10,11... | collective-permute-start | bytes 196616 | tf_op jit(solution)/shard_map/ppermute | solution.py:479
  127.7 15.6 %all-to-all-start.9 = ((f32[16,32,128]{2,1,0:T(8,128)}), f32[16,32,128]{2,1,0:T(8,128)S(1)}, u32[]{:S(2)}, u32[]{:S(2)}) async-start(f32[16,32,128]{2,1,0:T(8,128)} %bitcast.22), calls=%async_computation.9 | async-start | bytes 524288 | tf_op jit(solution)/shard_map/all_to_all | solution.py:482
  134.7 1.3 collective-permute-start.8

commit v3 on v2

--- a/solution.py
+++ b/solution.py
@@ -16,29 +16,52 @@
 BF16 = jnp.bfloat16
 CORE_SWAP = [(0, 1), (1, 0)]
 VMEM_BYTES = 24 * 1024 * 1024
-WHOLE_BYTES = 60 * 1024 * 1024
+
+
+def basis_of(place):
+    square = place * place
+    return [1.0 + 0.0 * place, place, 1.5 * square - 0.5, (2.5 * square - 1.5) * place]
 
 
 def consensus_tables():
-    place = (2.0 * np.arange(CHANNELS) + 1.0) / CHANNELS - 1.0
-    basis = np.stack(
-        [np.ones_like(place), place, 1.5 * place**2 - 0.5, 2.5 * place**3 - 1.5 * place], axis=1
-    )
-    solve = np.linalg.solve(basis.T @ basis, basis.T)
-    return basis, solve, basis @ solve
-
-
-def call(kernel, out_shapes, scratch=(), smem=(), hbm=(), n_in=0, cost=0, room=VMEM_BYTES):
-    spaces = [pltpu.SMEM if i in smem else pl.ANY if i in hbm else pltpu.VMEM for i in range(n_in)]
-    in_specs = [pl.BlockSpec(memory_space=space) for space in spaces]
+    basis = np.stack(basis_of((2.0 * np.arange(CHANNELS) + 1.0) / CHANNELS - 1.0), axis=1)
+    inverse = np.linalg.inv(basis.T @ basis)
+    return inverse, inverse @ basis.T
+
+
+GRAM_INVERSE, SOLVE = consensus_tables()
+
+
+def basis_at(channel):
+    place = (2.0 * jnp.full((8, 128), channel, jnp.int32).astype(F32) + 1.0) / CHANNELS - 1.0
+    return basis_of(place)
+
+
+def dot_terms(a, b):
+    total = a[0] * b[0]
+    for t in range(1, TERMS):
+        total = total + a[t] * b[t]
+    return total
+
+
+def weigh(values):
+    return [
+        sum(float(GRAM_INVERSE[t, u]) * values[u] for u in range(t % 2, TERMS, 2)) for t in range(TERMS)
+    ]
+
+
+def call(kernel, out_shapes, scratch=(), hbm=(), hbm_out=(), n_in=0):
+    def specs(count, outside):
+        return [pl.BlockSpec(memory_space=pl.ANY if i in outside else pltpu.VMEM) for i in range(count)]
+
     return pl.pallas_call(
         kernel,
         out_shape=[jax.ShapeDtypeStruct(s, d) for s, d in out_shapes],
-        in_specs=in_specs,
-        out_specs=[pl.BlockSpec(memory_space=pltpu.VMEM) for _ in out_shapes],
+        in_specs=specs(n_in, hbm),
+        out_specs=specs(len(out_shapes), hbm_out),
         scratch_shapes=list(scratch),
-        compiler_params=pltpu.CompilerParams(vmem_limit_bytes=room),
-        cost_estimate=pl.CostEstimate(flops=0, bytes_accessed=cost * 3_000_000 + 1000, transcendentals=0),
+        compiler_params=pltpu.CompilerParams(vmem_limit_bytes=VMEM_BYTES),
+        cost_estimate=pl.CostEstimate(flops=0, bytes_accessed=1000, transcendentals=0),
     )
 
 
@@ -132,7 +155,7 @@
 
 
 def prepare_kernel(
-    mark, coh_hbm, gains_hbm, duals_hbm, poly_hbm, pairs, penalty, tables,
+    mark, coh_hbm, gains_hbm, duals_hbm, poly_hbm, pairs, penalty,
     coh_keep, state_keep, rho_a, rho_f, send_0, send_1, send_2, send_3,
     coh, gains, duals, poly, wide, thin, sems,
 ):
@@ -147,17 +170,15 @@
     chan = lax.axis_index("chan")
     row = lax.broadcasted_iota(jnp.int32, (8, 128), 0)
     lane = lanes()
-    by_dir = jnp.zeros((8, 128), F32)
-    half_dir = jnp.zeros((8, 128), F32)
-    for q in range(4):
-        for s in range(8):
-            here = row == s
-            by_dir = jnp.where(here & (lane // 32 == q), penalty[q * 8 + s], by_dir)
-    for q in range(2):
-        for s in range(8):
-            here = row == s
-            half_dir = jnp.where(here & (lane // 64 == q), penalty[core * 16 + q * 8 + s], half_dir)
-    rho_a[...] = half_dir
+    given = jnp.broadcast_to(penalty[...], (8, 128))
+    column = [jnp.sum(jnp.where(lane == q * 8 + row, given, 0.0), axis=1, keepdims=True) for q in range(4)]
+    by_dir = jnp.broadcast_to(column[0], (8, 128))
+    for q in range(1, 4):
+        by_dir = jnp.where(lane // 32 == q, column[q], by_dir)
+    mine = jnp.full((8, 128), core, jnp.int32) == 0
+    low = jnp.where(mine, column[0], column[2])
+    high = jnp.where(mine, column[1], column[3])
+    rho_a[...] = jnp.where(lane < 64, low, high)
     rho_f[...] = by_dir
     send_3[32:40, :] = jnp.zeros((8, ROWS), F32)
     send_3[32:34, :] = pairs[...].astype(F32)
@@ -183,9 +204,11 @@
     thin[:, 0:32] = duals[...].reshape(256, 32)
     pack(1)
     copies[2].wait()
-    fitted = poly[:, :, 0, :] * tables[chan, 0]
+    place = (2.0 * chan.astype(F32) + 1.0) * (1.0 / CHANNELS) - 1.0
+    basis = basis_of(place)
+    fitted = poly[:, :, 0, :]
     for t in range(1, TERMS):
-        fitted = fitted + poly[:, :, t, :] * tables[chan, t]
+        fitted = fitted + poly[:, :, t, :] * basis[t]
     thin[:, 0:32] = fitted.reshape(256, 32)
     pack(2)
     copies[3].wait()
@@ -267,6 +290,10 @@
     received = (recv_0, recv_1, recv_2, recv_3)
     step_table(gathered, table)
     model(coh_own, received, vis, pairs, z_ref, w_ref, s_ref, table, near, far)
+
+
+def model_after_kernel(gathered, coh_own, recv_0, recv_1, recv_2, recv_3, vis, pairs, after, *rest):
+    model_kernel(gathered, coh_own, recv_0, recv_1, recv_2, recv_3, vis, pairs, *rest)
 
 
 def model(coh_own, received, vis, pairs, z_ref, w_ref, s_ref, table, near, far):
@@ -295,6 +322,22 @@
                 if own:
                     total = total + vis[i:i + 1, src:src + 128]
                 s_ref[i:i + 1, dst:dst + 128] = total
+
+
+def message_sums_kernel(
+    z_ref, w_ref, s_own, s_other, pairs, moment, moment_z, out, part_0, part_1, part_2, part_3, left, acc, hot
+):
+    chan = lax.axis_index("chan")
+    near = weigh(basis_at(chan))
+    far = weigh(basis_at(chan ^ 4))
+    own = comps(moment)
+    other = comps(moment_z)
+    for d, part in enumerate((part_0, part_1, part_2, part_3)):
+        at = basis_at(chan ^ d)
+        near_weight = dot_terms(at, near)
+        far_weight = dot_terms(at, far)
+        put(part, [near_weight * own[c] + far_weight * other[c] for c in range(8)])
+    sums_kernel(z_ref, w_ref, s_own, s_other, pairs, out, left, acc, hot)
 
 
 def sums_kernel(z_ref, w_ref, s_own, s_other, pairs, out, left, acc, hot):
@@ -373,31 +416,20 @@
     rho = rho_a[...]
     new = updated(received, comps(gains), comps(target), rho)
     put(gains_new, new)
-    old = comps(duals)
-    whole = [old[c] + rho * new[c] for c in range(8)]
     for d in range(8):
         put(spread, new, d * 64)
-        put(moment, whole, d * 64)
-
-
-def fit(tables, row, moments, first, stride, count):
-    result = []
-    for c in range(count):
-        total = None
-        for f in range(CHANNELS):
-            at = f * stride + first + c * 8
-            part = tables[row, 4 + f] * moments[at:at + 8, :]
-            total = part if total is None else total + part
-        result.append(total)
-    return result
-
-
-def update_consensus_kernel(received, gains, moments, duals, rho_a, tables, gains_new, spread, duals_new, target):
+    old = comps(duals)
+    put(moment, [old[c] + rho * new[c] for c in range(8)])
+
+
+def update_consensus_kernel(
+    received, gains, part_0, part_1, part_2, part_3, duals, rho_a, gains_new, spread, duals_new, target
+):
     rho = rho_a[...]
-    chan = lax.axis_index("chan")
     old_gains = comps(gains)
     old_duals = comps(duals)
-    fitted = fit(tables, chan, moments, 0, 64, 8)
+    parts = [comps(part) for part in (part_0, part_1, part_2, part_3)]
+    fitted = [(parts[0][c] + parts[1][c]) + (parts[2][c] + parts[3][c]) for c in range(8)]
     new_duals = [old_duals[c] + rho * (old_gains[c] - fitted[c]) for c in range(8)]
     aim = [0.5 * (rho * fitted[c] - new_duals[c]) for c in range(8)]
     put(duals_new, new_duals)
@@ -437,44 +469,58 @@
                 out[base + c * 8:base + (c + 1) * 8, :] = total
 
 
-def finish_kernel(moments, keep, recv, rho_f, tables, gains, duals, poly, thin, deep):
+def finish_kernel(
+    moments_hbm, keep, recv, rho_f, gains_hbm, duals_hbm, poly_hbm,
+    moments, gains, duals, poly, thin, deep, sems,
+):
+    load = pltpu.make_async_copy(moments_hbm, moments, sems.at[0])
+    load.start()
     chan = lax.axis_index("chan")
     rho = rho_f[...]
     low = lanes() < 64
-
-    def combine(row):
-        parts = [fit(tables, row, moments, half * 32, 64, 4) for half in range(2)]
-        real = [jnp.where(low, a, pltpu.roll(b, 64, 1)) for a, b in zip(*parts)]
-        imag = [jnp.where(low, pltpu.roll(a, 64, 1), b) for a, b in zip(*parts)]
-        return real + imag
 
     def place(ref, value, first, stride):
         for q in range(4):
             part = pltpu.roll(value, 128 - 32 * q, 1) if q else value
             ref[pl.ds(q * 8 * stride + first, 8, stride=stride), :] = part
 
-    for t in range(TERMS):
-        for c, value in enumerate(combine(8 + t)):
-            place(deep, value, c * 4 + t, 32)
-    poly[...] = deep[:, 0:32].reshape(32, 8, 4, 32)
-    fitted = combine(chan)
     now = [keep[c * 8:(c + 1) * 8, :] + recv[c * 8:(c + 1) * 8, :] for c in range(16)]
     for c in range(8):
         place(thin, now[c], c, 8)
     gains[...] = thin[:, 0:32].reshape(32, 8, 32)
+    stores = [pltpu.make_async_copy(gains, gains_hbm, sems.at[1])]
+    stores[0].start()
+    load.wait()
+    at = basis_at(chan)
+    fitted = [None] * 8
+    for t in range(TERMS):
+        halves = []
+        for half in range(2):
+            for c in range(4):
+                total = None
+                for f in range(CHANNELS):
+                    row = f * 64 + half * 32 + c * 8
+                    part = float(SOLVE[t, f]) * moments[row:row + 8, :]
+                    total = part if total is None else total + part
+                halves.append(total)
+        real = [jnp.where(low, halves[c], pltpu.roll(halves[4 + c], 64, 1)) for c in range(4)]
+        imag = [jnp.where(low, pltpu.roll(halves[c], 64, 1), halves[4 + c]) for c in range(4)]
+        for c, value in enumerate(real + imag):
+            place(deep, value, c * 4 + t, 32)
+            fitted[c] = value if t == 0 else fitted[c] + at[t] * value
+    poly[...] = deep[:, 0:32].reshape(32, 8, 4, 32)
+    stores.append(pltpu.make_async_copy(poly, poly_hbm, sems.at[2]))
+    stores[1].start()
     for c in range(8):
         place(thin, now[8 + c] + rho * (now[c] - fitted[c]), c, 8)
     duals[...] = thin[:, 0:32].reshape(32, 8, 32)
+    stores.append(pltpu.make_async_copy(duals, duals_hbm, sems.at[3]))
+    stores[2].start()
+    for store in stores:
+        store.wait()
 
 
 def local(coherency, visibilities, station_pairs, gains, duals, poly, penalty):
-    basis, solve, hat = consensus_tables()
-    constants = np.zeros((12, 12), np.float32)
-    constants[:8, :4] = basis
-    constants[:8, 4:] = hat
-    constants[8:, 4:] = solve
-    tables = jnp.asarray(constants)
-
     def swap(x):
         return lax.ppermute(x, "core", CORE_SWAP)
 
@@ -497,8 +543,8 @@
             pltpu.VMEM((32, 8, ROWS), BF16), state_in, state_in, pltpu.VMEM((32, 8, TERMS, 32), F32),
             pltpu.VMEM((ROWS // 128, 256, 128), F32), thin, pltpu.SemaphoreType.DMA((4,)),
         ],
-        smem=(6, 7), hbm=(0, 1, 2, 3, 4), n_in=8,
-    )(mark, coherency[0], gains[0], duals[0], poly, station_pairs, penalty, tables)
+        hbm=(0, 1, 2, 3, 4), n_in=7,
+    )(mark, coherency[0], gains[0], duals[0], poly, station_pairs, jnp.pad(penalty, (0, 96)).reshape(1, 128))
     received = [swap(x) for x in send]
     vis = visibilities[0]
 
@@ -519,10 +565,11 @@
         model_scratch, n_in=10,
     )(gathered, coh_keep, *received, vis, station_pairs, state_keep, rho_a)
 
-    def step_model(spread):
+    def step_model(spread, *after):
         gathered = exchange(spread, "st")
-        return call(model_kernel, model_outs, model_scratch, n_in=8)(
-            gathered, coh_keep, *received, vis, pairs
+        kernel = model_after_kernel if after else model_kernel
+        return call(kernel, model_outs, model_scratch, hbm=(8,), n_in=8 + len(after))(
+            gathered, coh_keep, *received, vis, pairs, *after
         )
 
     def step_sums(z, w, own):
@@ -530,13 +577,22 @@
         return exchange(parts, "st")
 
     gain, spread = call(update_kernel, [packed, wide], n_in=4)(step_sums(z, w, own), gain, target, rho_a)
-    gain, spread, moment = call(update_moment_kernel, [packed, wide, wide], n_in=5)(
+    gain, spread, moment = call(update_moment_kernel, [packed, wide, packed], n_in=5)(
         step_sums(*step_model(spread)), gain, target, dual, rho_a
     )
-    moments = exchange(moment, "chan")
-    gain, spread, dual, target = call(
-        update_consensus_kernel, [packed, wide, packed, packed], smem=(5,), n_in=6
-    )(step_sums(*step_model(spread)), gain, moments, dual, rho_a, tables)
+
+    def from_channel(x, distance):
+        return lax.ppermute(x, "chan", [(f, f ^ distance) for f in range(CHANNELS)])
+
+    moment_z = from_channel(moment, 4)
+    z, w, own = step_model(spread, moment_z)
+    parts, *messages = call(message_sums_kernel, [sums_out] + [packed] * 4, sums_scratch, n_in=7)(
+        z, w, own, swap(own), pairs, moment, moment_z
+    )
+    shares = [messages[0]] + [from_channel(messages[d], d) for d in (1, 2, 3)]
+    gain, spread, dual, target = call(update_consensus_kernel, [packed, wide, packed, packed], n_in=8)(
+        exchange(parts, "st"), gain, *shares, dual, rho_a
+    )
     keep, send, moment = call(update_last_kernel, [((128, 128), F32), ((128, 128), F32), wide], n_in=5)(
         step_sums(*step_model(spread)), gain, target, dual, rho_a
     )
@@ -544,9 +600,12 @@
     gains_out, duals_out, poly_out = call(
         finish_kernel,
         [((32, 8, 32), F32), ((32, 8, 32), F32), ((32, 8, 4, 32), F32)],
-        [pltpu.VMEM((256, 128), F32), pltpu.VMEM((1024, 128), F32)],
-        smem=(4,), n_in=5,
-    )(moments, keep, swap(send), rho_f, tables)
+        [
+            pltpu.VMEM((512, 128), F32), state_in, state_in, pltpu.VMEM((32, 8, TERMS, 32), F32),
+            thin, pltpu.VMEM((1024, 128), F32), pltpu.SemaphoreType.DMA((4,)),
+        ],
+        hbm=(0,), hbm_out=(0, 1, 2), n_in=4,
+    )(moments, keep, swap(send), rho_f)
     return gains_out[None], duals_out[None], poly_out
 
 

time: 146 us -> 140 us (0.959)
  blocking collectives: 67.6 us -> 50.6 us
  waiting for transfers between devices: 13.3 us -> 21.2 us
  starting transfers between devices: 35.9 us -> 40.7 us
    all_to_all x7 -> x5, blocking collectives: 67.6 us -> 50.6 us  [exchange(): return lax.all_to_all(x, axis, 0, 0, tiled=True)]
    ppermute x0 -> x4, starting transfers between devices: none -> 7.49 us  [from_channel(): return lax.ppermute(x, 'chan', [(f, f ^ distance) for f in range(CHANNELS)])]
    ppermute x0 -> x4, waiting for transfers between devices: none -> 5.85 us  [from_channel(): return lax.ppermute(x, 'chan', [(f, f ^ distance) for f in range(CHANNELS)])]
    ppermute x9, starting transfers between devices: 14.4 us -> 11.9 us  [swap(): return lax.ppermute(x, 'core', CORE_SWAP)]
    all_to_all x3 -> x4, waiting for transfers between devices: 7.43 us -> 9.55 us  [exchange(): return lax.all_to_all(x, axis, 0, 0, tiled=True)]
    pallas_call x5 -> x6, Pallas kernels: 7.39 us -> 9.43 us  [the longest x3 5.86 us: step_model(): call(kernel, model_outs, model_scratch, hbm=(8,), n_in=8 + len(after))]
    pallas_call x4 -> x3, Pallas kernels: 8.04 us -> 6.05 us  [step_sums(): call(sums_kernel, [sums_out], sums_scratch, n_in=5)]
    unnamed x20 -> x16, local copies, waits for them, and re-layouts: 4.24 us -> 2.92 us
  transfers between devices with their start and end apart: 12 -> 17, of which waited for: 10 -> 15; matrix products, arithmetic and copies ran while one was open for 0% -> 0% of each run, Pallas kernels for 4% -> 1%
where the time goes in v3:
time: 140 us; the launch traced here: 139 us
  blocking collectives  50.6 us (36%)
  starting transfers between devices  40.7 us (29%)
  Pallas kernels  22.5 us (16%)
  waiting for transfers between devices  21.2 us (15%)
  local copies, waits for them, and re-layouts  2.92 us (2%)
    all_to_all x5, blocking collectives, exchange(): return lax.all_to_all(x, axis, 0, 0, tiled=True)  50.6 us
    all_to_all x4, starting transfers between devices, exchange(): return lax.all_to_all(x, axis, 0, 0, tiled=True)  21.3 us
    ppermute x9, starting transfers between devices, swap(): return lax.ppermute(x, 'core', CORE_SWAP)  11.9 us
    all_to_all x4, waiting for transfers between devices, exchange(): return lax.all_to_all(x, axis, 0, 0, tiled=True)  9.55 us
    ppermute x4, starting transfers between devices, from_channel(): return lax.ppermute(x, 'chan', [(f, f ^ distance) for f in range(CHANNELS)])  7.49 us
    pallas_call x3, Pallas kernels, step_sums(): call(sums_kernel, [sums_out], sums_scratch, n_in=5)  6.05 us
    pallas_call x3, Pallas kernels, step_model(): call(kernel, model_outs, model_scratch, hbm=(8,), n_in=8 + len(after))  5.86 us
    ppermute x4, waiting for transfers between devices, from_channel(): return lax.ppermute(x, 'chan', [(f, f ^ distance) for f in range(CHANNELS)])  5.85 us
  transfers between devices with their start and end apart: 17, of which 15 were waited for; matrix products, arithmetic and copies ran while one was open for 0% of the time, Pallas kernels for 1%

profile of v3, /device:TPU:1, one launch (start us, length us, event | category | flops | bytes accessed | tf_op | source)
XLA Modules:
  0.0 138.8 jit_solution(405822691463377562)
XLA Ops:
  0.6 0.0 copy-start
  0.6 0.0 copy-start.3
  0.7 1.0 copy-done.3
  1.6 0.8 shard_map.94
  2.4 7.3 %all-to-all-start = ((f32[16,32,128]{2,1,0:T(8,128)}), f32[16,32,128]{2,1,0:T(8,128)S(1)}, u32[]{:S(2)}, u32[]{:S(2)}) async-start(f32[16,32,128]{2,1,0:T(8,128)} %bitcast.1), calls=%async_computation | async-start | bytes 524288 | tf_op jit(solution)/shard_map/all_to_all | solution.py:528
  9.7 0.0 copy-done.7
  9.8 0.0 copy-done
  9.8 0.0 copy-done.4
  9.8 0.0 copy-done.6
  9.8 0.0 copy-start.1
  9.8 1.0 copy-done.1
  10.8 0.9 copy-done.5
  11.7 1.6 %shard_map.95 = (f32[128,1024]{1,0:T(8,128)S(1)}, f32[192,128]{1,0:T(8,128)S(1)}, f32[8,128]{1,0:T(8,128)S(1)}, f32[8,128]{1,0:T(8,128)S(1)}, f32[40,1024]{1,0:T...) custom-call(f32[8,128]{1,0:T(8,128)S(1)} %get-tuple-element.50.mark, ...), custom_call_target="tpu_custom_call" | custom-call | bytes 1000 | tf_op jit(solution)/shard_map/pallas_call | solution.py:539
  13.4 0.2 collective-permute-start
  13.6 0.4 collective-permute-start.1
  14.0 0.1 collective-permute-start.2
  14.1 0.4 collective-permute-start.3
  14.5 0.4 collective-permute-done.recv_0
  14.9 0.2 collective-permute-done.1.recv_1
  15.1 0.3 collective-permute-done.2.recv_2
  15.4 0.2 collective-permute-done.3.recv_3
  15.6 1.5 %all-to-all-done = f32[16,32,128]{2,1,0:T(8,128)S(1)} async-done(((f32[16,32,128]{2,1,0:T(8,128)}), f32[16,32,128]{2,1,0:T(8,128)S(1)}, u32[]{:S(2)}, u32[]{:S(2)}) %all-to-all-start) | async-done | bytes 262176 | tf_op jit(solution)/shard_map/all_to_all | solution.py:528
  17.1 2.1 %shard_map.96 = (f32[128,2048]{1,0:T(8,128)S(1)}, f32[128,2048]{1,0:T(8,128)S(1)}, f32[8,2048]{1,0:T(8,128)S(1)}, s32[2,2048]{1,0:T(2,128)S(1)}, f32[64,128]{1,0...) custom-call(f32[512,128]{1,0:T(8,128)S(1)} %bitcast.34, f32[128,1024]{1,0:T(8,128)S(1)} %get-tuple-element.51.coh_own, ...), custom_call_target="tpu_custom_call" | custom-call | bytes 1000 | tf_op jit(solution)/shard_map/pallas_call | solution.py:562
  19.2 0.5 collective-permute-start.4
  19.7 0.9 collective-permute-done.4.s_other
  20.6 2.1 %shard_map.97 = f32[768,128]{1,0:T(8,128)S(1)} custom-call(f32[128,2048]{1,0:T(8,128)S(1)} %get-tuple-element.58.z_ref, f32[128,2048]{1,0:T(8,128)S(1)} %get-tuple-element.59.w_ref, f32[8,2048]{1,0:T(8,128)S(1)} %get-tuple-element.60.s_own, f32[8,2048]{1,0:T(8,128)S(1)} %collective-permute-done.4.s_other, s32[2,2048]{1,0:T(2,128)S(1)} %get-tuple-element.61.pairs), custom_call_target="tpu_custom_call" | custom-call | bytes 1000 | tf_op jit(solution)/shard_map/pallas_call | solution.py:576
  22.7 11.2 %all_to_all.99 = f32[8,96,128]{2,1,0:T(8,128)S(1)} all-to-all(f32[8,96,128]{2,1,0:T(8,128)S(1)} %bitcast.28), channel_id=1, replica_groups=mesh['chan'=8,'st'=8,'core'=2] {'st'}, dimensions={0} | all-to-all | bytes 786432 | tf_op jit(solution)/shard_map/all_to_all | solution.py:528
  33.8 0.1 shard_map.98
  33.9 8.6 %all_to_all.100 = f32[8,64,128]{2,1,0:T(8,128)S(1)} all-to-all(f32[8,64,128]{2,1,0:T(8,128)S(1)} %bitcast.46), channel_id=1, replica_groups=mesh['chan'=8,'st'=8,'core'=2] {'st'}, dimensions={0} | all-to-all | bytes 524288 | tf_op jit(solution)/shard_map/all_to_all | solution.py:528
  42.5 2.0 %shard_map.99 = (f32[128,2048]{1,0:T(8,128)S(1)}, f32[128,2048]{1,0:T(8,128)S(1)}, f32[8,2048]{1,0:T(8,128)S(1)}) custom-call(f32[512,128]{1,0:T(8,128)S(1)} %bitcast.37, f32[128,1024]{1,0:T(8,128)S(1)} %get-tuple-element.51.coh_own, f32[40,1024]{1,0:T(8,128)S(1)} %collective-permute-done.recv_0, f32[40,1024]{1,0:T(8,128)S(1)} %collective-permute-done.1.recv_1, ...), custom_call_target="tpu_custom_call" | custom-call | bytes 1000 | tf_op jit(solution)/shard_map/pallas_call | solution.py:571
  44.4 2.9 %collective-permute-start.5 = (f32[8,2048]{1,0:T(8,128)S(1)}, f32[8,2048]{1,0:T(8,128)S(1)}, u32[]{:S(2)}, u32[]{:S(2)}) collective-permute-start(f32[8,2048]{1,0:T(8,128)S(1)} %get-tuple-element.67.s_own), channel_id=1, source_target_pairs={{0,1},{1,0},{2,3},{3,2},{4,5},{5,4},{6,7},{7,6},{8,9},{9,8},{10,11... | collective-permute-start | bytes 196616 | tf_op jit(solution)/shard_map/ppermute | solution.py:525
  47.3 0.9 collective-permute-done.5.s_other
  48.2 2.0 %shard_map.100 = f32[768,128]{1,0:T(8,128)S(1)} custom-call(f32[128,2048]{1,0:T(8,128)S(1)} %get-tuple-element.65.z_ref, f32[128,2048]{1,0:T(8,128)S(1)} %get-tuple-element.66.w_ref, f32[8,2048]{1,0:T(8,128)S(1)} %get-tuple-element.67.s_own, f32[8,2048]{1,0:T(8,128)S(1)} %collective-permute-done.5.s_other, s32[2,2048]{1,0:T(2,128)S(1)} %get-tuple-element.61.pairs), custom_call_target="tpu_custom_call" | custom-call | bytes 1000 | tf_op jit(solution)/shard_map/pallas_call | solution.py:576
  50.2 10.2 %all_to_all.101 = f32[8,96,128]{2,1,0:T(8,128)S(1)} all-to-all(f32[8,96,128]{2,1,0:T(8,128)S(1)} %bitcast.30), channel_id=1, replica_groups=mesh['chan'=8,'st'=8,'core'=2] {'st'}, dimensions={0} | all-to-all | bytes 786432 | tf_op jit(solution)/shard_map/all_to_all | solution.py:528
  60.4 0.8 shard_map.101
  61.2 3.4 %all-to-all-start.4 = ((f32[8,64,128]{2,1,0:T(8,128)}), f32[8,64,128]{2,1,0:T(8,128)S(1)}, u32[]{:S(2)}, u32[]{:S(2)}) async-start(f32[8,64,128]{2,1,0:T(8,128)} %bitcast.13), calls=%async_computation.4 | async-start | bytes 524288 | tf_op jit(solution)/shard_map/all_to_all | solution.py:528
  64.6 3.6 %collective-permute-start.6 = (f32[64,128]{1,0:T(8,128)S(1)}, f32[64,128]{1,0:T(8,128)S(1)}, u32[]{:S(2)}, u32[]{:S(2)}) collective-permute-start(f32[64,128]{1,0:T(8,128)S(1)} %get-tuple-element.71.moment), channel_id=1, source_target_pairs={{0,64},{16,80},{32,96},{48,112},{64,0},{80,16},{96,32},{112,48},{1... | collective-permute-start | bytes 98312 | tf_op jit(solution)/shard_map/ppermute | solution.py:585
  68.2 1.6 %collective-permute-done.6.after.moment_z = f32[64,128]{1,0:T(8,128)S(1)} collective-permute-done((f32[64,128]{1,0:T(8,128)S(1)}, f32[64,128]{1,0:T(8,128)S(1)}, u32[]{:S(2)}, u32[]{:S(2)}) %collective-permute-start.6) | collective-permute-done | bytes 32800 | tf_op jit(solution)/shard_map/ppermute | solution.py:585
  69.8 0.6 all-to-all-done.4
  70.4 2.0 %shard_map.102 = (f32[128,2048]{1,0:T(8,128)S(1)}, f32[128,2048]{1,0:T(8,128)S(1)}, f32[8,2048]{1,0:T(8,128)S(1)}) custom-call(f32[512,128]{1,0:T(8,128)S(1)} %bitcast.35, f32[128,1024]{1,0:T(8,128)S(1)} %get-tuple-element.51.coh_own, f32[40,1024]{1,0:T(8,128)S(1)} %collective-permute-done.recv_0, f32[40,1024]{1,0:T(8,128)S(1)} %collective-permute-done.1.recv_1, ...), custom_call_target="tpu_custom_call" | custom-call | bytes 1000 | tf_op jit(solution)/shard_map/pallas_call | solution.py:571
  72.3 3.1 %collective-permute-start.7 = (f32[8,2048]{1,0:T(8,128)S(1)}, f32[8,2048]{1,0:T(8,128)S(1)}, u32[]{:S(2)}, u32[]{:S(2)}) collective-permute-start(f32[8,2048]{1,0:T(8,128)S(1)} %get-tuple-element.74.s_own), channel_id=1, source_target_pairs={{0,1},{1,0},{2,3},{3,2},{4,5},{5,4},{6,7},{7,6},{8,9},{9,8},{10,11... | collective-permute-start | bytes 196616 | tf_op jit(solution)/shard_map/ppermute | solution.py:525
  75.4 0.9 collective-permute-done.7.s_other
  76.3 2.8 %shard_map.103 = (f32[768,128]{1,0:T(8,128)}, f32[64,128]{1,0:T(8,128)S(1)}, f32[64,128]{1,0:T(8,128)S(1)}, f32[64,128]{1,0:T(8,128)S(1)}, f32[64,128]{1,0:T(8,128)S(1)}) custom-call(f32[128,2048]{1,0:T(8,128)S(1)} %get-tuple-element.72.z_ref, f32[128,2048]{1,0:T(8,128)S(1)} %get-tuple-element.73.w_ref, f32[8,2048]{1,0:T(8,128)S(1)} %get-tuple-element.74.s_own, ...), custom_call_target="tpu_custom_call" | custom-call | bytes 1000 | tf_op jit(solution)/shard_map/pallas_call | solution.py:589
  79.1 4.9 %all-to-all-start.5 = ((f32[8,96,128]{2,1,0:T(8,128)}), f32[8,96,128]{2,1,0:T(8,128)S(1)}, u32[]{:S(2)}, u32[]{:S(2)}) async-start(f32[8,96,128]{2,1,0:T(8,128)} %bitcast.15), calls=%async_computation.5 | async-start | bytes 786432 | tf_op jit(solution)/shard_map/all_to_all | solution.py:528
  84.0 1.3 collective-permute-start.8
  85.3 2.6 %collective-permute-start.9 = (f32[64,128]{1,0:T(8,128)S(1)}, f32[64,128]{1,0:T(8,128)S(1)}, u32[]{:S(2)}, u32[]{:S(2)}) collective-permute-start(f32[64,128]{1,0:T(8,128)S(1)} %get-tuple-element.79), channel_id=1, source_target_pairs={{0,32},{16,48},{32,0},{48,16},{64,96},{80,112},{96,64},{112,80},{1... | collective-permute-start | bytes 98312 | tf_op jit(solution)/shard_map/ppermute | solution.py:585
  87.9 0.0 collective-permute-start.10
  87.9 0.0 collective-permute-done.8.part_1
  87.9 1.6 %collective-permute-done.9.part_2 = f32[64,128]{1,0:T(8,128)S(1)} collective-permute-done((f32[64,128]{1,0:T(8,128)S(1)}, f32[64,128]{1,0:T(8,128)S(1)}, u32[]{:S(2)}, u32[]{:S(2)}) %collective-permute-start.9) | collective-permute-done | bytes 32800 | tf_op jit(solution)/shard_map/ppermute | solution.py:585
  89.5 2.6 %collective-permute-done.10.part_3 = f32[64,128]{1,0:T(8,128)S(1)} collective-permute-done((f32[64,128]{1,0:T(8,128)S(1)}, f32[64,128]{1,0:T(8,128)S(1)}, u32[]{:S(2)}, u32[]{:S(2)}) %collective-permute-start.10) | collective-permute-done | bytes 32800 | tf_op jit(solution)/shard_map/ppermute | solution.py:585
  92.2 0.0 all-to-all-done.5
  92.2 0.1 shard_map.104
  92.2 10.4 %all_to_all.102 = f32[8,64,128]{2,1,0:T(8,128)S(1)} all-to-all(f32[8,64,128]{2,1,0:T(8,128)S(1)} %bitcast.45), channel_id=1, replica_groups=mesh['chan'=8,'st'=8,'core'=2] {'st'}, dimensions={0} | all-to-all | bytes 524288 | tf_op jit(solution)/shard_map/all_to_all | solution.py:528
  102.7 2.0 %shard_map.105 = (f32[128,2048]{1,0:T(8,128)S(1)}, f32[128,2048]{1,0:T(8,128)S(1)}, f32[8,2048]{1,0:T(8,128)S(1)}) custom-call(f32[512,128]{1,0:T(8,128)S(1)} %bitcast.36, f32[128,1024]{1,0:T(8,128)S(1)} %get-tuple-element.51.coh_own, f32[40,1024]{1,0:T(8,128)S(1)} %collective-permute-done.recv_0, f32[40,1024]{1,0:T(8,128)S(1)} %collective-permute-done.1.recv_1, ...), custom_call_target="tpu_custom_call" | custom-call | bytes 1000 | tf_op jit(solution)/shard_map/pallas_call | solution.py:571
  104.6 4.1 %collective-permute-start.11 = (f32[8,2048]{1,0:T(8,128)S(1)}, f32[8,2048]{1,0:T(8,128)S(1)}, u32[]{:S(2)}, u32[]{:S(2)}) collective-permute-start(f32[8,2048]{1,0:T(8,128)S(1)} %get-tuple-element.84.s_own), channel_id=1, source_target_pairs={{0,1},{1,0},{2,3},{3,2},{4,5},{5,4},{6,7},{7,6},{8,9},{9,8},{10,11... | collective-permute-start | bytes 196616 | tf_op jit(solution)/shard_map/ppermute | solution.py:525
  108.8 0.9 collective-permute-done.11.s_other
  109.7 2.0 %shard_map.106 = f32[768,128]{1,0:T(8,128)S(1)} custom-call(f32[128,2048]{1,0:T(8,128)S(1)} %get-tuple-element.82.z_ref, f32[128,2048]{1,0:T(8,128)S(1)} %get-tuple-element.83.w_ref, f32[8,2048]{1,0:T(8,128)S(1)} %get-tuple-element.84.s_own, f32[8,2048]{1,0:T(8,128)S(1)} %collective-permute-done.11.s_other, s32[2,2048]{1,0:T(2,128)S(1)} %get-tuple-element.61.pairs), custom_call_target="tpu_custom_call" | custom-call | bytes 1000 | tf_op jit(solution)/shard_map/pallas_call | solution.py:576
  111.6 10.2 %all_to_all.103 = f32[8,96,128]{2,1,0:T(8,128)S(1)} all-to-all(f32[8,96,128]{2,1,0:T(8,128)S(1)} %bitcast.27), channel_id=1, replica_groups=mesh['chan'=8,'st'=8,'core'=2] {'st'}, dimensions={0} | all-to-all | bytes 786432 | tf_op jit(solution)/shard_map/all_to_all | solution.py:528
  121.9 0.8 shard_map.107
  122.7 5.7 %all-to-all-start.8 = ((f32[16,32,128]{2,1,0:T(8,128)}), f32[16,32,128]{2,1,0:T(8,128)S(1)}, u32[]{:S(2)}, u32[]{:S(2)}) async-start(f32[16,32,128]{2,1,0:T(8,128)} %bitcast.21), calls=%async_computation.8 | async-start | bytes 524288 | tf_op jit(solution)/shard_map/all_to_all | solution.py:528
  128.4 0.2 collective-permute-start.12
  128.6 1.1 collective-permute-done.12.recv
  129.6 7.4 %all-to-all-done.8 = f32[16,32,128]{2,1,0:T(8,128)S(1)} async-done(((f32[16,32,128]{2,1,0:T(8,128)}), f32[16,32,128]{2,1,0:T(8,128)S(1)}, u32[]{:S(2)}, u32[]{:S(2)}) %all-to-all-start.8) | async-done | bytes 262176 | tf_op jit(solution)/shard_map/all_to_all | solution.py:528
  137.1 1.6 %shard_map.108 = (f32[32,8,32]{2,1,0:T(8,128)}, f32[32,8,32]{2,1,0:T(8,128)}, f32[32,8,4,32]{3,2,1,0:T(4,128)}) custom-call(f32[512,128]{1,0:T(8,128)S(1)} %bitcast.33, f32[128,128]{1,0:T(8,128)S(1)} %get-tuple-element.89.keep, f32[128,128]{1,0:T(8,128)S(1)} %collective-permute-done.12.recv, f32[8,128]{1,0:T(8,128)S(1)} %get-tuple-element.91.rho_f), custom_call_target="tpu_custom_call" | custom-call | bytes 1000 | tf_op jit(solution)/shard_map/pallas_call | solution.py:600
  (7 shorter events, 0.0 us)
Async XLA Ops:
  0.6 9.1 %copy-start = (bf16[1,32,8,1024]{3,2,1,0:T(8,128)(2,1)S(1)}, bf16[1,32,8,1024]{3,2,1,0:T(8,128)(2,1)}, u32[]{:S(2)}) copy-start(bf16[1,32,8,1024]{3,2,1,0:T(8,128)(2,1)} %param.7) | copy-start | bytes 1572868
  0.6 1.0 copy-start.3
  1.6 8.1 %copy-start.7 = (f32[32]{0:T(128)S(1)}, f32[32]{0:T(128)}, u32[]{:S(2)}) copy-start(f32[32]{0:T(128)} %param.13) | copy-start | bytes 388
  2.4 7.3 %copy-start.4 = (f32[1,32,8,32]{3,2,1,0:T(8,128)S(1)}, f32[1,32,8,32]{3,2,1,0:T(8,128)}, u32[]{:S(2)}) copy-start(f32[1,32,8,32]{3,2,1,0:T(8,128)} %param.10) | copy-start | bytes 98308
  2.4 7.3 %copy-start.6 = (s32[2,1024]{1,0:T(2,128)S(1)}, s32[2,1024]{1,0:T(2,128)}, u32[]{:S(2)}) copy-start(s32[2,1024]{1,0:T(2,128)} %pairs_own.1) | copy-start | bytes 24580
  2.4 14.7 %all-to-all-start = ((f32[16,32,128]{2,1,0:T(8,128)}), f32[16,32,128]{2,1,0:T(8,128)S(1)}, u32[]{:S(2)}, u32[]{:S(2)}) async-start(f32[16,32,128]{2,1,0:T(8,128)} %bitcast.1), calls=%async_computation | async-start | bytes 524288 | tf_op jit(solution)/shard_map/all_to_all | solution.py:528
  9.8 1.0 copy-start.1
  10.8 0.9 copy-start.5
  11.7 5.4 %copy-start.2 = (f32[1,8,1024]{2,1,0:T(8,128)S(1)}, f32[1,8,1024]{2,1,0:T(8,128)}, u32[]{:S(2)}) copy-start(f32[1,8,1024]{2,1,0:T(8,128)} %param.8) | copy-start | bytes 98308
  13.4 1.5 %collective-permute-start = (f32[40,1024]{1,0:T(8,128)S(1)}, f32[40,1024]{1,0:T(8,128)S(1)}, u32[]{:S(2)}, u32[]{:S(2)}) collective-permute-start(f32[40,1024]{1,0:T(8,128)S(1)} %get-tuple-element.52), channel_id=1, source_target_pairs={{0,1},{1,0},{2,3},{3,2},{4,5},{5,4},{6,7},{7,6},{8,9},{9,8},{10,11... | collective-permute-start | bytes 491528 | tf_op jit(solution)/shard_map/ppermute | solution.py:525
  13.6 1.5 %collective-permute-start.1 = (f32[40,1024]{1,0:T(8,128)S(1)}, f32[40,1024]{1,0:T(8,128)S(1)}, u32[]{:S(2)}, u32[]{:S(2)}) collective-permute-start(f32[40,1024]{1,0:T(8,128)S(1)} %get-tuple-element.53), channel_id=1, source_target_pairs={{0,1},{1,0},{2,3},{3,2},{4,5},{5,4},{6,7},{7,6},{8,9},{9,8},{10,11... | collective-permute-start | bytes 491528 | tf_op jit(solution)/shard_map/ppermute | solution.py:525
  14.0 1.4 %collective-permute-start.2 = (f32[40,1024]{1,0:T(8,128)S(1)}, f32[40,1024]{1,0:T(8,128)S(1)}, u32[]{:S(2)}, u32[]{:S(2)}) collective-permute-start(f32[40,1024]{1,0:T(8,128)S(1)} %get-tuple-element.54), channel_id=1, source_target_pairs={{0,1},{1,0},{2,3},{3,2},{4,5},{5,4},{6,7},{7,6},{8,9},{9,8},{10,11... | collective-permute-start | bytes 491528 | tf_op jit(solution)/shard_map/ppermute | solution.py:525
  14.1 1.5 %collective-permute-start.3 = (f32[40,1024]{1,0:T(8,128)S(1)}, f32[40,1024]{1,0:T(8,128)S(1)}, u32[]{:S(2)}, u32[]{:S(2)}) collective-permute-start(f32[40,1024]{1,0:T(8,128)S(1)} %get-tuple-element.55), channel_id=1, source_target_pairs={{0,1},{1,0},{2,3},{3,2},{4,5},{5,4},{6,7},{7,6},{8,9},{9,8},{10,11... | collective-permute-start | bytes 491528 | tf_op jit(solution)/shard_map/ppermute | solution.py:525
  19.2 1.4 collective-permute-start.4
  44.4 3.8 %collective-permute-start.5 = (f32[8,2048]{1,0:T(8,128)S(1)}, f32[8,2048]{1,0:T(8,128)S(1)}, u32[]{:S(2)}, u32[]{:S(2)}) collective-permute-start(f32[8,2048]{1,0:T(8,128)S(1)} %get-tuple-element.67.s_own), channel_id=1, source_target_pairs={{0,1},{1,0},{2,3},{3,2},{4,5},{5,4},{6,7},{7,6},{8,9},{9,8},{10,11... | collective-permute-start | bytes 196616 | tf_op jit(solution)/shard_map/ppermute | solution.py:525
  61.2 9.2 %all-to-all-start.4 = ((f32[8,64,128]{2,1,0:T(8,128)}), f32[8,64,128]{2,1,0:T(8,128)S(1)}, u32[]{:S(2)}, u32[]{:S(2)}) async-start(f32[8,64,128]{2,1,0:T(8,128)} %bitcast.13), calls=%async_computation.4 | async-start | bytes 524288 | tf_op jit(solution)/shard_map/all_to_all | solution.py:528
  64.6 5.2 %collective-permute-start.6 = (f32[64,128]{1,0:T(8,128)S(1)}, f32[64,128]{1,0:T(8,128)S(1)}, u32[]{:S(2)}, u32[]{:S(2)}) collective-permute-start(f32[64,128]{1,0:T(8,128)S(1)} %get-tuple-element.71.moment), channel_id=1, source_target_pairs={{0,64},{16,80},{32,96},{48,112},{64,0},{80,16},{96,32},{112,48},{1... | collective-permute-start | bytes 98312 | tf_op jit(solution)/shard_map/ppermute | solution.py:585
  72.3 4.0 %collective-permute-start.7 = (f32[8,2048]{1,0:T(8,128)S(1)}, f32[8,2048]{1,0:T(8,128)S(1)}, u32[]{:S(2)}, u32[]{:S(2)}) collective-permute-start(f32[8,2048]{1,0:T(8,128)S(1)} %get-tuple-element.74.s_own), channel_id=1, source_target_pairs={{0,1},{1,0},{2,3},{3,2},{4,5},{5,4},{6,7},{7,6},{8,9},{9,8},{10,11... | collective-permute-start | bytes 196616 | tf_op jit(solution)/shard_map/ppermute | solution.py:525
  79.1 13.1 %all-to-all-start.5 = ((f32[8,96,128]{2,1,0:T(8,128)}), f32[8,96,128]{2,1,0:T(8,128)S(1)}, u32[]{:S(2)}, u32[]{:S(2)}) async-start(f32[8,96,128]{2,1,0:T(8,128)} %bitcast.15), calls=%async_computation.5 | async-start | bytes 786432 | tf_op jit(solution)/shard_map/all_to_all | solution.py:528
  84.0 3.9 %collective-permute-start.8 = (f32[64,128]{1,0:T(8,128)S(1)}, f32[64,128]{1,0:T(8,128)S(1)}, u32[]{:S(2)}, u32[]{:S(2)}) collective-permute-start(f32[64,128]{1,0:T(8,128)S(1)} %get-tuple-element.78), channel_id=1, source_target_pairs={{0,16},{16,0},{32,48},{48,32},{64,80},{80,64},{96,112},{112,96},{1... | collective-permute-start | bytes 98312 | tf_op jit(solution)/shard_map/ppermute | solution.py:585
  85.3 4.3 %collective-permute-start.9 = (f32[64,128]{1,0:T(8,128)S(1)}, f32[64,128]{1,0:T(8,128)S(1)}, u32[]{:S(2)}, u32[]{:S(2)}) collective-permute-start(f32[64,128]{1,0:T(8,128)S(1)} %get-tuple-element.79), channel_id=1, source_target_pairs={{0,32},{16,48},{32,0},{48,16},{64,96},{80,112},{96,64},{112,80},{1... | collective-permute-start | bytes 98312 | tf_op jit(solution)/shard_map/ppermute | solution.py:585
  87.9 4.3 %collective-permute-start.10 = (f32[64,128]{1,0:T(8,128)S(1)}, f32[64,128]{1,0:T(8,128)S(1)}, u32[]{:S(2)}, u32[]{:S(2)}) collective-permute-start(f32[64,128]{1,0:T(8,128)S(1)} %get-tuple-element.80), channel_id=1, source_target_pairs={{0,48},{16,32},{32,16},{48,0},{64,112},{80,96},{96,80},{112,64},{1... | collective-permute-start | bytes 98312 | tf_op jit(solution)/shard_map/ppermute | solution.py:585
  104.6 5.0 %collective-permute-start.11 = (f32[8,2048]{1,0:T(8,128)S(1)}, f32[8,2048]{1,0:T(8,128)S(1)}, u32[]{:S(2)}, u32[]{:S(2)}) collective-permute-start(f32[8,2048]{1,0:T(8,128)S(1)} %get-tuple-element.84.s_own), channel_id=1, source_target_pairs={{0,1},{1,0},{2,3},{3,2},{4,5},{5,4},{6,7},{7,6},{8,9},{9,8},{10,11... | collective-permute-start | bytes 196616 | tf_op jit(solution)/shard_map/ppermute | solution.py:525
  122.7 14.4 %all-to-all-start.8 = ((f32[16,32,128]{2,1,0:T(8,128)}), f32[16,32,128]{2,1,0:T(8,128)S(1)}, u32[]{:S(2)}, u32[]{:S(2)}) async-start(f32[16,32,128]{2,1,0:T(8,128)} %bitcast.21), calls=%async_computation.8 | async-start | bytes 524288 | tf_op jit(solution)/shard_map/all_to_all | solution.py:528
  128.4 1.3 collective-permute-start.12

commit v4 on v3

--- a/solution.py
+++ b/solution.py
@@ -220,8 +220,9 @@
             send[c // 2][(c % 2) * 16:(c % 2) * 16 + 16, cols] = wide[t, pl.ds((1 - core) * 128 + c, 16, stride=8), :]
 
 
-def one_hot(pairs, side, j):
-    index = jnp.broadcast_to(pairs[side:side + 1, j * BLOCK:(j + 1) * BLOCK], (16, BLOCK)).astype(jnp.int16)
+def one_hot(pairs, first, side, j):
+    index = pairs[first + side:first + side + 1, j * BLOCK:(j + 1) * BLOCK].astype(jnp.int32)
+    index = jnp.broadcast_to(index, (16, BLOCK)).astype(jnp.int16)
     index = jnp.concatenate([index] * (STATIONS // 16), axis=0)
     here = lax.broadcasted_iota(jnp.int16, (STATIONS, BLOCK), 0) == index
     return jnp.where(here, jnp.ones((STATIONS, BLOCK), BF16), jnp.zeros((STATIONS, BLOCK), BF16))
@@ -262,13 +263,29 @@
             put_table(table, c, t, first, second)
 
 
-def first_model_kernel(
-    gathered, coh_own, recv_0, recv_1, recv_2, recv_3, vis, pairs_own, state_keep, rho_a,
-    z_ref, w_ref, s_ref, pairs, gains, duals, target, table, near, far,
+def first_own_kernel(gathered, coh, vis, pairs, z_ref, w_ref, s_ref, table, near, far):
+    start_table(gathered, table)
+    model(lambda i: (coh, i * 16), vis, pairs, 0, z_ref, w_ref, s_ref, table, near, far)
+
+
+def own_kernel(gathered, coh, vis, pairs, z_ref, w_ref, s_ref, table, near, far):
+    step_table(gathered, table)
+    model(lambda i: (coh, i * 16), vis, pairs, 0, z_ref, w_ref, s_ref, table, near, far)
+
+
+def own_after_kernel(gathered, coh, vis, pairs, after, *rest):
+    own_kernel(gathered, coh, vis, pairs, *rest)
+
+
+def other_kernel(table, recv_0, recv_1, recv_2, recv_3, z_ref, w_ref, s_ref, near, far):
+    received = (recv_0, recv_1, recv_2, recv_3)
+    model(lambda i: (received[i // 2], (i % 2) * 16), None, recv_3, 32, z_ref, w_ref, s_ref, table, near, far)
+
+
+def first_other_kernel(
+    table, recv_0, recv_1, recv_2, recv_3, state_keep, rho_a, z_ref, w_ref, s_ref, gains, duals, target, near, far
 ):
     received = (recv_0, recv_1, recv_2, recv_3)
-    pairs[0:2, 0:ROWS] = pairs_own[...]
-    pairs[0:2, ROWS:] = recv_3[32:34, :].astype(jnp.int32)
     half_rho = 0.5 * rho_a[...]
     for c in range(8):
         at = c * 8
@@ -280,52 +297,38 @@
         gains[at:at + 8, :] = state[0]
         duals[at:at + 8, :] = state[1]
         target[at:at + 8, :] = half_rho * state[2] - 0.5 * state[1]
-    start_table(gathered, table)
-    model(coh_own, received, vis, pairs, z_ref, w_ref, s_ref, table, near, far)
-
-
-def model_kernel(
-    gathered, coh_own, recv_0, recv_1, recv_2, recv_3, vis, pairs, z_ref, w_ref, s_ref, table, near, far
-):
-    received = (recv_0, recv_1, recv_2, recv_3)
-    step_table(gathered, table)
-    model(coh_own, received, vis, pairs, z_ref, w_ref, s_ref, table, near, far)
-
-
-def model_after_kernel(gathered, coh_own, recv_0, recv_1, recv_2, recv_3, vis, pairs, after, *rest):
-    model_kernel(gathered, coh_own, recv_0, recv_1, recv_2, recv_3, vis, pairs, *rest)
-
-
-def model(coh_own, received, vis, pairs, z_ref, w_ref, s_ref, table, near, far):
-    for j in range(2 * ROWS // BLOCK):
-        own = j < ROWS // BLOCK
-        col = (j * BLOCK) % ROWS
+    other_kernel(table, *received, z_ref, w_ref, s_ref, near, far)
+
+
+def model(coh_at, vis, pairs, first, z_ref, w_ref, s_ref, table, near, far):
+    for j in range(ROWS // BLOCK):
         for side, dest in ((0, near), (1, far)):
-            both = jnp.dot(table[...], one_hot(pairs, side, j), preferred_element_type=F32)
+            both = jnp.dot(table[...], one_hot(pairs, first, side, j), preferred_element_type=F32)
             dest[j % 2] = both[:128] + both[128:]
         for l in range(BLOCK // 128):
-            src = col + l * 128
-            dst = j * BLOCK + l * 128
+            at = j * BLOCK + l * 128
+
+            def coherency(i):
+                ref, row = coh_at(i)
+                return ref[row:row + 16, at:at + 128]
+
             gp = matrix(lambda i: near[j % 2, i * 16:(i + 1) * 16, l * 128:(l + 1) * 128])
             gq = matrix(lambda i: far[j % 2, i * 16:(i + 1) * 16, l * 128:(l + 1) * 128])
-            if own:
-                cc = matrix(lambda i: coh_own[i * 16:(i + 1) * 16, src:src + 128])
-            else:
-                cc = matrix(lambda i: received[i // 2][(i % 2) * 16:(i % 2) * 16 + 16, src:src + 128])
+            cc = matrix(coherency)
             z = product_nh(cc, gq)
             w = product(gp, cc)
             m = product(gp, z)
             for i in range(8):
-                z_ref[i * 16:(i + 1) * 16, dst:dst + 128] = z[i // 4][i % 4]
-                w_ref[i * 16:(i + 1) * 16, dst:dst + 128] = w[i // 4][i % 4]
+                z_ref[i * 16:(i + 1) * 16, at:at + 128] = z[i // 4][i % 4]
+                w_ref[i * 16:(i + 1) * 16, at:at + 128] = w[i // 4][i % 4]
                 total = -jnp.sum(m[i // 4][i % 4], axis=0, keepdims=True)
-                if own:
-                    total = total + vis[i:i + 1, src:src + 128]
-                s_ref[i:i + 1, dst:dst + 128] = total
+                if vis is not None:
+                    total = total + vis[i:i + 1, at:at + 128]
+                s_ref[i:i + 1, at:at + 128] = total
 
 
 def message_sums_kernel(
-    z_ref, w_ref, s_own, s_other, pairs, moment, moment_z, out, part_0, part_1, part_2, part_3, left, acc, hot
+    z_ref, w_ref, s_here, s_there, pairs, before, moment, moment_z, out, part_0, part_1, part_2, part_3, left, acc, hot
 ):
     chan = lax.axis_index("chan")
     near = weigh(basis_at(chan))
@@ -337,16 +340,15 @@
         near_weight = dot_terms(at, near)
         far_weight = dot_terms(at, far)
         put(part, [near_weight * own[c] + far_weight * other[c] for c in range(8)])
-    sums_kernel(z_ref, w_ref, s_own, s_other, pairs, out, left, acc, hot)
-
-
-def sums_kernel(z_ref, w_ref, s_own, s_other, pairs, out, left, acc, hot):
-    steps = 2 * ROWS // BLOCK
+    sums_own_kernel(z_ref, w_ref, s_here, s_there, pairs, before, out, left, acc, hot)
+
+
+def half_sums(z_ref, w_ref, s_here, s_there, pairs, first, before, left, acc, hot):
+    steps = ROWS // BLOCK
     for j in range(steps):
         for l in range(BLOCK // 128):
             src = j * BLOCK + l * 128
-            swapped = (src + ROWS) % (2 * ROWS)
-            r = matrix(lambda i: s_own[i:i + 1, src:src + 128] + s_other[i:i + 1, swapped:swapped + 128])
+            r = matrix(lambda i: s_here[i:i + 1, src:src + 128] + s_there[i:i + 1, src:src + 128])
             z = matrix(lambda i: z_ref[i * 16:(i + 1) * 16, src:src + 128])
             w = matrix(lambda i: w_ref[i * 16:(i + 1) * 16, src:src + 128])
             for side, (num, den) in enumerate(
@@ -358,12 +360,20 @@
                     left[j, i * 16:(i + 1) * 16, at:at + 128] = high
                     left[j, 192 + i * 16:192 + (i + 1) * 16, at:at + 128] = rest
         for side in range(2):
-            hot[j, :, side * BLOCK:(side + 1) * BLOCK] = one_hot(pairs, side, j)
+            hot[j, :, side * BLOCK:(side + 1) * BLOCK] = one_hot(pairs, first, side, j)
         total = lax.dot_general(left[j], hot[j], (((1,), (1,)), ((), ())), preferred_element_type=F32)
         if j == 0:
-            acc[...] = total
+            acc[...] = total if before is None else before[...] + total
         else:
             acc[...] += total
+
+
+def sums_other_kernel(z_ref, w_ref, s_here, s_there, recv_3, acc, left, hot):
+    half_sums(z_ref, w_ref, s_here, s_there, recv_3, 32, None, left, acc, hot)
+
+
+def sums_own_kernel(z_ref, w_ref, s_here, s_there, pairs, before, out, left, acc, hot):
+    half_sums(z_ref, w_ref, s_here, s_there, pairs, 0, before, left, acc, hot)
     low = lanes() < 64
     for c in range(12):
         for t in range(4):
@@ -548,53 +558,61 @@
     received = [swap(x) for x in send]
     vis = visibilities[0]
 
-    model_outs = [((128, 2 * ROWS), F32), ((128, 2 * ROWS), F32), ((8, 2 * ROWS), F32)]
-    model_scratch = [
-        pltpu.VMEM((256, STATIONS), BF16), pltpu.VMEM((2, 128, BLOCK), F32), pltpu.VMEM((2, 128, BLOCK), F32)
-    ]
+    half_outs = [((128, ROWS), F32), ((128, ROWS), F32), ((8, ROWS), F32)]
+    table_out = ((256, STATIONS), BF16)
+    pair_scratch = [pltpu.VMEM((2, 128, BLOCK), F32)] * 2
     sums_out = ((768, 128), F32)
-    blocks = 2 * ROWS // BLOCK
-    sums_scratch = [
-        pltpu.VMEM((blocks, 384, 2 * BLOCK), BF16),
-        pltpu.VMEM((384, STATIONS), F32),
-        pltpu.VMEM((blocks, STATIONS, 2 * BLOCK), BF16),
-    ]
-    z, w, own, pairs, gain, dual, target = call(
-        first_model_kernel,
-        model_outs + [((2, 2 * ROWS), jnp.int32), packed, packed, packed],
-        model_scratch, n_in=10,
-    )(gathered, coh_keep, *received, vis, station_pairs, state_keep, rho_a)
+    blocks = ROWS // BLOCK
+    left = pltpu.VMEM((blocks, 384, 2 * BLOCK), BF16)
+    hot = pltpu.VMEM((blocks, STATIONS, 2 * BLOCK), BF16)
+    total = pltpu.VMEM((384, STATIONS), F32)
+
+    *own, table = call(first_own_kernel, half_outs + [table_out], pair_scratch, n_in=4)(
+        gathered, coh_keep, vis, station_pairs
+    )
+    *other, gain, dual, target = call(
+        first_other_kernel, half_outs + [packed, packed, packed], pair_scratch, n_in=7
+    )(table, *received, state_keep, rho_a)
 
     def step_model(spread, *after):
-        gathered = exchange(spread, "st")
-        kernel = model_after_kernel if after else model_kernel
-        return call(kernel, model_outs, model_scratch, hbm=(8,), n_in=8 + len(after))(
-            gathered, coh_keep, *received, vis, pairs, *after
+        kernel = own_after_kernel if after else own_kernel
+        *own, table = call(kernel, half_outs + [table_out], pair_scratch, hbm=(4,), n_in=4 + len(after))(
+            exchange(spread, "st"), coh_keep, vis, station_pairs, *after
         )
-
-    def step_sums(z, w, own):
-        (parts,) = call(sums_kernel, [sums_out], sums_scratch, n_in=5)(z, w, own, swap(own), pairs)
-        return exchange(parts, "st")
-
-    gain, spread = call(update_kernel, [packed, wide], n_in=4)(step_sums(z, w, own), gain, target, rho_a)
+        other = call(other_kernel, half_outs, pair_scratch, n_in=5)(table, *received)
+        return own, other
+
+    def step_sums(own, other, kernel=sums_own_kernel, outs=(), extra=()):
+        from_own = swap(own[2])
+        from_other = swap(other[2])
+        (before,) = call(sums_other_kernel, [((384, STATIONS), F32)], [left, hot], n_in=5)(
+            *other, from_own, received[3]
+        )
+        return call(kernel, [sums_out, *outs], [left, total, hot], n_in=6 + len(extra))(
+            *own, from_other, station_pairs, before, *extra
+        )
+
+    def step(own, other):
+        return exchange(step_sums(own, other)[0], "st")
+
+    gain, spread = call(update_kernel, [packed, wide], n_in=4)(step(own, other), gain, target, rho_a)
     gain, spread, moment = call(update_moment_kernel, [packed, wide, packed], n_in=5)(
-        step_sums(*step_model(spread)), gain, target, dual, rho_a
+        step(*step_model(spread)), gain, target, dual, rho_a
     )
 
     def from_channel(x, distance):
         return lax.ppermute(x, "chan", [(f, f ^ distance) for f in range(CHANNELS)])
 
     moment_z = from_channel(moment, 4)
-    z, w, own = step_model(spread, moment_z)
-    parts, *messages = call(message_sums_kernel, [sums_out] + [packed] * 4, sums_scratch, n_in=7)(
-        z, w, own, swap(own), pairs, moment, moment_z
+    parts, *messages = step_sums(
+        *step_model(spread, moment_z), message_sums_kernel, [packed] * 4, (moment, moment_z)
     )
     shares = [messages[0]] + [from_channel(messages[d], d) for d in (1, 2, 3)]
     gain, spread, dual, target = call(update_consensus_kernel, [packed, wide, packed, packed], n_in=8)(
         exchange(parts, "st"), gain, *shares, dual, rho_a
     )
-    keep, send, moment = call(update_last_kernel, [((128, 128), F32), ((128, 128), F32), wide], n_in=5)(
-        step_sums(*step_model(spread)), gain, target, dual, rho_a
+    keep, send, moment = call(update_last_kernel, [((128, 128), F32), ((1024, 128), F32), wide], n_in=5)(
+        step(*step_model(spread)), gain, target, dual, rho_a
     )
     moments = exchange(moment, ("chan", "core"))
     gains_out, duals_out, poly_out = call(

time: 140 us -> 137 us (0.979)
  waiting for transfers between devices: 21.2 us -> 9.72 us
  blocking collectives: 50.6 us -> 61.6 us
  starting transfers between devices: 40.7 us -> 37.7 us
    all_to_all x5 -> x6, blocking collectives: 50.6 us -> 61.6 us  [exchange(): return lax.all_to_all(x, axis, 0, 0, tiled=True)]
    all_to_all x4 -> x3, waiting for transfers between devices: 9.55 us -> 3.25 us  [exchange(): return lax.all_to_all(x, axis, 0, 0, tiled=True)]
    all_to_all x4 -> x3, starting transfers between devices: 21.3 us -> 15.6 us  [exchange(): return lax.all_to_all(x, axis, 0, 0, tiled=True)]
    ppermute x9 -> x13, waiting for transfers between devices: 5.8 us -> 0.43 us  [swap(): return lax.ppermute(x, 'core', CORE_SWAP)]
    ppermute x9 -> x13, starting transfers between devices: 11.9 us -> 14.8 us  [swap(): return lax.ppermute(x, 'core', CORE_SWAP)]
    pallas_call x9 -> x17, Pallas kernels: 17.6 us -> 18.3 us  [the longest x4 5.53 us: step_sums(): call(kernel, [sums_out, *outs], [left, total, hot], n_in=6 + len(extra))]
  transfers between devices with their start and end apart: 17 -> 20, of which waited for: 15 -> 8; matrix products, arithmetic and copies ran while one was open for 0% -> 0% of each run, Pallas kernels for 1% -> 8%
where the time goes in v4:
time: 137 us; the launch traced here: 136 us
  blocking collectives  61.6 us (45%)
  starting transfers between devices  37.7 us (28%)
  Pallas kernels  23.2 us (17%)
  waiting for transfers between devices  9.72 us (7%)
  local copies, waits for them, and re-layouts  2.92 us (2%)
    all_to_all x6, blocking collectives, exchange(): return lax.all_to_all(x, axis, 0, 0, tiled=True)  61.6 us
    all_to_all x3, starting transfers between devices, exchange(): return lax.all_to_all(x, axis, 0, 0, tiled=True)  15.6 us
    ppermute x13, starting transfers between devices, swap(): return lax.ppermute(x, 'core', CORE_SWAP)  14.8 us
    ppermute x4, starting transfers between devices, from_channel(): return lax.ppermute(x, 'chan', [(f, f ^ distance) for f in range(CHANNELS)])  7.3 us
    ppermute x4, waiting for transfers between devices, from_channel(): return lax.ppermute(x, 'chan', [(f, f ^ distance) for f in range(CHANNELS)])  6.03 us
    pallas_call x4, Pallas kernels, step_sums(): call(kernel, [sums_out, *outs], [left, total, hot], n_in=6 + len(extra))  5.53 us
    pallas_call x4, Pallas kernels, step_sums(): call(sums_other_kernel, [((384, STATIONS), F32)], [left, hot], n_in=5)  4.2 us
    all_to_all x3, waiting for transfers between devices, exchange(): return lax.all_to_all(x, axis, 0, 0, tiled=True)  3.25 us
  transfers between devices with their start and end apart: 20, of which 8 were waited for; matrix products, arithmetic and copies ran while one was open for 0% of the time, Pallas kernels for 8%

profile of v4, /device:TPU:1, one launch (start us, length us, event | category | flops | bytes accessed | tf_op | source)
XLA Modules:
  0.0 136.3 jit_solution(4841761329477821310)
XLA Ops:
  0.6 0.0 copy-start.3
  0.7 1.0 copy-done.3
  1.6 0.8 shard_map.94
  2.4 7.3 %all-to-all-start = ((f32[16,32,128]{2,1,0:T(8,128)}), f32[16,32,128]{2,1,0:T(8,128)S(1)}, u32[]{:S(2)}, u32[]{:S(2)}) async-start(f32[16,32,128]{2,1,0:T(8,128)} %bitcast.1), calls=%async_computation | async-start | bytes 524288 | tf_op jit(solution)/shard_map/all_to_all | solution.py:538
  9.8 0.0 copy-start.2
  9.8 1.0 copy-done.2
  10.8 0.9 copy-done.6
  11.7 1.6 %shard_map.95 = (f32[128,1024]{1,0:T(8,128)S(1)}, f32[192,128]{1,0:T(8,128)S(1)}, f32[8,128]{1,0:T(8,128)S(1)}, f32[8,128]{1,0:T(8,128)S(1)}, f32[40,1024]{1,0:T...) custom-call(f32[8,128]{1,0:T(8,128)S(1)} %get-tuple-element.65.mark, ...), custom_call_target="tpu_custom_call" | custom-call | bytes 1000 | tf_op jit(solution)/shard_map/pallas_call | solution.py:549
  13.4 0.2 collective-permute-start
  13.6 0.4 collective-permute-start.1
  14.0 0.1 collective-permute-start.2
  14.1 0.4 collective-permute-start.3
  14.5 2.6 %all-to-all-done = f32[16,32,128]{2,1,0:T(8,128)S(1)} async-done(((f32[16,32,128]{2,1,0:T(8,128)}), f32[16,32,128]{2,1,0:T(8,128)S(1)}, u32[]{:S(2)}, u32[]{:S(2)}) %all-to-all-start) | async-done | bytes 262176 | tf_op jit(solution)/shard_map/all_to_all | solution.py:538
  17.1 1.2 shard_map.96
  18.3 0.5 collective-permute-start.5
  18.8 0.0 collective-permute-done.3.recv_3
  18.8 1.0 shard_map.97
  19.8 0.2 collective-permute-start.4
  20.0 1.1 shard_map.98.before
  21.1 0.0 collective-permute-done.4.s_there
  21.1 1.2 shard_map.99
  22.3 10.2 %all_to_all.99 = f32[8,96,128]{2,1,0:T(8,128)S(1)} all-to-all(f32[8,96,128]{2,1,0:T(8,128)S(1)} %bitcast.27), channel_id=1, replica_groups=mesh['chan'=8,'st'=8,'core'=2] {'st'}, dimensions={0} | all-to-all | bytes 786432 | tf_op jit(solution)/shard_map/all_to_all | solution.py:538
  32.5 0.1 shard_map.100
  32.6 8.5 %all_to_all.100 = f32[8,64,128]{2,1,0:T(8,128)S(1)} all-to-all(f32[8,64,128]{2,1,0:T(8,128)S(1)} %bitcast.47), channel_id=1, replica_groups=mesh['chan'=8,'st'=8,'core'=2] {'st'}, dimensions={0} | all-to-all | bytes 524288 | tf_op jit(solution)/shard_map/all_to_all | solution.py:538
  41.1 1.1 shard_map.101
  42.2 2.8 %collective-permute-start.7 = (f32[8,1024]{1,0:T(8,128)S(1)}, f32[8,1024]{1,0:T(8,128)S(1)}, u32[]{:S(2)}, u32[]{:S(2)}) collective-permute-start(f32[8,1024]{1,0:T(8,128)S(1)} %get-tuple-element.85.s_here), channel_id=1, source_target_pairs={{0,1},{1,0},{2,3},{3,2},{4,5},{5,4},{6,7},{7,6},{8,9},{9,8},{10,11... | collective-permute-start | bytes 98312 | tf_op jit(solution)/shard_map/ppermute | solution.py:535
  45.0 1.0 shard_map.102
  46.0 0.3 collective-permute-start.6
  46.3 0.0 collective-permute-done.7.s_there
  46.3 1.0 shard_map.103.before
  47.4 0.1 collective-permute-done.6.s_there
  47.5 1.2 shard_map.104
  48.7 10.2 %all_to_all.101 = f32[8,96,128]{2,1,0:T(8,128)S(1)} all-to-all(f32[8,96,128]{2,1,0:T(8,128)S(1)} %bitcast.28), channel_id=1, replica_groups=mesh['chan'=8,'st'=8,'core'=2] {'st'}, dimensions={0} | all-to-all | bytes 786432 | tf_op jit(solution)/shard_map/all_to_all | solution.py:538
  58.9 0.8 shard_map.105
  59.7 3.4 %all-to-all-start.4 = ((f32[8,64,128]{2,1,0:T(8,128)}), f32[8,64,128]{2,1,0:T(8,128)S(1)}, u32[]{:S(2)}, u32[]{:S(2)}) async-start(f32[8,64,128]{2,1,0:T(8,128)} %bitcast.13), calls=%async_computation.4 | async-start | bytes 524288 | tf_op jit(solution)/shard_map/all_to_all | solution.py:538
  63.1 3.4 %collective-permute-start.8 = (f32[64,128]{1,0:T(8,128)S(1)}, f32[64,128]{1,0:T(8,128)S(1)}, u32[]{:S(2)}, u32[]{:S(2)}) collective-permute-start(f32[64,128]{1,0:T(8,128)S(1)} %get-tuple-element.93.moment), channel_id=1, source_target_pairs={{0,64},{16,80},{32,96},{48,112},{64,0},{80,16},{96,32},{112,48},{1... | collective-permute-start | bytes 98312 | tf_op jit(solution)/shard_map/ppermute | solution.py:604
  66.5 1.8 %collective-permute-done.8.after.moment_z = f32[64,128]{1,0:T(8,128)S(1)} collective-permute-done((f32[64,128]{1,0:T(8,128)S(1)}, f32[64,128]{1,0:T(8,128)S(1)}, u32[]{:S(2)}, u32[]{:S(2)}) %collective-permute-start.8) | collective-permute-done | bytes 32800 | tf_op jit(solution)/shard_map/ppermute | solution.py:604
  68.2 0.6 all-to-all-done.4
  68.8 1.1 shard_map.106
  69.9 3.1 %collective-permute-start.10 = (f32[8,1024]{1,0:T(8,128)S(1)}, f32[8,1024]{1,0:T(8,128)S(1)}, u32[]{:S(2)}, u32[]{:S(2)}) collective-permute-start(f32[8,1024]{1,0:T(8,128)S(1)} %get-tuple-element.96.s_here), channel_id=1, source_target_pairs={{0,1},{1,0},{2,3},{3,2},{4,5},{5,4},{6,7},{7,6},{8,9},{9,8},{10,11... | collective-permute-start | bytes 98312 | tf_op jit(solution)/shard_map/ppermute | solution.py:535
  73.0 1.0 shard_map.107
  74.0 0.1 collective-permute-start.9
  74.1 1.0 shard_map.108.before
  75.2 0.1 collective-permute-done.9.s_there
  75.3 2.0 %shard_map.109 = (f32[768,128]{1,0:T(8,128)}, f32[64,128]{1,0:T(8,128)S(1)}, f32[64,128]{1,0:T(8,128)S(1)}, f32[64,128]{1,0:T(8,128)S(1)}, f32[64,128]{1,0:T(8,128)S(1)}) custom-call(f32[128,1024]{1,0:T(8,128)S(1)} %get-tuple-element.94.z_ref, f32[128,1024]{1,0:T(8,128)S(1)} %get-tuple-element.95.w_ref, f32[8,1024]{1,0:T(8,128)S(1)} %get-tuple-element.96.s_here, ...), custom_call_target="tpu_custom_call" | custom-call | bytes 1000 | tf_op jit(solution)/shard_map/pallas_call | solution.py:591
  77.3 4.9 %all-to-all-start.5 = ((f32[8,96,128]{2,1,0:T(8,128)}), f32[8,96,128]{2,1,0:T(8,128)S(1)}, u32[]{:S(2)}, u32[]{:S(2)}) async-start(f32[8,96,128]{2,1,0:T(8,128)} %bitcast.15), calls=%async_computation.5 | async-start | bytes 786432 | tf_op jit(solution)/shard_map/all_to_all | solution.py:538
  82.2 1.3 collective-permute-start.11
  83.5 2.6 %collective-permute-start.12 = (f32[64,128]{1,0:T(8,128)S(1)}, f32[64,128]{1,0:T(8,128)S(1)}, u32[]{:S(2)}, u32[]{:S(2)}) collective-permute-start(f32[64,128]{1,0:T(8,128)S(1)} %get-tuple-element.105), channel_id=1, source_target_pairs={{0,32},{16,48},{32,0},{48,16},{64,96},{80,112},{96,64},{112,80},{1... | collective-permute-start | bytes 98312 | tf_op jit(solution)/shard_map/ppermute | solution.py:604
  86.1 1.6 %collective-permute-done.12.part_2 = f32[64,128]{1,0:T(8,128)S(1)} collective-permute-done((f32[64,128]{1,0:T(8,128)S(1)}, f32[64,128]{1,0:T(8,128)S(1)}, u32[]{:S(2)}, u32[]{:S(2)}) %collective-permute-start.12) | collective-permute-done | bytes 32800 | tf_op jit(solution)/shard_map/ppermute | solution.py:604
  87.7 2.6 %collective-permute-done.13.part_3 = f32[64,128]{1,0:T(8,128)S(1)} collective-permute-done((f32[64,128]{1,0:T(8,128)S(1)}, f32[64,128]{1,0:T(8,128)S(1)}, u32[]{:S(2)}, u32[]{:S(2)}) %collective-permute-start.13) | collective-permute-done | bytes 32800 | tf_op jit(solution)/shard_map/ppermute | solution.py:604
  90.4 0.1 shard_map.110
  90.4 10.4 %all_to_all.102 = f32[8,64,128]{2,1,0:T(8,128)S(1)} all-to-all(f32[8,64,128]{2,1,0:T(8,128)S(1)} %bitcast.46), channel_id=1, replica_groups=mesh['chan'=8,'st'=8,'core'=2] {'st'}, dimensions={0} | all-to-all | bytes 524288 | tf_op jit(solution)/shard_map/all_to_all | solution.py:538
  100.9 1.1 shard_map.111
  101.9 4.2 %collective-permute-start.15 = (f32[8,1024]{1,0:T(8,128)S(1)}, f32[8,1024]{1,0:T(8,128)S(1)}, u32[]{:S(2)}, u32[]{:S(2)}) collective-permute-start(f32[8,1024]{1,0:T(8,128)S(1)} %get-tuple-element.110.s_here), channel_id=1, source_target_pairs={{0,1},{1,0},{2,3},{3,2},{4,5},{5,4},{6,7},{7,6},{8,9},{9,8},{10,11... | collective-permute-start | bytes 98312 | tf_op jit(solution)/shard_map/ppermute | solution.py:535
  106.1 1.0 shard_map.112
  107.1 0.3 collective-permute-start.14
  107.4 1.0 shard_map.113.before
  108.5 0.1 collective-permute-done.14.s_there
  108.6 1.2 shard_map.114
  109.8 9.9 %all_to_all.103 = f32[8,96,128]{2,1,0:T(8,128)S(1)} all-to-all(f32[8,96,128]{2,1,0:T(8,128)S(1)} %bitcast.29), channel_id=1, replica_groups=mesh['chan'=8,'st'=8,'core'=2] {'st'}, dimensions={0} | all-to-all | bytes 786432 | tf_op jit(solution)/shard_map/all_to_all | solution.py:538
  119.7 0.2 shard_map.115
  119.9 2.3 %collective-permute-start.16 = (f32[1024,128]{1,0:T(8,128)S(1)}, f32[1024,128]{1,0:T(8,128)S(1)}, u32[]{:S(2)}, u32[]{:S(2)}) collective-permute-start(f32[1024,128]{1,0:T(8,128)S(1)} %get-tuple-element.120), channel_id=1, source_target_pairs={{0,1},{1,0},{2,3},{3,2},{4,5},{5,4},{6,7},{7,6},{8,9},{9,8},{10,11... | collective-permute-start | bytes 1572872 | tf_op jit(solution)/shard_map/ppermute | solution.py:535
  122.1 12.4 %all_to_all.104 = f32[16,32,128]{2,1,0:T(8,128)S(1)} all-to-all(f32[16,32,128]{2,1,0:T(8,128)S(1)} %bitcast.45), channel_id=1, replica_groups=mesh['chan'=8,'st'=8,'core'=2] {'chan','core'}, dimensions={0} | all-to-all | bytes 524288 | tf_op jit(solution)/shard_map/all_to_all | solution.py:538
  134.6 1.6 %shard_map.116 = (f32[32,8,32]{2,1,0:T(8,128)}, f32[32,8,32]{2,1,0:T(8,128)}, f32[32,8,4,32]{3,2,1,0:T(4,128)}) custom-call(f32[512,128]{1,0:T(8,128)S(1)} %bitcast.37, f32[128,128]{1,0:T(8,128)S(1)} %get-tuple-element.119.keep, f32[1024,128]{1,0:T(8,128)S(1)} %collective-permute-done.16.recv, f32[8,128]{1,0:T(8,128)S(1)} %get-tuple-element.121.rho_f), custom_call_target="tpu_custom_call" | custom-call | bytes 1000 | tf_op jit(solution)/shard_map/pallas_call | solution.py:618
  (22 shorter events, 0.1 us)
Async XLA Ops:
  0.6 9.1 %copy-start.1 = (bf16[1,32,8,1024]{3,2,1,0:T(8,128)(2,1)S(1)}, bf16[1,32,8,1024]{3,2,1,0:T(8,128)(2,1)}, u32[]{:S(2)}) copy-start(bf16[1,32,8,1024]{3,2,1,0:T(8,128)(2,1)} %param.7) | copy-start | bytes 1572868
  0.6 1.0 copy-start.3
  1.6 8.1 %copy-start.7 = (f32[32]{0:T(128)S(1)}, f32[32]{0:T(128)}, u32[]{:S(2)}) copy-start(f32[32]{0:T(128)} %param.13) | copy-start | bytes 388
  2.4 7.3 %copy-start = (s32[2,1024]{1,0:T(2,128)S(1)}, s32[2,1024]{1,0:T(2,128)}, u32[]{:S(2)}) copy-start(s32[2,1024]{1,0:T(2,128)} %pairs.17) | copy-start | bytes 24580
  2.4 7.3 %copy-start.4 = (f32[1,32,8,32]{3,2,1,0:T(8,128)S(1)}, f32[1,32,8,32]{3,2,1,0:T(8,128)}, u32[]{:S(2)}) copy-start(f32[1,32,8,32]{3,2,1,0:T(8,128)} %param.10) | copy-start | bytes 98308
  2.4 14.7 %all-to-all-start = ((f32[16,32,128]{2,1,0:T(8,128)}), f32[16,32,128]{2,1,0:T(8,128)S(1)}, u32[]{:S(2)}, u32[]{:S(2)}) async-start(f32[16,32,128]{2,1,0:T(8,128)} %bitcast.1), calls=%async_computation | async-start | bytes 524288 | tf_op jit(solution)/shard_map/all_to_all | solution.py:538
  9.8 1.0 copy-start.2
  10.8 0.9 copy-start.6
  11.7 5.4 %copy-start.5 = (f32[1,8,1024]{2,1,0:T(8,128)S(1)}, f32[1,8,1024]{2,1,0:T(8,128)}, u32[]{:S(2)}) copy-start(f32[1,8,1024]{2,1,0:T(8,128)} %param.8) | copy-start | bytes 98308
  13.4 5.4 %collective-permute-start = (f32[40,1024]{1,0:T(8,128)S(1)}, f32[40,1024]{1,0:T(8,128)S(1)}, u32[]{:S(2)}, u32[]{:S(2)}) collective-permute-start(f32[40,1024]{1,0:T(8,128)S(1)} %get-tuple-element.71), channel_id=1, source_target_pairs={{0,1},{1,0},{2,3},{3,2},{4,5},{5,4},{6,7},{7,6},{8,9},{9,8},{10,11... | collective-permute-start | bytes 491528 | tf_op jit(solution)/shard_map/ppermute | solution.py:535
  13.6 5.2 %collective-permute-start.1 = (f32[40,1024]{1,0:T(8,128)S(1)}, f32[40,1024]{1,0:T(8,128)S(1)}, u32[]{:S(2)}, u32[]{:S(2)}) collective-permute-start(f32[40,1024]{1,0:T(8,128)S(1)} %get-tuple-element.72), channel_id=1, source_target_pairs={{0,1},{1,0},{2,3},{3,2},{4,5},{5,4},{6,7},{7,6},{8,9},{9,8},{10,11... | collective-permute-start | bytes 491528 | tf_op jit(solution)/shard_map/ppermute | solution.py:535
  14.0 4.8 %collective-permute-start.2 = (f32[40,1024]{1,0:T(8,128)S(1)}, f32[40,1024]{1,0:T(8,128)S(1)}, u32[]{:S(2)}, u32[]{:S(2)}) collective-permute-start(f32[40,1024]{1,0:T(8,128)S(1)} %get-tuple-element.73), channel_id=1, source_target_pairs={{0,1},{1,0},{2,3},{3,2},{4,5},{5,4},{6,7},{7,6},{8,9},{9,8},{10,11... | collective-permute-start | bytes 491528 | tf_op jit(solution)/shard_map/ppermute | solution.py:535
  14.1 4.7 %collective-permute-start.3 = (f32[40,1024]{1,0:T(8,128)S(1)}, f32[40,1024]{1,0:T(8,128)S(1)}, u32[]{:S(2)}, u32[]{:S(2)}) collective-permute-start(f32[40,1024]{1,0:T(8,128)S(1)} %get-tuple-element.74), channel_id=1, source_target_pairs={{0,1},{1,0},{2,3},{3,2},{4,5},{5,4},{6,7},{7,6},{8,9},{9,8},{10,11... | collective-permute-start | bytes 491528 | tf_op jit(solution)/shard_map/ppermute | solution.py:535
  18.3 1.7 %collective-permute-start.5 = (f32[8,1024]{1,0:T(8,128)S(1)}, f32[8,1024]{1,0:T(8,128)S(1)}, u32[]{:S(2)}, u32[]{:S(2)}) collective-permute-start(f32[8,1024]{1,0:T(8,128)S(1)} %get-tuple-element.69.s_here), channel_id=1, source_target_pairs={{0,1},{1,0},{2,3},{3,2},{4,5},{5,4},{6,7},{7,6},{8,9},{9,8},{10,11... | collective-permute-start | bytes 98312 | tf_op jit(solution)/shard_map/ppermute | solution.py:535
  19.8 1.3 collective-permute-start.4
  42.2 4.1 %collective-permute-start.7 = (f32[8,1024]{1,0:T(8,128)S(1)}, f32[8,1024]{1,0:T(8,128)S(1)}, u32[]{:S(2)}, u32[]{:S(2)}) collective-permute-start(f32[8,1024]{1,0:T(8,128)S(1)} %get-tuple-element.85.s_here), channel_id=1, source_target_pairs={{0,1},{1,0},{2,3},{3,2},{4,5},{5,4},{6,7},{7,6},{8,9},{9,8},{10,11... | collective-permute-start | bytes 98312 | tf_op jit(solution)/shard_map/ppermute | solution.py:535
  46.0 1.5 %collective-permute-start.6 = (f32[8,1024]{1,0:T(8,128)S(1)}, f32[8,1024]{1,0:T(8,128)S(1)}, u32[]{:S(2)}, u32[]{:S(2)}) collective-permute-start(f32[8,1024]{1,0:T(8,128)S(1)} %get-tuple-element.87.s_here), channel_id=1, source_target_pairs={{0,1},{1,0},{2,3},{3,2},{4,5},{5,4},{6,7},{7,6},{8,9},{9,8},{10,11... | collective-permute-start | bytes 98312 | tf_op jit(solution)/shard_map/ppermute | solution.py:535
  59.7 9.2 %all-to-all-start.4 = ((f32[8,64,128]{2,1,0:T(8,128)}), f32[8,64,128]{2,1,0:T(8,128)S(1)}, u32[]{:S(2)}, u32[]{:S(2)}) async-start(f32[8,64,128]{2,1,0:T(8,128)} %bitcast.13), calls=%async_computation.4 | async-start | bytes 524288 | tf_op jit(solution)/shard_map/all_to_all | solution.py:538
  63.1 5.1 %collective-permute-start.8 = (f32[64,128]{1,0:T(8,128)S(1)}, f32[64,128]{1,0:T(8,128)S(1)}, u32[]{:S(2)}, u32[]{:S(2)}) collective-permute-start(f32[64,128]{1,0:T(8,128)S(1)} %get-tuple-element.93.moment), channel_id=1, source_target_pairs={{0,64},{16,80},{32,96},{48,112},{64,0},{80,16},{96,32},{112,48},{1... | collective-permute-start | bytes 98312 | tf_op jit(solution)/shard_map/ppermute | solution.py:604
  69.9 4.2 %collective-permute-start.10 = (f32[8,1024]{1,0:T(8,128)S(1)}, f32[8,1024]{1,0:T(8,128)S(1)}, u32[]{:S(2)}, u32[]{:S(2)}) collective-permute-start(f32[8,1024]{1,0:T(8,128)S(1)} %get-tuple-element.96.s_here), channel_id=1, source_target_pairs={{0,1},{1,0},{2,3},{3,2},{4,5},{5,4},{6,7},{7,6},{8,9},{9,8},{10,11... | collective-permute-start | bytes 98312 | tf_op jit(solution)/shard_map/ppermute | solution.py:535
  74.0 1.3 collective-permute-start.9
  77.3 13.1 %all-to-all-start.5 = ((f32[8,96,128]{2,1,0:T(8,128)}), f32[8,96,128]{2,1,0:T(8,128)S(1)}, u32[]{:S(2)}, u32[]{:S(2)}) async-start(f32[8,96,128]{2,1,0:T(8,128)} %bitcast.15), calls=%async_computation.5 | async-start | bytes 786432 | tf_op jit(solution)/shard_map/all_to_all | solution.py:538
  82.2 3.9 %collective-permute-start.11 = (f32[64,128]{1,0:T(8,128)S(1)}, f32[64,128]{1,0:T(8,128)S(1)}, u32[]{:S(2)}, u32[]{:S(2)}) collective-permute-start(f32[64,128]{1,0:T(8,128)S(1)} %get-tuple-element.104), channel_id=1, source_target_pairs={{0,16},{16,0},{32,48},{48,32},{64,80},{80,64},{96,112},{112,96},{1... | collective-permute-start | bytes 98312 | tf_op jit(solution)/shard_map/ppermute | solution.py:604
  83.5 4.3 %collective-permute-start.12 = (f32[64,128]{1,0:T(8,128)S(1)}, f32[64,128]{1,0:T(8,128)S(1)}, u32[]{:S(2)}, u32[]{:S(2)}) collective-permute-start(f32[64,128]{1,0:T(8,128)S(1)} %get-tuple-element.105), channel_id=1, source_target_pairs={{0,32},{16,48},{32,0},{48,16},{64,96},{80,112},{96,64},{112,80},{1... | collective-permute-start | bytes 98312 | tf_op jit(solution)/shard_map/ppermute | solution.py:604
  86.1 4.3 %collective-permute-start.13 = (f32[64,128]{1,0:T(8,128)S(1)}, f32[64,128]{1,0:T(8,128)S(1)}, u32[]{:S(2)}, u32[]{:S(2)}) collective-permute-start(f32[64,128]{1,0:T(8,128)S(1)} %get-tuple-element.106), channel_id=1, source_target_pairs={{0,48},{16,32},{32,16},{48,0},{64,112},{80,96},{96,80},{112,64},{1... | collective-permute-start | bytes 98312 | tf_op jit(solution)/shard_map/ppermute | solution.py:604
  101.9 5.5 %collective-permute-start.15 = (f32[8,1024]{1,0:T(8,128)S(1)}, f32[8,1024]{1,0:T(8,128)S(1)}, u32[]{:S(2)}, u32[]{:S(2)}) collective-permute-start(f32[8,1024]{1,0:T(8,128)S(1)} %get-tuple-element.110.s_here), channel_id=1, source_target_pairs={{0,1},{1,0},{2,3},{3,2},{4,5},{5,4},{6,7},{7,6},{8,9},{9,8},{10,11... | collective-permute-start | bytes 98312 | tf_op jit(solution)/shard_map/ppermute | solution.py:535
  107.1 1.5 %collective-permute-start.14 = (f32[8,1024]{1,0:T(8,128)S(1)}, f32[8,1024]{1,0:T(8,128)S(1)}, u32[]{:S(2)}, u32[]{:S(2)}) collective-permute-start(f32[8,1024]{1,0:T(8,128)S(1)} %get-tuple-element.112.s_here), channel_id=1, source_target_pairs={{0,1},{1,0},{2,3},{3,2},{4,5},{5,4},{6,7},{7,6},{8,9},{9,8},{10,11... | collective-permute-start | bytes 98312 | tf_op jit(solution)/shard_map/ppermute | solution.py:535
  119.9 14.7 %collective-permute-start.16 = (f32[1024,128]{1,0:T(8,128)S(1)}, f32[1024,128]{1,0:T(8,128)S(1)}, u32[]{:S(2)}, u32[]{:S(2)}) collective-permute-start(f32[1024,128]{1,0:T(8,128)S(1)} %get-tuple-element.120), channel_id=1, source_target_pairs={{0,1},{1,0},{2,3},{3,2},{4,5},{5,4},{6,7},{7,6},{8,9},{9,8},{10,11... | collective-permute-start | bytes 1572872 | tf_op jit(solution)/shard_map/ppermute | solution.py:535

commit v5 on v4

--- a/solution.py
+++ b/solution.py
@@ -273,13 +273,13 @@
     model(lambda i: (coh, i * 16), vis, pairs, 0, z_ref, w_ref, s_ref, table, near, far)
 
 
-def own_after_kernel(gathered, coh, vis, pairs, after, *rest):
-    own_kernel(gathered, coh, vis, pairs, *rest)
-
-
 def other_kernel(table, recv_0, recv_1, recv_2, recv_3, z_ref, w_ref, s_ref, near, far):
     received = (recv_0, recv_1, recv_2, recv_3)
     model(lambda i: (received[i // 2], (i % 2) * 16), None, recv_3, 32, z_ref, w_ref, s_ref, table, near, far)
+
+
+def other_after_kernel(table, recv_0, recv_1, recv_2, recv_3, after, *rest):
+    other_kernel(table, recv_0, recv_1, recv_2, recv_3, *rest)
 
 
 def first_other_kernel(
@@ -480,11 +480,8 @@
 
 
 def finish_kernel(
-    moments_hbm, keep, recv, rho_f, gains_hbm, duals_hbm, poly_hbm,
-    moments, gains, duals, poly, thin, deep, sems,
+    moments, keep, recv, rho_f, gains_hbm, duals_hbm, poly_hbm, gains, duals, poly, thin, deep, sems
 ):
-    load = pltpu.make_async_copy(moments_hbm, moments, sems.at[0])
-    load.start()
     chan = lax.axis_index("chan")
     rho = rho_f[...]
     low = lanes() < 64
@@ -498,9 +495,8 @@
     for c in range(8):
         place(thin, now[c], c, 8)
     gains[...] = thin[:, 0:32].reshape(32, 8, 32)
-    stores = [pltpu.make_async_copy(gains, gains_hbm, sems.at[1])]
+    stores = [pltpu.make_async_copy(gains, gains_hbm, sems.at[0])]
     stores[0].start()
-    load.wait()
     at = basis_at(chan)
     fitted = [None] * 8
     for t in range(TERMS):
@@ -519,12 +515,12 @@
             place(deep, value, c * 4 + t, 32)
             fitted[c] = value if t == 0 else fitted[c] + at[t] * value
     poly[...] = deep[:, 0:32].reshape(32, 8, 4, 32)
-    stores.append(pltpu.make_async_copy(poly, poly_hbm, sems.at[2]))
+    stores.append(pltpu.make_async_copy(poly, poly_hbm, sems.at[1]))
     stores[1].start()
     for c in range(8):
         place(thin, now[8 + c] + rho * (now[c] - fitted[c]), c, 8)
     duals[...] = thin[:, 0:32].reshape(32, 8, 32)
-    stores.append(pltpu.make_async_copy(duals, duals_hbm, sems.at[3]))
+    stores.append(pltpu.make_async_copy(duals, duals_hbm, sems.at[2]))
     stores[2].start()
     for store in stores:
         store.wait()
@@ -575,11 +571,11 @@
     )(table, *received, state_keep, rho_a)
 
     def step_model(spread, *after):
-        kernel = own_after_kernel if after else own_kernel
-        *own, table = call(kernel, half_outs + [table_out], pair_scratch, hbm=(4,), n_in=4 + len(after))(
-            exchange(spread, "st"), coh_keep, vis, station_pairs, *after
+        *own, table = call(own_kernel, half_outs + [table_out], pair_scratch, n_in=4)(
+            exchange(spread, "st"), coh_keep, vis, station_pairs
         )
-        other = call(other_kernel, half_outs, pair_scratch, n_in=5)(table, *received)
+        kernel = other_after_kernel if after else other_kernel
+        other = call(kernel, half_outs, pair_scratch, hbm=(5,), n_in=5 + len(after))(table, *received, *after)
         return own, other
 
     def step_sums(own, other, kernel=sums_own_kernel, outs=(), extra=()):
@@ -619,10 +615,10 @@
         finish_kernel,
         [((32, 8, 32), F32), ((32, 8, 32), F32), ((32, 8, 4, 32), F32)],
         [
-            pltpu.VMEM((512, 128), F32), state_in, state_in, pltpu.VMEM((32, 8, TERMS, 32), F32),
-            thin, pltpu.VMEM((1024, 128), F32), pltpu.SemaphoreType.DMA((4,)),
+            state_in, state_in, pltpu.VMEM((32, 8, TERMS, 32), F32),
+            thin, pltpu.VMEM((1024, 128), F32), pltpu.SemaphoreType.DMA((3,)),
         ],
-        hbm=(0,), hbm_out=(0, 1, 2), n_in=4,
+        hbm_out=(0, 1, 2), n_in=4,
     )(moments, keep, swap(send), rho_f)
     return gains_out[None], duals_out[None], poly_out
 

time: 137 us -> 136 us (level)
  starting transfers between devices: 37.7 us -> 35.9 us
    all_to_all x3, waiting for transfers between devices: 3.25 us -> 5.02 us  [exchange(): return lax.all_to_all(x, axis, 0, 0, tiled=True)]
    ppermute x4, waiting for transfers between devices: 6.03 us -> 4.27 us  [from_channel(): return lax.ppermute(x, 'chan', [(f, f ^ distance) for f in range(CHANNELS)])]
  transfers between devices with their start and end apart: 20 -> 20, of which waited for: 8 -> 7; matrix products, arithmetic and copies ran while one was open for 0% -> 0% of each run, Pallas kernels for 8% -> 9%
where the time goes in v5:
time: 136 us
  blocking collectives  62.7 us (46%)
  starting transfers between devices  35.9 us (26%)
  Pallas kernels  23.2 us (17%)
  waiting for transfers between devices  9.72 us (7%)
  local copies, waits for them, and re-layouts  2.92 us (2%)
    all_to_all x6, blocking collectives, exchange(): return lax.all_to_all(x, axis, 0, 0, tiled=True)  62.7 us
    all_to_all x3, starting transfers between devices, exchange(): return lax.all_to_all(x, axis, 0, 0, tiled=True)  14.3 us
    ppermute x13, starting transfers between devices, swap(): return lax.ppermute(x, 'core', CORE_SWAP)  14.3 us
    ppermute x4, starting transfers between devices, from_channel(): return lax.ppermute(x, 'chan', [(f, f ^ distance) for f in range(CHANNELS)])  7.31 us
    pallas_call x4, Pallas kernels, step_sums(): call(kernel, [sums_out, *outs], [left, total, hot], n_in=6 + len(extra))  5.53 us
    all_to_all x3, waiting for transfers between devices, exchange(): return lax.all_to_all(x, axis, 0, 0, tiled=True)  5.02 us
    ppermute x4, waiting for transfers between devices, from_channel(): return lax.ppermute(x, 'chan', [(f, f ^ distance) for f in range(CHANNELS)])  4.27 us
    pallas_call x4, Pallas kernels, step_sums(): call(sums_other_kernel, [((384, STATIONS), F32)], [left, hot], n_in=5)  4.2 us
  transfers between devices with their start and end apart: 20, of which 7 were waited for; matrix products, arithmetic and copies ran while one was open for 0% of the time, Pallas kernels for 9%

profile of v5, /device:TPU:1, one launch (start us, length us, event | category | flops | bytes accessed | tf_op | source)
XLA Modules:
  0.0 135.5 jit_solution(803075405669772515)
XLA Ops:
  0.6 0.0 copy-start.4
  0.7 1.0 copy-done.4
  1.6 0.8 shard_map.94
  2.4 7.3 %all-to-all-start = ((f32[16,32,128]{2,1,0:T(8,128)}), f32[16,32,128]{2,1,0:T(8,128)S(1)}, u32[]{:S(2)}, u32[]{:S(2)}) async-start(f32[16,32,128]{2,1,0:T(8,128)} %bitcast.1), calls=%async_computation | async-start | bytes 524288 | tf_op jit(solution)/shard_map/all_to_all | solution.py:534
  9.8 0.0 copy-start.2
  9.8 1.0 copy-done.2
  10.8 0.9 copy-done.6
  11.7 1.6 %shard_map.95 = (f32[128,1024]{1,0:T(8,128)S(1)}, f32[192,128]{1,0:T(8,128)S(1)}, f32[8,128]{1,0:T(8,128)S(1)}, f32[8,128]{1,0:T(8,128)S(1)}, f32[40,1024]{1,0:T...) custom-call(f32[8,128]{1,0:T(8,128)S(1)} %get-tuple-element.65.mark, ...), custom_call_target="tpu_custom_call" | custom-call | bytes 1000 | tf_op jit(solution)/shard_map/pallas_call | solution.py:545
  13.4 0.2 collective-permute-start
  13.6 0.4 collective-permute-start.1
  14.0 0.1 collective-permute-start.2
  14.1 0.4 collective-permute-start.3
  14.5 2.6 %all-to-all-done = f32[16,32,128]{2,1,0:T(8,128)S(1)} async-done(((f32[16,32,128]{2,1,0:T(8,128)}), f32[16,32,128]{2,1,0:T(8,128)S(1)}, u32[]{:S(2)}, u32[]{:S(2)}) %all-to-all-start) | async-done | bytes 262176 | tf_op jit(solution)/shard_map/all_to_all | solution.py:534
  17.1 1.2 shard_map.96
  18.4 0.5 collective-permute-start.5
  18.8 0.0 collective-permute-done.recv_0
  18.8 0.0 collective-permute-done.1.recv_1
  18.8 0.0 collective-permute-done.2.recv_2
  18.9 1.0 shard_map.97
  19.9 0.2 collective-permute-start.4
  20.1 1.1 shard_map.98.before
  21.1 0.0 collective-permute-done.4.s_there
  21.2 1.2 shard_map.99
  22.4 10.2 %all_to_all.99 = f32[8,96,128]{2,1,0:T(8,128)S(1)} all-to-all(f32[8,96,128]{2,1,0:T(8,128)S(1)} %bitcast.27), channel_id=1, replica_groups=mesh['chan'=8,'st'=8,'core'=2] {'st'}, dimensions={0} | all-to-all | bytes 786432 | tf_op jit(solution)/shard_map/all_to_all | solution.py:534
  32.6 0.1 shard_map.100
  32.6 8.5 %all_to_all.100 = f32[8,64,128]{2,1,0:T(8,128)S(1)} all-to-all(f32[8,64,128]{2,1,0:T(8,128)S(1)} %bitcast.47), channel_id=1, replica_groups=mesh['chan'=8,'st'=8,'core'=2] {'st'}, dimensions={0} | all-to-all | bytes 524288 | tf_op jit(solution)/shard_map/all_to_all | solution.py:534
  41.2 1.1 shard_map.101
  42.2 2.8 %collective-permute-start.7 = (f32[8,1024]{1,0:T(8,128)S(1)}, f32[8,1024]{1,0:T(8,128)S(1)}, u32[]{:S(2)}, u32[]{:S(2)}) collective-permute-start(f32[8,1024]{1,0:T(8,128)S(1)} %get-tuple-element.85.s_here), channel_id=1, source_target_pairs={{0,1},{1,0},{2,3},{3,2},{4,5},{5,4},{6,7},{7,6},{8,9},{9,8},{10,11... | collective-permute-start | bytes 98312 | tf_op jit(solution)/shard_map/ppermute | solution.py:531
  45.1 1.0 shard_map.102
  46.1 0.3 collective-permute-start.6
  46.4 1.0 shard_map.103.before
  47.4 0.1 collective-permute-done.6.s_there
  47.6 1.2 shard_map.104
  48.8 10.2 %all_to_all.101 = f32[8,96,128]{2,1,0:T(8,128)S(1)} all-to-all(f32[8,96,128]{2,1,0:T(8,128)S(1)} %bitcast.28), channel_id=1, replica_groups=mesh['chan'=8,'st'=8,'core'=2] {'st'}, dimensions={0} | all-to-all | bytes 786432 | tf_op jit(solution)/shard_map/all_to_all | solution.py:534
  59.0 0.8 shard_map.105
  59.7 3.4 %all-to-all-start.4 = ((f32[8,64,128]{2,1,0:T(8,128)}), f32[8,64,128]{2,1,0:T(8,128)S(1)}, u32[]{:S(2)}, u32[]{:S(2)}) async-start(f32[8,64,128]{2,1,0:T(8,128)} %bitcast.13), calls=%async_computation.4 | async-start | bytes 524288 | tf_op jit(solution)/shard_map/all_to_all | solution.py:534
  63.1 3.4 %collective-permute-start.8 = (f32[64,128]{1,0:T(8,128)S(1)}, f32[64,128]{1,0:T(8,128)S(1)}, u32[]{:S(2)}, u32[]{:S(2)}) collective-permute-start(f32[64,128]{1,0:T(8,128)S(1)} %get-tuple-element.97.moment), channel_id=1, source_target_pairs={{0,64},{16,80},{32,96},{48,112},{64,0},{80,16},{96,32},{112,48},{1... | collective-permute-start | bytes 98312 | tf_op jit(solution)/shard_map/ppermute | solution.py:600
  66.5 2.4 %all-to-all-done.4 = f32[8,64,128]{2,1,0:T(8,128)S(1)} async-done(((f32[8,64,128]{2,1,0:T(8,128)}), f32[8,64,128]{2,1,0:T(8,128)S(1)}, u32[]{:S(2)}, u32[]{:S(2)}) %all-to-all-start.4) | async-done | bytes 262176 | tf_op jit(solution)/shard_map/all_to_all | solution.py:534
  68.9 1.1 shard_map.106
  70.0 3.1 %collective-permute-start.10 = (f32[8,1024]{1,0:T(8,128)S(1)}, f32[8,1024]{1,0:T(8,128)S(1)}, u32[]{:S(2)}, u32[]{:S(2)}) collective-permute-start(f32[8,1024]{1,0:T(8,128)S(1)} %get-tuple-element.95.s_here), channel_id=1, source_target_pairs={{0,1},{1,0},{2,3},{3,2},{4,5},{5,4},{6,7},{7,6},{8,9},{9,8},{10,11... | collective-permute-start | bytes 98312 | tf_op jit(solution)/shard_map/ppermute | solution.py:531
  73.1 1.0 shard_map.107
  74.1 0.1 collective-permute-start.9
  74.2 1.0 shard_map.108.before
  75.2 0.1 collective-permute-done.9.s_there
  75.4 2.0 %shard_map.109 = (f32[768,128]{1,0:T(8,128)}, f32[64,128]{1,0:T(8,128)S(1)}, f32[64,128]{1,0:T(8,128)S(1)}, f32[64,128]{1,0:T(8,128)S(1)}, f32[64,128]{1,0:T(8,128)S(1)}) custom-call(f32[128,1024]{1,0:T(8,128)S(1)} %get-tuple-element.93.z_ref, f32[128,1024]{1,0:T(8,128)S(1)} %get-tuple-element.94.w_ref, f32[8,1024]{1,0:T(8,128)S(1)} %get-tuple-element.95.s_here, ...), custom_call_target="tpu_custom_call" | custom-call | bytes 1000 | tf_op jit(solution)/shard_map/pallas_call | solution.py:587
  77.3 3.6 %all-to-all-start.5 = ((f32[8,96,128]{2,1,0:T(8,128)}), f32[8,96,128]{2,1,0:T(8,128)S(1)}, u32[]{:S(2)}, u32[]{:S(2)}) async-start(f32[8,96,128]{2,1,0:T(8,128)} %bitcast.15), calls=%async_computation.5 | async-start | bytes 786432 | tf_op jit(solution)/shard_map/all_to_all | solution.py:534
  80.9 1.3 collective-permute-start.11
  82.2 2.6 %collective-permute-start.12 = (f32[64,128]{1,0:T(8,128)S(1)}, f32[64,128]{1,0:T(8,128)S(1)}, u32[]{:S(2)}, u32[]{:S(2)}) collective-permute-start(f32[64,128]{1,0:T(8,128)S(1)} %get-tuple-element.105), channel_id=1, source_target_pairs={{0,32},{16,48},{32,0},{48,16},{64,96},{80,112},{96,64},{112,80},{1... | collective-permute-start | bytes 98312 | tf_op jit(solution)/shard_map/ppermute | solution.py:600
  84.9 1.6 %collective-permute-done.12.part_2 = f32[64,128]{1,0:T(8,128)S(1)} collective-permute-done((f32[64,128]{1,0:T(8,128)S(1)}, f32[64,128]{1,0:T(8,128)S(1)}, u32[]{:S(2)}, u32[]{:S(2)}) %collective-permute-start.12) | collective-permute-done | bytes 32800 | tf_op jit(solution)/shard_map/ppermute | solution.py:600
  86.5 2.6 %collective-permute-done.13.part_3 = f32[64,128]{1,0:T(8,128)S(1)} collective-permute-done((f32[64,128]{1,0:T(8,128)S(1)}, f32[64,128]{1,0:T(8,128)S(1)}, u32[]{:S(2)}, u32[]{:S(2)}) %collective-permute-start.13) | collective-permute-done | bytes 32800 | tf_op jit(solution)/shard_map/ppermute | solution.py:600
  89.1 0.1 shard_map.110
  89.2 10.4 %all_to_all.102 = f32[8,64,128]{2,1,0:T(8,128)S(1)} all-to-all(f32[8,64,128]{2,1,0:T(8,128)S(1)} %bitcast.46), channel_id=1, replica_groups=mesh['chan'=8,'st'=8,'core'=2] {'st'}, dimensions={0} | all-to-all | bytes 524288 | tf_op jit(solution)/shard_map/all_to_all | solution.py:534
  99.6 1.1 shard_map.111
  100.7 3.9 %collective-permute-start.15 = (f32[8,1024]{1,0:T(8,128)S(1)}, f32[8,1024]{1,0:T(8,128)S(1)}, u32[]{:S(2)}, u32[]{:S(2)}) collective-permute-start(f32[8,1024]{1,0:T(8,128)S(1)} %get-tuple-element.110.s_here), channel_id=1, source_target_pairs={{0,1},{1,0},{2,3},{3,2},{4,5},{5,4},{6,7},{7,6},{8,9},{9,8},{10,11... | collective-permute-start | bytes 98312 | tf_op jit(solution)/shard_map/ppermute | solution.py:531
  104.6 1.0 shard_map.112
  105.6 0.3 collective-permute-start.14
  106.0 1.1 shard_map.113.before
  107.0 0.1 collective-permute-done.14.s_there
  107.2 1.2 shard_map.114
  108.4 10.2 %all_to_all.103 = f32[8,96,128]{2,1,0:T(8,128)S(1)} all-to-all(f32[8,96,128]{2,1,0:T(8,128)S(1)} %bitcast.29), channel_id=1, replica_groups=mesh['chan'=8,'st'=8,'core'=2] {'st'}, dimensions={0} | all-to-all | bytes 786432 | tf_op jit(solution)/shard_map/all_to_all | solution.py:534
  118.5 0.2 shard_map.115
  118.7 2.0 %collective-permute-start.16 = (f32[1024,128]{1,0:T(8,128)S(1)}, f32[1024,128]{1,0:T(8,128)S(1)}, u32[]{:S(2)}, u32[]{:S(2)}) collective-permute-start(f32[1024,128]{1,0:T(8,128)S(1)} %get-tuple-element.120), channel_id=1, source_target_pairs={{0,1},{1,0},{2,3},{3,2},{4,5},{5,4},{6,7},{7,6},{8,9},{9,8},{10,11... | collective-permute-start | bytes 1572872 | tf_op jit(solution)/shard_map/ppermute | solution.py:531
  120.7 13.2 %all_to_all.104 = f32[16,32,128]{2,1,0:T(8,128)S(1)} all-to-all(f32[16,32,128]{2,1,0:T(8,128)S(1)} %bitcast.45), channel_id=1, replica_groups=mesh['chan'=8,'st'=8,'core'=2] {'chan','core'}, dimensions={0} | all-to-all | bytes 524288 | tf_op jit(solution)/shard_map/all_to_all | solution.py:534
  133.8 1.5 %shard_map.116 = (f32[32,8,32]{2,1,0:T(8,128)}, f32[32,8,32]{2,1,0:T(8,128)}, f32[32,8,4,32]{3,2,1,0:T(4,128)}) custom-call(f32[512,128]{1,0:T(8,128)S(1)} %bitcast.37, f32[128,128]{1,0:T(8,128)S(1)} %get-tuple-element.119.keep, f32[1024,128]{1,0:T(8,128)S(1)} %collective-permute-done.16.recv, f32[8,128]{1,0:T(8,128)S(1)} %get-tuple-element.121.rho_f), custom_call_target="tpu_custom_call" | custom-call | bytes 1000 | tf_op jit(solution)/shard_map/pallas_call | solution.py:614
  (22 shorter events, 0.1 us)
Async XLA Ops:
  0.6 9.1 %copy-start.1 = (bf16[1,32,8,1024]{3,2,1,0:T(8,128)(2,1)S(1)}, bf16[1,32,8,1024]{3,2,1,0:T(8,128)(2,1)}, u32[]{:S(2)}) copy-start(bf16[1,32,8,1024]{3,2,1,0:T(8,128)(2,1)} %param.7) | copy-start | bytes 1572868
  0.6 1.0 copy-start.4
  1.6 8.1 %copy-start.7 = (f32[32]{0:T(128)S(1)}, f32[32]{0:T(128)}, u32[]{:S(2)}) copy-start(f32[32]{0:T(128)} %param.13) | copy-start | bytes 388
  2.4 7.3 %copy-start = (s32[2,1024]{1,0:T(2,128)S(1)}, s32[2,1024]{1,0:T(2,128)}, u32[]{:S(2)}) copy-start(s32[2,1024]{1,0:T(2,128)} %pairs.17) | copy-start | bytes 24580
  2.4 7.3 %copy-start.5 = (f32[1,32,8,32]{3,2,1,0:T(8,128)S(1)}, f32[1,32,8,32]{3,2,1,0:T(8,128)}, u32[]{:S(2)}) copy-start(f32[1,32,8,32]{3,2,1,0:T(8,128)} %param.10) | copy-start | bytes 98308
  2.4 14.7 %all-to-all-start = ((f32[16,32,128]{2,1,0:T(8,128)}), f32[16,32,128]{2,1,0:T(8,128)S(1)}, u32[]{:S(2)}, u32[]{:S(2)}) async-start(f32[16,32,128]{2,1,0:T(8,128)} %bitcast.1), calls=%async_computation | async-start | bytes 524288 | tf_op jit(solution)/shard_map/all_to_all | solution.py:534
  9.8 1.0 copy-start.2
  10.8 0.9 copy-start.6
  11.7 5.4 %copy-start.3 = (f32[1,8,1024]{2,1,0:T(8,128)S(1)}, f32[1,8,1024]{2,1,0:T(8,128)}, u32[]{:S(2)}) copy-start(f32[1,8,1024]{2,1,0:T(8,128)} %param.8) | copy-start | bytes 98308
  13.4 5.4 %collective-permute-start = (f32[40,1024]{1,0:T(8,128)S(1)}, f32[40,1024]{1,0:T(8,128)S(1)}, u32[]{:S(2)}, u32[]{:S(2)}) collective-permute-start(f32[40,1024]{1,0:T(8,128)S(1)} %get-tuple-element.71), channel_id=1, source_target_pairs={{0,1},{1,0},{2,3},{3,2},{4,5},{5,4},{6,7},{7,6},{8,9},{9,8},{10,11... | collective-permute-start | bytes 491528 | tf_op jit(solution)/shard_map/ppermute | solution.py:531
  13.6 5.3 %collective-permute-start.1 = (f32[40,1024]{1,0:T(8,128)S(1)}, f32[40,1024]{1,0:T(8,128)S(1)}, u32[]{:S(2)}, u32[]{:S(2)}) collective-permute-start(f32[40,1024]{1,0:T(8,128)S(1)} %get-tuple-element.72), channel_id=1, source_target_pairs={{0,1},{1,0},{2,3},{3,2},{4,5},{5,4},{6,7},{7,6},{8,9},{9,8},{10,11... | collective-permute-start | bytes 491528 | tf_op jit(solution)/shard_map/ppermute | solution.py:531
  14.0 4.9 %collective-permute-start.2 = (f32[40,1024]{1,0:T(8,128)S(1)}, f32[40,1024]{1,0:T(8,128)S(1)}, u32[]{:S(2)}, u32[]{:S(2)}) collective-permute-start(f32[40,1024]{1,0:T(8,128)S(1)} %get-tuple-element.73), channel_id=1, source_target_pairs={{0,1},{1,0},{2,3},{3,2},{4,5},{5,4},{6,7},{7,6},{8,9},{9,8},{10,11... | collective-permute-start | bytes 491528 | tf_op jit(solution)/shard_map/ppermute | solution.py:531
  14.1 4.8 %collective-permute-start.3 = (f32[40,1024]{1,0:T(8,128)S(1)}, f32[40,1024]{1,0:T(8,128)S(1)}, u32[]{:S(2)}, u32[]{:S(2)}) collective-permute-start(f32[40,1024]{1,0:T(8,128)S(1)} %get-tuple-element.74), channel_id=1, source_target_pairs={{0,1},{1,0},{2,3},{3,2},{4,5},{5,4},{6,7},{7,6},{8,9},{9,8},{10,11... | collective-permute-start | bytes 491528 | tf_op jit(solution)/shard_map/ppermute | solution.py:531
  18.4 1.7 %collective-permute-start.5 = (f32[8,1024]{1,0:T(8,128)S(1)}, f32[8,1024]{1,0:T(8,128)S(1)}, u32[]{:S(2)}, u32[]{:S(2)}) collective-permute-start(f32[8,1024]{1,0:T(8,128)S(1)} %get-tuple-element.69.s_here), channel_id=1, source_target_pairs={{0,1},{1,0},{2,3},{3,2},{4,5},{5,4},{6,7},{7,6},{8,9},{9,8},{10,11... | collective-permute-start | bytes 98312 | tf_op jit(solution)/shard_map/ppermute | solution.py:531
  19.9 1.3 collective-permute-start.4
  42.2 4.1 %collective-permute-start.7 = (f32[8,1024]{1,0:T(8,128)S(1)}, f32[8,1024]{1,0:T(8,128)S(1)}, u32[]{:S(2)}, u32[]{:S(2)}) collective-permute-start(f32[8,1024]{1,0:T(8,128)S(1)} %get-tuple-element.85.s_here), channel_id=1, source_target_pairs={{0,1},{1,0},{2,3},{3,2},{4,5},{5,4},{6,7},{7,6},{8,9},{9,8},{10,11... | collective-permute-start | bytes 98312 | tf_op jit(solution)/shard_map/ppermute | solution.py:531
  46.1 1.5 %collective-permute-start.6 = (f32[8,1024]{1,0:T(8,128)S(1)}, f32[8,1024]{1,0:T(8,128)S(1)}, u32[]{:S(2)}, u32[]{:S(2)}) collective-permute-start(f32[8,1024]{1,0:T(8,128)S(1)} %get-tuple-element.87.s_here), channel_id=1, source_target_pairs={{0,1},{1,0},{2,3},{3,2},{4,5},{5,4},{6,7},{7,6},{8,9},{9,8},{10,11... | collective-permute-start | bytes 98312 | tf_op jit(solution)/shard_map/ppermute | solution.py:531
  59.7 9.2 %all-to-all-start.4 = ((f32[8,64,128]{2,1,0:T(8,128)}), f32[8,64,128]{2,1,0:T(8,128)S(1)}, u32[]{:S(2)}, u32[]{:S(2)}) async-start(f32[8,64,128]{2,1,0:T(8,128)} %bitcast.13), calls=%async_computation.4 | async-start | bytes 524288 | tf_op jit(solution)/shard_map/all_to_all | solution.py:534
  63.1 9.9 %collective-permute-start.8 = (f32[64,128]{1,0:T(8,128)S(1)}, f32[64,128]{1,0:T(8,128)S(1)}, u32[]{:S(2)}, u32[]{:S(2)}) collective-permute-start(f32[64,128]{1,0:T(8,128)S(1)} %get-tuple-element.97.moment), channel_id=1, source_target_pairs={{0,64},{16,80},{32,96},{48,112},{64,0},{80,16},{96,32},{112,48},{1... | collective-permute-start | bytes 98312 | tf_op jit(solution)/shard_map/ppermute | solution.py:600
  70.0 4.2 %collective-permute-start.10 = (f32[8,1024]{1,0:T(8,128)S(1)}, f32[8,1024]{1,0:T(8,128)S(1)}, u32[]{:S(2)}, u32[]{:S(2)}) collective-permute-start(f32[8,1024]{1,0:T(8,128)S(1)} %get-tuple-element.95.s_here), channel_id=1, source_target_pairs={{0,1},{1,0},{2,3},{3,2},{4,5},{5,4},{6,7},{7,6},{8,9},{9,8},{10,11... | collective-permute-start | bytes 98312 | tf_op jit(solution)/shard_map/ppermute | solution.py:531
  74.1 1.3 collective-permute-start.9
  77.3 11.8 %all-to-all-start.5 = ((f32[8,96,128]{2,1,0:T(8,128)}), f32[8,96,128]{2,1,0:T(8,128)S(1)}, u32[]{:S(2)}, u32[]{:S(2)}) async-start(f32[8,96,128]{2,1,0:T(8,128)} %bitcast.15), calls=%async_computation.5 | async-start | bytes 786432 | tf_op jit(solution)/shard_map/all_to_all | solution.py:534
  80.9 3.9 %collective-permute-start.11 = (f32[64,128]{1,0:T(8,128)S(1)}, f32[64,128]{1,0:T(8,128)S(1)}, u32[]{:S(2)}, u32[]{:S(2)}) collective-permute-start(f32[64,128]{1,0:T(8,128)S(1)} %get-tuple-element.104), channel_id=1, source_target_pairs={{0,16},{16,0},{32,48},{48,32},{64,80},{80,64},{96,112},{112,96},{1... | collective-permute-start | bytes 98312 | tf_op jit(solution)/shard_map/ppermute | solution.py:600
  82.2 4.3 %collective-permute-start.12 = (f32[64,128]{1,0:T(8,128)S(1)}, f32[64,128]{1,0:T(8,128)S(1)}, u32[]{:S(2)}, u32[]{:S(2)}) collective-permute-start(f32[64,128]{1,0:T(8,128)S(1)} %get-tuple-element.105), channel_id=1, source_target_pairs={{0,32},{16,48},{32,0},{48,16},{64,96},{80,112},{96,64},{112,80},{1... | collective-permute-start | bytes 98312 | tf_op jit(solution)/shard_map/ppermute | solution.py:600
  84.9 4.3 %collective-permute-start.13 = (f32[64,128]{1,0:T(8,128)S(1)}, f32[64,128]{1,0:T(8,128)S(1)}, u32[]{:S(2)}, u32[]{:S(2)}) collective-permute-start(f32[64,128]{1,0:T(8,128)S(1)} %get-tuple-element.106), channel_id=1, source_target_pairs={{0,48},{16,32},{32,16},{48,0},{64,112},{80,96},{96,80},{112,64},{1... | collective-permute-start | bytes 98312 | tf_op jit(solution)/shard_map/ppermute | solution.py:600
  100.7 5.3 %collective-permute-start.15 = (f32[8,1024]{1,0:T(8,128)S(1)}, f32[8,1024]{1,0:T(8,128)S(1)}, u32[]{:S(2)}, u32[]{:S(2)}) collective-permute-start(f32[8,1024]{1,0:T(8,128)S(1)} %get-tuple-element.110.s_here), channel_id=1, source_target_pairs={{0,1},{1,0},{2,3},{3,2},{4,5},{5,4},{6,7},{7,6},{8,9},{9,8},{10,11... | collective-permute-start | bytes 98312 | tf_op jit(solution)/shard_map/ppermute | solution.py:531
  105.6 1.5 %collective-permute-start.14 = (f32[8,1024]{1,0:T(8,128)S(1)}, f32[8,1024]{1,0:T(8,128)S(1)}, u32[]{:S(2)}, u32[]{:S(2)}) collective-permute-start(f32[8,1024]{1,0:T(8,128)S(1)} %get-tuple-element.112.s_here), channel_id=1, source_target_pairs={{0,1},{1,0},{2,3},{3,2},{4,5},{5,4},{6,7},{7,6},{8,9},{9,8},{10,11... | collective-permute-start | bytes 98312 | tf_op jit(solution)/shard_map/ppermute | solution.py:531
  118.7 15.1 %collective-permute-start.16 = (f32[1024,128]{1,0:T(8,128)S(1)}, f32[1024,128]{1,0:T(8,128)S(1)}, u32[]{:S(2)}, u32[]{:S(2)}) collective-permute-start(f32[1024,128]{1,0:T(8,128)S(1)} %get-tuple-element.120), channel_id=1, source_target_pairs={{0,1},{1,0},{2,3},{3,2},{4,5},{5,4},{6,7},{7,6},{8,9},{9,8},{10,11... | collective-permute-start | bytes 1572872 | tf_op jit(solution)/shard_map/ppermute | solution.py:531

commit v6 on v5

--- a/solution.py
+++ b/solution.py
@@ -499,6 +499,7 @@
     stores[0].start()
     at = basis_at(chan)
     fitted = [None] * 8
+    terms = []
     for t in range(TERMS):
         halves = []
         for half in range(2):
@@ -511,17 +512,23 @@
                 halves.append(total)
         real = [jnp.where(low, halves[c], pltpu.roll(halves[4 + c], 64, 1)) for c in range(4)]
         imag = [jnp.where(low, pltpu.roll(halves[c], 64, 1), halves[4 + c]) for c in range(4)]
+        terms.append(real + imag)
         for c, value in enumerate(real + imag):
-            place(deep, value, c * 4 + t, 32)
             fitted[c] = value if t == 0 else fitted[c] + at[t] * value
-    poly[...] = deep[:, 0:32].reshape(32, 8, 4, 32)
-    stores.append(pltpu.make_async_copy(poly, poly_hbm, sems.at[1]))
-    stores[1].start()
     for c in range(8):
         place(thin, now[8 + c] + rho * (now[c] - fitted[c]), c, 8)
     duals[...] = thin[:, 0:32].reshape(32, 8, 32)
-    stores.append(pltpu.make_async_copy(duals, duals_hbm, sems.at[2]))
-    stores[2].start()
+    stores.append(pltpu.make_async_copy(duals, duals_hbm, sems.at[1]))
+    stores[1].start()
+    for q in range(4):
+        for t in range(TERMS):
+            for c in range(8):
+                part = pltpu.roll(terms[t][c], 128 - 32 * q, 1) if q else terms[t][c]
+                deep[pl.ds(q * 256 + c * 4 + t, 8, stride=32), :] = part
+        dirs = pl.ds(q * 8, 8)
+        poly[dirs] = deep[q * 256:(q + 1) * 256, 0:32].reshape(8, 8, TERMS, 32)
+        stores.append(pltpu.make_async_copy(poly.at[dirs], poly_hbm.at[dirs], sems.at[2 + q]))
+        stores[-1].start()
     for store in stores:
         store.wait()
 
@@ -616,7 +623,7 @@
         [((32, 8, 32), F32), ((32, 8, 32), F32), ((32, 8, 4, 32), F32)],
         [
             state_in, state_in, pltpu.VMEM((32, 8, TERMS, 32), F32),
-            thin, pltpu.VMEM((1024, 128), F32), pltpu.SemaphoreType.DMA((3,)),
+            thin, pltpu.VMEM((1024, 128), F32), pltpu.SemaphoreType.DMA((6,)),
         ],
         hbm_out=(0, 1, 2), n_in=4,
     )(moments, keep, swap(send), rho_f)

time: 136 us -> 136 us (level)
  no operation moved by 1% of the time
where the time goes in v6:
time: 136 us; the launch traced here: 135 us
  blocking collectives  62.7 us (46%)
  starting transfers between devices  35.9 us (26%)
  Pallas kernels  23 us (17%)
  waiting for transfers between devices  9.72 us (7%)
  local copies, waits for them, and re-layouts  2.92 us (2%)
    all_to_all x6, blocking collectives, exchange(): return lax.all_to_all(x, axis, 0, 0, tiled=True)  62.7 us
    all_to_all x3, starting transfers between devices, exchange(): return lax.all_to_all(x, axis, 0, 0, tiled=True)  14.3 us
    ppermute x13, starting transfers between devices, swap(): return lax.ppermute(x, 'core', CORE_SWAP)  14.3 us
    ppermute x4, starting transfers between devices, from_channel(): return lax.ppermute(x, 'chan', [(f, f ^ distance) for f in range(CHANNELS)])  7.31 us
    pallas_call x4, Pallas kernels, step_sums(): call(kernel, [sums_out, *outs], [left, total, hot], n_in=6 + len(extra))  5.53 us
    all_to_all x3, waiting for transfers between devices, exchange(): return lax.all_to_all(x, axis, 0, 0, tiled=True)  5.02 us
    ppermute x4, waiting for transfers between devices, from_channel(): return lax.ppermute(x, 'chan', [(f, f ^ distance) for f in range(CHANNELS)])  4.27 us
    pallas_call x4, Pallas kernels, step_sums(): call(sums_other_kernel, [((384, STATIONS), F32)], [left, hot], n_in=5)  4.2 us
  transfers between devices with their start and end apart: 20, of which 7 were waited for; matrix products, arithmetic and copies ran while one was open for 0% of the time, Pallas kernels for 9%

profile of v6, /device:TPU:1, one launch (start us, length us, event | category | flops | bytes accessed | tf_op | source)
XLA Modules:
  0.0 135.3 jit_solution(15083054779596771586)
XLA Ops:
  0.6 0.0 copy-start.4
  0.7 1.0 copy-done.4
  1.6 0.8 shard_map.94
  2.4 7.3 %all-to-all-start = ((f32[16,32,128]{2,1,0:T(8,128)}), f32[16,32,128]{2,1,0:T(8,128)S(1)}, u32[]{:S(2)}, u32[]{:S(2)}) async-start(f32[16,32,128]{2,1,0:T(8,128)} %bitcast.1), calls=%async_computation | async-start | bytes 524288 | tf_op jit(solution)/shard_map/all_to_all | solution.py:541
  9.8 0.0 copy-start.2
  9.8 1.0 copy-done.2
  10.8 0.9 copy-done.6
  11.7 1.6 %shard_map.95 = (f32[128,1024]{1,0:T(8,128)S(1)}, f32[192,128]{1,0:T(8,128)S(1)}, f32[8,128]{1,0:T(8,128)S(1)}, f32[8,128]{1,0:T(8,128)S(1)}, f32[40,1024]{1,0:T...) custom-call(f32[8,128]{1,0:T(8,128)S(1)} %get-tuple-element.65.mark, ...), custom_call_target="tpu_custom_call" | custom-call | bytes 1000 | tf_op jit(solution)/shard_map/pallas_call | solution.py:552
  13.4 0.2 collective-permute-start
  13.6 0.4 collective-permute-start.1
  14.0 0.1 collective-permute-start.2
  14.1 0.4 collective-permute-start.3
  14.5 2.6 %all-to-all-done = f32[16,32,128]{2,1,0:T(8,128)S(1)} async-done(((f32[16,32,128]{2,1,0:T(8,128)}), f32[16,32,128]{2,1,0:T(8,128)S(1)}, u32[]{:S(2)}, u32[]{:S(2)}) %all-to-all-start) | async-done | bytes 262176 | tf_op jit(solution)/shard_map/all_to_all | solution.py:541
  17.1 1.2 shard_map.96
  18.4 0.5 collective-permute-start.5
  18.8 0.0 collective-permute-done.recv_0
  18.8 0.0 collective-permute-done.1.recv_1
  18.8 0.0 collective-permute-done.2.recv_2
  18.9 1.0 shard_map.97
  19.9 0.2 collective-permute-start.4
  20.1 1.1 shard_map.98.before
  21.1 0.0 collective-permute-done.4.s_there
  21.2 1.2 shard_map.99
  22.4 10.2 %all_to_all.99 = f32[8,96,128]{2,1,0:T(8,128)S(1)} all-to-all(f32[8,96,128]{2,1,0:T(8,128)S(1)} %bitcast.27), channel_id=1, replica_groups=mesh['chan'=8,'st'=8,'core'=2] {'st'}, dimensions={0} | all-to-all | bytes 786432 | tf_op jit(solution)/shard_map/all_to_all | solution.py:541
  32.6 0.1 shard_map.100
  32.6 8.5 %all_to_all.100 = f32[8,64,128]{2,1,0:T(8,128)S(1)} all-to-all(f32[8,64,128]{2,1,0:T(8,128)S(1)} %bitcast.47), channel_id=1, replica_groups=mesh['chan'=8,'st'=8,'core'=2] {'st'}, dimensions={0} | all-to-all | bytes 524288 | tf_op jit(solution)/shard_map/all_to_all | solution.py:541
  41.2 1.1 shard_map.101
  42.2 2.8 %collective-permute-start.7 = (f32[8,1024]{1,0:T(8,128)S(1)}, f32[8,1024]{1,0:T(8,128)S(1)}, u32[]{:S(2)}, u32[]{:S(2)}) collective-permute-start(f32[8,1024]{1,0:T(8,128)S(1)} %get-tuple-element.85.s_here), channel_id=1, source_target_pairs={{0,1},{1,0},{2,3},{3,2},{4,5},{5,4},{6,7},{7,6},{8,9},{9,8},{10,11... | collective-permute-start | bytes 98312 | tf_op jit(solution)/shard_map/ppermute | solution.py:538
  45.1 1.0 shard_map.102
  46.1 0.3 collective-permute-start.6
  46.4 1.0 shard_map.103.before
  47.4 0.1 collective-permute-done.6.s_there
  47.6 1.2 shard_map.104
  48.8 10.2 %all_to_all.101 = f32[8,96,128]{2,1,0:T(8,128)S(1)} all-to-all(f32[8,96,128]{2,1,0:T(8,128)S(1)} %bitcast.28), channel_id=1, replica_groups=mesh['chan'=8,'st'=8,'core'=2] {'st'}, dimensions={0} | all-to-all | bytes 786432 | tf_op jit(solution)/shard_map/all_to_all | solution.py:541
  59.0 0.8 shard_map.105
  59.7 3.4 %all-to-all-start.4 = ((f32[8,64,128]{2,1,0:T(8,128)}), f32[8,64,128]{2,1,0:T(8,128)S(1)}, u32[]{:S(2)}, u32[]{:S(2)}) async-start(f32[8,64,128]{2,1,0:T(8,128)} %bitcast.13), calls=%async_computation.4 | async-start | bytes 524288 | tf_op jit(solution)/shard_map/all_to_all | solution.py:541
  63.1 3.4 %collective-permute-start.8 = (f32[64,128]{1,0:T(8,128)S(1)}, f32[64,128]{1,0:T(8,128)S(1)}, u32[]{:S(2)}, u32[]{:S(2)}) collective-permute-start(f32[64,128]{1,0:T(8,128)S(1)} %get-tuple-element.97.moment), channel_id=1, source_target_pairs={{0,64},{16,80},{32,96},{48,112},{64,0},{80,16},{96,32},{112,48},{1... | collective-permute-start | bytes 98312 | tf_op jit(solution)/shard_map/ppermute | solution.py:607
  66.5 2.4 %all-to-all-done.4 = f32[8,64,128]{2,1,0:T(8,128)S(1)} async-done(((f32[8,64,128]{2,1,0:T(8,128)}), f32[8,64,128]{2,1,0:T(8,128)S(1)}, u32[]{:S(2)}, u32[]{:S(2)}) %all-to-all-start.4) | async-done | bytes 262176 | tf_op jit(solution)/shard_map/all_to_all | solution.py:541
  68.9 1.1 shard_map.106
  70.0 3.1 %collective-permute-start.10 = (f32[8,1024]{1,0:T(8,128)S(1)}, f32[8,1024]{1,0:T(8,128)S(1)}, u32[]{:S(2)}, u32[]{:S(2)}) collective-permute-start(f32[8,1024]{1,0:T(8,128)S(1)} %get-tuple-element.95.s_here), channel_id=1, source_target_pairs={{0,1},{1,0},{2,3},{3,2},{4,5},{5,4},{6,7},{7,6},{8,9},{9,8},{10,11... | collective-permute-start | bytes 98312 | tf_op jit(solution)/shard_map/ppermute | solution.py:538
  73.1 1.0 shard_map.107
  74.1 0.1 collective-permute-start.9
  74.2 1.0 shard_map.108.before
  75.2 0.1 collective-permute-done.9.s_there
  75.4 2.0 %shard_map.109 = (f32[768,128]{1,0:T(8,128)}, f32[64,128]{1,0:T(8,128)S(1)}, f32[64,128]{1,0:T(8,128)S(1)}, f32[64,128]{1,0:T(8,128)S(1)}, f32[64,128]{1,0:T(8,128)S(1)}) custom-call(f32[128,1024]{1,0:T(8,128)S(1)} %get-tuple-element.93.z_ref, f32[128,1024]{1,0:T(8,128)S(1)} %get-tuple-element.94.w_ref, f32[8,1024]{1,0:T(8,128)S(1)} %get-tuple-element.95.s_here, ...), custom_call_target="tpu_custom_call" | custom-call | bytes 1000 | tf_op jit(solution)/shard_map/pallas_call | solution.py:594
  77.3 3.6 %all-to-all-start.5 = ((f32[8,96,128]{2,1,0:T(8,128)}), f32[8,96,128]{2,1,0:T(8,128)S(1)}, u32[]{:S(2)}, u32[]{:S(2)}) async-start(f32[8,96,128]{2,1,0:T(8,128)} %bitcast.15), calls=%async_computation.5 | async-start | bytes 786432 | tf_op jit(solution)/shard_map/all_to_all | solution.py:541
  80.9 1.3 collective-permute-start.11
  82.2 2.6 %collective-permute-start.12 = (f32[64,128]{1,0:T(8,128)S(1)}, f32[64,128]{1,0:T(8,128)S(1)}, u32[]{:S(2)}, u32[]{:S(2)}) collective-permute-start(f32[64,128]{1,0:T(8,128)S(1)} %get-tuple-element.105), channel_id=1, source_target_pairs={{0,32},{16,48},{32,0},{48,16},{64,96},{80,112},{96,64},{112,80},{1... | collective-permute-start | bytes 98312 | tf_op jit(solution)/shard_map/ppermute | solution.py:607
  84.9 1.6 %collective-permute-done.12.part_2 = f32[64,128]{1,0:T(8,128)S(1)} collective-permute-done((f32[64,128]{1,0:T(8,128)S(1)}, f32[64,128]{1,0:T(8,128)S(1)}, u32[]{:S(2)}, u32[]{:S(2)}) %collective-permute-start.12) | collective-permute-done | bytes 32800 | tf_op jit(solution)/shard_map/ppermute | solution.py:607
  86.5 2.6 %collective-permute-done.13.part_3 = f32[64,128]{1,0:T(8,128)S(1)} collective-permute-done((f32[64,128]{1,0:T(8,128)S(1)}, f32[64,128]{1,0:T(8,128)S(1)}, u32[]{:S(2)}, u32[]{:S(2)}) %collective-permute-start.13) | collective-permute-done | bytes 32800 | tf_op jit(solution)/shard_map/ppermute | solution.py:607
  89.1 0.1 shard_map.110
  89.2 10.4 %all_to_all.102 = f32[8,64,128]{2,1,0:T(8,128)S(1)} all-to-all(f32[8,64,128]{2,1,0:T(8,128)S(1)} %bitcast.46), channel_id=1, replica_groups=mesh['chan'=8,'st'=8,'core'=2] {'st'}, dimensions={0} | all-to-all | bytes 524288 | tf_op jit(solution)/shard_map/all_to_all | solution.py:541
  99.6 1.1 shard_map.111
  100.7 3.9 %collective-permute-start.15 = (f32[8,1024]{1,0:T(8,128)S(1)}, f32[8,1024]{1,0:T(8,128)S(1)}, u32[]{:S(2)}, u32[]{:S(2)}) collective-permute-start(f32[8,1024]{1,0:T(8,128)S(1)} %get-tuple-element.110.s_here), channel_id=1, source_target_pairs={{0,1},{1,0},{2,3},{3,2},{4,5},{5,4},{6,7},{7,6},{8,9},{9,8},{10,11... | collective-permute-start | bytes 98312 | tf_op jit(solution)/shard_map/ppermute | solution.py:538
  104.6 1.0 shard_map.112
  105.6 0.3 collective-permute-start.14
  106.0 1.1 shard_map.113.before
  107.0 0.1 collective-permute-done.14.s_there
  107.2 1.2 shard_map.114
  108.4 10.2 %all_to_all.103 = f32[8,96,128]{2,1,0:T(8,128)S(1)} all-to-all(f32[8,96,128]{2,1,0:T(8,128)S(1)} %bitcast.29), channel_id=1, replica_groups=mesh['chan'=8,'st'=8,'core'=2] {'st'}, dimensions={0} | all-to-all | bytes 786432 | tf_op jit(solution)/shard_map/all_to_all | solution.py:541
  118.5 0.2 shard_map.115
  118.7 2.0 %collective-permute-start.16 = (f32[1024,128]{1,0:T(8,128)S(1)}, f32[1024,128]{1,0:T(8,128)S(1)}, u32[]{:S(2)}, u32[]{:S(2)}) collective-permute-start(f32[1024,128]{1,0:T(8,128)S(1)} %get-tuple-element.120), channel_id=1, source_target_pairs={{0,1},{1,0},{2,3},{3,2},{4,5},{5,4},{6,7},{7,6},{8,9},{9,8},{10,11... | collective-permute-start | bytes 1572872 | tf_op jit(solution)/shard_map/ppermute | solution.py:538
  120.7 13.2 %all_to_all.104 = f32[16,32,128]{2,1,0:T(8,128)S(1)} all-to-all(f32[16,32,128]{2,1,0:T(8,128)S(1)} %bitcast.45), channel_id=1, replica_groups=mesh['chan'=8,'st'=8,'core'=2] {'chan','core'}, dimensions={0} | all-to-all | bytes 524288 | tf_op jit(solution)/shard_map/all_to_all | solution.py:541
  133.8 1.3 shard_map.116
  (22 shorter events, 0.1 us)
Async XLA Ops:
  0.6 9.1 %copy-start.1 = (bf16[1,32,8,1024]{3,2,1,0:T(8,128)(2,1)S(1)}, bf16[1,32,8,1024]{3,2,1,0:T(8,128)(2,1)}, u32[]{:S(2)}) copy-start(bf16[1,32,8,1024]{3,2,1,0:T(8,128)(2,1)} %param.7) | copy-start | bytes 1572868
  0.6 1.0 copy-start.4
  1.6 8.1 %copy-start.7 = (f32[32]{0:T(128)S(1)}, f32[32]{0:T(128)}, u32[]{:S(2)}) copy-start(f32[32]{0:T(128)} %param.13) | copy-start | bytes 388
  2.4 7.3 %copy-start = (s32[2,1024]{1,0:T(2,128)S(1)}, s32[2,1024]{1,0:T(2,128)}, u32[]{:S(2)}) copy-start(s32[2,1024]{1,0:T(2,128)} %pairs.17) | copy-start | bytes 24580
  2.4 7.3 %copy-start.5 = (f32[1,32,8,32]{3,2,1,0:T(8,128)S(1)}, f32[1,32,8,32]{3,2,1,0:T(8,128)}, u32[]{:S(2)}) copy-start(f32[1,32,8,32]{3,2,1,0:T(8,128)} %param.10) | copy-start | bytes 98308
  2.4 14.7 %all-to-all-start = ((f32[16,32,128]{2,1,0:T(8,128)}), f32[16,32,128]{2,1,0:T(8,128)S(1)}, u32[]{:S(2)}, u32[]{:S(2)}) async-start(f32[16,32,128]{2,1,0:T(8,128)} %bitcast.1), calls=%async_computation | async-start | bytes 524288 | tf_op jit(solution)/shard_map/all_to_all | solution.py:541
  9.8 1.0 copy-start.2
  10.8 0.9 copy-start.6
  11.7 5.4 %copy-start.3 = (f32[1,8,1024]{2,1,0:T(8,128)S(1)}, f32[1,8,1024]{2,1,0:T(8,128)}, u32[]{:S(2)}) copy-start(f32[1,8,1024]{2,1,0:T(8,128)} %param.8) | copy-start | bytes 98308
  13.4 5.4 %collective-permute-start = (f32[40,1024]{1,0:T(8,128)S(1)}, f32[40,1024]{1,0:T(8,128)S(1)}, u32[]{:S(2)}, u32[]{:S(2)}) collective-permute-start(f32[40,1024]{1,0:T(8,128)S(1)} %get-tuple-element.71), channel_id=1, source_target_pairs={{0,1},{1,0},{2,3},{3,2},{4,5},{5,4},{6,7},{7,6},{8,9},{9,8},{10,11... | collective-permute-start | bytes 491528 | tf_op jit(solution)/shard_map/ppermute | solution.py:538
  13.6 5.3 %collective-permute-start.1 = (f32[40,1024]{1,0:T(8,128)S(1)}, f32[40,1024]{1,0:T(8,128)S(1)}, u32[]{:S(2)}, u32[]{:S(2)}) collective-permute-start(f32[40,1024]{1,0:T(8,128)S(1)} %get-tuple-element.72), channel_id=1, source_target_pairs={{0,1},{1,0},{2,3},{3,2},{4,5},{5,4},{6,7},{7,6},{8,9},{9,8},{10,11... | collective-permute-start | bytes 491528 | tf_op jit(solution)/shard_map/ppermute | solution.py:538
  14.0 4.9 %collective-permute-start.2 = (f32[40,1024]{1,0:T(8,128)S(1)}, f32[40,1024]{1,0:T(8,128)S(1)}, u32[]{:S(2)}, u32[]{:S(2)}) collective-permute-start(f32[40,1024]{1,0:T(8,128)S(1)} %get-tuple-element.73), channel_id=1, source_target_pairs={{0,1},{1,0},{2,3},{3,2},{4,5},{5,4},{6,7},{7,6},{8,9},{9,8},{10,11... | collective-permute-start | bytes 491528 | tf_op jit(solution)/shard_map/ppermute | solution.py:538
  14.1 4.8 %collective-permute-start.3 = (f32[40,1024]{1,0:T(8,128)S(1)}, f32[40,1024]{1,0:T(8,128)S(1)}, u32[]{:S(2)}, u32[]{:S(2)}) collective-permute-start(f32[40,1024]{1,0:T(8,128)S(1)} %get-tuple-element.74), channel_id=1, source_target_pairs={{0,1},{1,0},{2,3},{3,2},{4,5},{5,4},{6,7},{7,6},{8,9},{9,8},{10,11... | collective-permute-start | bytes 491528 | tf_op jit(solution)/shard_map/ppermute | solution.py:538
  18.4 1.7 %collective-permute-start.5 = (f32[8,1024]{1,0:T(8,128)S(1)}, f32[8,1024]{1,0:T(8,128)S(1)}, u32[]{:S(2)}, u32[]{:S(2)}) collective-permute-start(f32[8,1024]{1,0:T(8,128)S(1)} %get-tuple-element.69.s_here), channel_id=1, source_target_pairs={{0,1},{1,0},{2,3},{3,2},{4,5},{5,4},{6,7},{7,6},{8,9},{9,8},{10,11... | collective-permute-start | bytes 98312 | tf_op jit(solution)/shard_map/ppermute | solution.py:538
  19.9 1.3 collective-permute-start.4
  42.2 4.1 %collective-permute-start.7 = (f32[8,1024]{1,0:T(8,128)S(1)}, f32[8,1024]{1,0:T(8,128)S(1)}, u32[]{:S(2)}, u32[]{:S(2)}) collective-permute-start(f32[8,1024]{1,0:T(8,128)S(1)} %get-tuple-element.85.s_here), channel_id=1, source_target_pairs={{0,1},{1,0},{2,3},{3,2},{4,5},{5,4},{6,7},{7,6},{8,9},{9,8},{10,11... | collective-permute-start | bytes 98312 | tf_op jit(solution)/shard_map/ppermute | solution.py:538
  46.1 1.5 %collective-permute-start.6 = (f32[8,1024]{1,0:T(8,128)S(1)}, f32[8,1024]{1,0:T(8,128)S(1)}, u32[]{:S(2)}, u32[]{:S(2)}) collective-permute-start(f32[8,1024]{1,0:T(8,128)S(1)} %get-tuple-element.87.s_here), channel_id=1, source_target_pairs={{0,1},{1,0},{2,3},{3,2},{4,5},{5,4},{6,7},{7,6},{8,9},{9,8},{10,11... | collective-permute-start | bytes 98312 | tf_op jit(solution)/shard_map/ppermute | solution.py:538
  59.7 9.2 %all-to-all-start.4 = ((f32[8,64,128]{2,1,0:T(8,128)}), f32[8,64,128]{2,1,0:T(8,128)S(1)}, u32[]{:S(2)}, u32[]{:S(2)}) async-start(f32[8,64,128]{2,1,0:T(8,128)} %bitcast.13), calls=%async_computation.4 | async-start | bytes 524288 | tf_op jit(solution)/shard_map/all_to_all | solution.py:541
  63.1 9.9 %collective-permute-start.8 = (f32[64,128]{1,0:T(8,128)S(1)}, f32[64,128]{1,0:T(8,128)S(1)}, u32[]{:S(2)}, u32[]{:S(2)}) collective-permute-start(f32[64,128]{1,0:T(8,128)S(1)} %get-tuple-element.97.moment), channel_id=1, source_target_pairs={{0,64},{16,80},{32,96},{48,112},{64,0},{80,16},{96,32},{112,48},{1... | collective-permute-start | bytes 98312 | tf_op jit(solution)/shard_map/ppermute | solution.py:607
  70.0 4.2 %collective-permute-start.10 = (f32[8,1024]{1,0:T(8,128)S(1)}, f32[8,1024]{1,0:T(8,128)S(1)}, u32[]{:S(2)}, u32[]{:S(2)}) collective-permute-start(f32[8,1024]{1,0:T(8,128)S(1)} %get-tuple-element.95.s_here), channel_id=1, source_target_pairs={{0,1},{1,0},{2,3},{3,2},{4,5},{5,4},{6,7},{7,6},{8,9},{9,8},{10,11... | collective-permute-start | bytes 98312 | tf_op jit(solution)/shard_map/ppermute | solution.py:538
  74.1 1.3 collective-permute-start.9
  77.3 11.8 %all-to-all-start.5 = ((f32[8,96,128]{2,1,0:T(8,128)}), f32[8,96,128]{2,1,0:T(8,128)S(1)}, u32[]{:S(2)}, u32[]{:S(2)}) async-start(f32[8,96,128]{2,1,0:T(8,128)} %bitcast.15), calls=%async_computation.5 | async-start | bytes 786432 | tf_op jit(solution)/shard_map/all_to_all | solution.py:541
  80.9 3.9 %collective-permute-start.11 = (f32[64,128]{1,0:T(8,128)S(1)}, f32[64,128]{1,0:T(8,128)S(1)}, u32[]{:S(2)}, u32[]{:S(2)}) collective-permute-start(f32[64,128]{1,0:T(8,128)S(1)} %get-tuple-element.104), channel_id=1, source_target_pairs={{0,16},{16,0},{32,48},{48,32},{64,80},{80,64},{96,112},{112,96},{1... | collective-permute-start | bytes 98312 | tf_op jit(solution)/shard_map/ppermute | solution.py:607
  82.2 4.3 %collective-permute-start.12 = (f32[64,128]{1,0:T(8,128)S(1)}, f32[64,128]{1,0:T(8,128)S(1)}, u32[]{:S(2)}, u32[]{:S(2)}) collective-permute-start(f32[64,128]{1,0:T(8,128)S(1)} %get-tuple-element.105), channel_id=1, source_target_pairs={{0,32},{16,48},{32,0},{48,16},{64,96},{80,112},{96,64},{112,80},{1... | collective-permute-start | bytes 98312 | tf_op jit(solution)/shard_map/ppermute | solution.py:607
  84.9 4.3 %collective-permute-start.13 = (f32[64,128]{1,0:T(8,128)S(1)}, f32[64,128]{1,0:T(8,128)S(1)}, u32[]{:S(2)}, u32[]{:S(2)}) collective-permute-start(f32[64,128]{1,0:T(8,128)S(1)} %get-tuple-element.106), channel_id=1, source_target_pairs={{0,48},{16,32},{32,16},{48,0},{64,112},{80,96},{96,80},{112,64},{1... | collective-permute-start | bytes 98312 | tf_op jit(solution)/shard_map/ppermute | solution.py:607
  100.7 5.3 %collective-permute-start.15 = (f32[8,1024]{1,0:T(8,128)S(1)}, f32[8,1024]{1,0:T(8,128)S(1)}, u32[]{:S(2)}, u32[]{:S(2)}) collective-permute-start(f32[8,1024]{1,0:T(8,128)S(1)} %get-tuple-element.110.s_here), channel_id=1, source_target_pairs={{0,1},{1,0},{2,3},{3,2},{4,5},{5,4},{6,7},{7,6},{8,9},{9,8},{10,11... | collective-permute-start | bytes 98312 | tf_op jit(solution)/shard_map/ppermute | solution.py:538
  105.6 1.5 %collective-permute-start.14 = (f32[8,1024]{1,0:T(8,128)S(1)}, f32[8,1024]{1,0:T(8,128)S(1)}, u32[]{:S(2)}, u32[]{:S(2)}) collective-permute-start(f32[8,1024]{1,0:T(8,128)S(1)} %get-tuple-element.112.s_here), channel_id=1, source_target_pairs={{0,1},{1,0},{2,3},{3,2},{4,5},{5,4},{6,7},{7,6},{8,9},{9,8},{10,11... | collective-permute-start | bytes 98312 | tf_op jit(solution)/shard_map/ppermute | solution.py:538
  118.7 15.1 %collective-permute-start.16 = (f32[1024,128]{1,0:T(8,128)S(1)}, f32[1024,128]{1,0:T(8,128)S(1)}, u32[]{:S(2)}, u32[]{:S(2)}) collective-permute-start(f32[1024,128]{1,0:T(8,128)S(1)} %get-tuple-element.120), channel_id=1, source_target_pairs={{0,1},{1,0},{2,3},{3,2},{4,5},{5,4},{6,7},{7,6},{8,9},{9,8},{10,11... | collective-permute-start | bytes 1572872 | tf_op jit(solution)/shard_map/ppermute | solution.py:538

commit v7 on v6

--- a/solution.py
+++ b/solution.py
@@ -137,9 +137,9 @@
 
 
 def spread_kernel(gains, spread, mark, thin):
-    thin[...] = jnp.zeros((256, 128), F32)
+    thin[...] = jnp.zeros((264, 128), F32)
     mark[...] = jnp.zeros((8, 128), F32)
-    thin[:, 0:32] = gains[...].reshape(256, 32)
+    thin[0:256, 0:32] = gains[...].reshape(256, 32)
     for half in range(2):
         for c in range(4):
             total = None
@@ -196,12 +196,12 @@
                 else:
                     send[which][32:40, c * 128:(c + 1) * 128] = total
 
-    thin[...] = jnp.zeros((256, 128), F32)
+    thin[...] = jnp.zeros((264, 128), F32)
     copies[0].wait()
-    thin[:, 0:32] = gains[...].reshape(256, 32)
+    thin[0:256, 0:32] = gains[...].reshape(256, 32)
     pack(0)
     copies[1].wait()
-    thin[:, 0:32] = duals[...].reshape(256, 32)
+    thin[0:256, 0:32] = duals[...].reshape(256, 32)
     pack(1)
     copies[2].wait()
     place = (2.0 * chan.astype(F32) + 1.0) * (1.0 / CHANNELS) - 1.0
@@ -209,12 +209,12 @@
     fitted = poly[:, :, 0, :]
     for t in range(1, TERMS):
         fitted = fitted + poly[:, :, t, :] * basis[t]
-    thin[:, 0:32] = fitted.reshape(256, 32)
+    thin[0:256, 0:32] = fitted.reshape(256, 32)
     pack(2)
     copies[3].wait()
     for t in range(ROWS // 128):
         cols = slice(t * 128, (t + 1) * 128)
-        wide[t] = coh[:, :, cols].astype(F32).reshape(256, 128)
+        wide[t, 0:256, :] = coh[:, :, cols].astype(F32).reshape(256, 128)
         for c in range(8):
             coh_keep[c * 16:(c + 1) * 16, cols] = wide[t, pl.ds(core * 128 + c, 16, stride=8), :]
             send[c // 2][(c % 2) * 16:(c % 2) * 16 + 16, cols] = wide[t, pl.ds((1 - core) * 128 + c, 16, stride=8), :]
@@ -494,7 +494,7 @@
     now = [keep[c * 8:(c + 1) * 8, :] + recv[c * 8:(c + 1) * 8, :] for c in range(16)]
     for c in range(8):
         place(thin, now[c], c, 8)
-    gains[...] = thin[:, 0:32].reshape(32, 8, 32)
+    gains[...] = thin[0:256, 0:32].reshape(32, 8, 32)
     stores = [pltpu.make_async_copy(gains, gains_hbm, sems.at[0])]
     stores[0].start()
     at = basis_at(chan)
@@ -517,7 +517,7 @@
             fitted[c] = value if t == 0 else fitted[c] + at[t] * value
     for c in range(8):
         place(thin, now[8 + c] + rho * (now[c] - fitted[c]), c, 8)
-    duals[...] = thin[:, 0:32].reshape(32, 8, 32)
+    duals[...] = thin[0:256, 0:32].reshape(32, 8, 32)
     stores.append(pltpu.make_async_copy(duals, duals_hbm, sems.at[1]))
     stores[1].start()
     for q in range(4):
@@ -544,7 +544,7 @@
     wide = ((512, 128), F32)
     small = ((8, 128), F32)
     state_in = pltpu.VMEM((32, 8, 32), F32)
-    thin = pltpu.VMEM((256, 128), F32)
+    thin = pltpu.VMEM((264, 128), F32)
     spread, mark = call(
         spread_kernel, [wide, small], [thin], n_in=1
     )(gains[0])
@@ -554,7 +554,7 @@
         [((128, ROWS), F32), ((192, 128), F32), small, small] + [((40, ROWS), F32)] * 4,
         [
             pltpu.VMEM((32, 8, ROWS), BF16), state_in, state_in, pltpu.VMEM((32, 8, TERMS, 32), F32),
-            pltpu.VMEM((ROWS // 128, 256, 128), F32), thin, pltpu.SemaphoreType.DMA((4,)),
+            pltpu.VMEM((ROWS // 128, 264, 128), F32), thin, pltpu.SemaphoreType.DMA((4,)),
         ],
         hbm=(0, 1, 2, 3, 4), n_in=7,
     )(mark, coherency[0], gains[0], duals[0], poly, station_pairs, jnp.pad(penalty, (0, 96)).reshape(1, 128))
@@ -623,7 +623,7 @@
         [((32, 8, 32), F32), ((32, 8, 32), F32), ((32, 8, 4, 32), F32)],
         [
             state_in, state_in, pltpu.VMEM((32, 8, TERMS, 32), F32),
-            thin, pltpu.VMEM((1024, 128), F32), pltpu.SemaphoreType.DMA((6,)),
+            thin, pltpu.VMEM((1056, 128), F32), pltpu.SemaphoreType.DMA((6,)),
         ],
         hbm_out=(0, 1, 2), n_in=4,
     )(moments, keep, swap(send), rho_f)

time: 136 us -> 136 us (level)
  no operation moved by 1% of the time
where the time goes in v7:
time: 136 us; the launch traced here: 135 us
  blocking collectives  62.7 us (46%)
  starting transfers between devices  35.9 us (26%)
  Pallas kernels  23 us (17%)
  waiting for transfers between devices  9.71 us (7%)
  local copies, waits for them, and re-layouts  2.92 us (2%)
    all_to_all x6, blocking collectives, exchange(): return lax.all_to_all(x, axis, 0, 0, tiled=True)  62.7 us
    all_to_all x3, starting transfers between devices, exchange(): return lax.all_to_all(x, axis, 0, 0, tiled=True)  14.3 us
    ppermute x13, starting transfers between devices, swap(): return lax.ppermute(x, 'core', CORE_SWAP)  14.3 us
    ppermute x4, starting transfers between devices, from_channel(): return lax.ppermute(x, 'chan', [(f, f ^ distance) for f in range(CHANNELS)])  7.31 us
    pallas_call x4, Pallas kernels, step_sums(): call(kernel, [sums_out, *outs], [left, total, hot], n_in=6 + len(extra))  5.53 us
    all_to_all x3, waiting for transfers between devices, exchange(): return lax.all_to_all(x, axis, 0, 0, tiled=True)  5.01 us
    ppermute x4, waiting for transfers between devices, from_channel(): return lax.ppermute(x, 'chan', [(f, f ^ distance) for f in range(CHANNELS)])  4.27 us
    pallas_call x4, Pallas kernels, step_sums(): call(sums_other_kernel, [((384, STATIONS), F32)], [left, hot], n_in=5)  4.2 us
  transfers between devices with their start and end apart: 20, of which 7 were waited for; matrix products, arithmetic and copies ran while one was open for 0% of the time, Pallas kernels for 9%

profile of v7, /device:TPU:1, one launch (start us, length us, event | category | flops | bytes accessed | tf_op | source)
XLA Modules:
  0.0 135.3 jit_solution(4721125248326505412)
XLA Ops:
  0.6 0.0 copy-start.4
  0.7 1.0 copy-done.4
  1.6 0.8 shard_map.94
  2.4 7.3 %all-to-all-start = ((f32[16,32,128]{2,1,0:T(8,128)}), f32[16,32,128]{2,1,0:T(8,128)S(1)}, u32[]{:S(2)}, u32[]{:S(2)}) async-start(f32[16,32,128]{2,1,0:T(8,128)} %bitcast.1), calls=%async_computation | async-start | bytes 524288 | tf_op jit(solution)/shard_map/all_to_all | solution.py:541
  9.8 0.0 copy-start.2
  9.8 1.0 copy-done.2
  10.8 0.9 copy-done.6
  11.7 1.6 %shard_map.95 = (f32[128,1024]{1,0:T(8,128)S(1)}, f32[192,128]{1,0:T(8,128)S(1)}, f32[8,128]{1,0:T(8,128)S(1)}, f32[8,128]{1,0:T(8,128)S(1)}, f32[40,1024]{1,0:T...) custom-call(f32[8,128]{1,0:T(8,128)S(1)} %get-tuple-element.65.mark, ...), custom_call_target="tpu_custom_call" | custom-call | bytes 1000 | tf_op jit(solution)/shard_map/pallas_call | solution.py:552
  13.4 0.2 collective-permute-start
  13.6 0.4 collective-permute-start.1
  14.0 0.1 collective-permute-start.2
  14.1 0.4 collective-permute-start.3
  14.5 2.6 %all-to-all-done = f32[16,32,128]{2,1,0:T(8,128)S(1)} async-done(((f32[16,32,128]{2,1,0:T(8,128)}), f32[16,32,128]{2,1,0:T(8,128)S(1)}, u32[]{:S(2)}, u32[]{:S(2)}) %all-to-all-start) | async-done | bytes 262176 | tf_op jit(solution)/shard_map/all_to_all | solution.py:541
  17.1 1.2 shard_map.96
  18.4 0.5 collective-permute-start.5
  18.8 0.0 collective-permute-done.recv_0
  18.8 0.0 collective-permute-done.1.recv_1
  18.8 0.0 collective-permute-done.2.recv_2
  18.9 1.0 shard_map.97
  19.9 0.2 collective-permute-start.4
  20.1 1.1 shard_map.98.before
  21.1 0.0 collective-permute-done.4.s_there
  21.2 1.2 shard_map.99
  22.4 10.2 %all_to_all.99 = f32[8,96,128]{2,1,0:T(8,128)S(1)} all-to-all(f32[8,96,128]{2,1,0:T(8,128)S(1)} %bitcast.27), channel_id=1, replica_groups=mesh['chan'=8,'st'=8,'core'=2] {'st'}, dimensions={0} | all-to-all | bytes 786432 | tf_op jit(solution)/shard_map/all_to_all | solution.py:541
  32.6 0.1 shard_map.100
  32.6 8.5 %all_to_all.100 = f32[8,64,128]{2,1,0:T(8,128)S(1)} all-to-all(f32[8,64,128]{2,1,0:T(8,128)S(1)} %bitcast.47), channel_id=1, replica_groups=mesh['chan'=8,'st'=8,'core'=2] {'st'}, dimensions={0} | all-to-all | bytes 524288 | tf_op jit(solution)/shard_map/all_to_all | solution.py:541
  41.2 1.1 shard_map.101
  42.2 2.8 %collective-permute-start.7 = (f32[8,1024]{1,0:T(8,128)S(1)}, f32[8,1024]{1,0:T(8,128)S(1)}, u32[]{:S(2)}, u32[]{:S(2)}) collective-permute-start(f32[8,1024]{1,0:T(8,128)S(1)} %get-tuple-element.85.s_here), channel_id=1, source_target_pairs={{0,1},{1,0},{2,3},{3,2},{4,5},{5,4},{6,7},{7,6},{8,9},{9,8},{10,11... | collective-permute-start | bytes 98312 | tf_op jit(solution)/shard_map/ppermute | solution.py:538
  45.1 1.0 shard_map.102
  46.1 0.3 collective-permute-start.6
  46.4 1.0 shard_map.103.before
  47.4 0.1 collective-permute-done.6.s_there
  47.6 1.2 shard_map.104
  48.8 10.2 %all_to_all.101 = f32[8,96,128]{2,1,0:T(8,128)S(1)} all-to-all(f32[8,96,128]{2,1,0:T(8,128)S(1)} %bitcast.28), channel_id=1, replica_groups=mesh['chan'=8,'st'=8,'core'=2] {'st'}, dimensions={0} | all-to-all | bytes 786432 | tf_op jit(solution)/shard_map/all_to_all | solution.py:541
  59.0 0.8 shard_map.105
  59.7 3.4 %all-to-all-start.4 = ((f32[8,64,128]{2,1,0:T(8,128)}), f32[8,64,128]{2,1,0:T(8,128)S(1)}, u32[]{:S(2)}, u32[]{:S(2)}) async-start(f32[8,64,128]{2,1,0:T(8,128)} %bitcast.13), calls=%async_computation.4 | async-start | bytes 524288 | tf_op jit(solution)/shard_map/all_to_all | solution.py:541
  63.1 3.4 %collective-permute-start.8 = (f32[64,128]{1,0:T(8,128)S(1)}, f32[64,128]{1,0:T(8,128)S(1)}, u32[]{:S(2)}, u32[]{:S(2)}) collective-permute-start(f32[64,128]{1,0:T(8,128)S(1)} %get-tuple-element.97.moment), channel_id=1, source_target_pairs={{0,64},{16,80},{32,96},{48,112},{64,0},{80,16},{96,32},{112,48},{1... | collective-permute-start | bytes 98312 | tf_op jit(solution)/shard_map/ppermute | solution.py:607
  66.5 2.4 %all-to-all-done.4 = f32[8,64,128]{2,1,0:T(8,128)S(1)} async-done(((f32[8,64,128]{2,1,0:T(8,128)}), f32[8,64,128]{2,1,0:T(8,128)S(1)}, u32[]{:S(2)}, u32[]{:S(2)}) %all-to-all-start.4) | async-done | bytes 262176 | tf_op jit(solution)/shard_map/all_to_all | solution.py:541
  68.9 1.1 shard_map.106
  70.0 3.1 %collective-permute-start.10 = (f32[8,1024]{1,0:T(8,128)S(1)}, f32[8,1024]{1,0:T(8,128)S(1)}, u32[]{:S(2)}, u32[]{:S(2)}) collective-permute-start(f32[8,1024]{1,0:T(8,128)S(1)} %get-tuple-element.95.s_here), channel_id=1, source_target_pairs={{0,1},{1,0},{2,3},{3,2},{4,5},{5,4},{6,7},{7,6},{8,9},{9,8},{10,11... | collective-permute-start | bytes 98312 | tf_op jit(solution)/shard_map/ppermute | solution.py:538
  73.1 1.0 shard_map.107
  74.1 0.1 collective-permute-start.9
  74.2 1.0 shard_map.108.before
  75.2 0.1 collective-permute-done.9.s_there
  75.4 2.0 %shard_map.109 = (f32[768,128]{1,0:T(8,128)}, f32[64,128]{1,0:T(8,128)S(1)}, f32[64,128]{1,0:T(8,128)S(1)}, f32[64,128]{1,0:T(8,128)S(1)}, f32[64,128]{1,0:T(8,128)S(1)}) custom-call(f32[128,1024]{1,0:T(8,128)S(1)} %get-tuple-element.93.z_ref, f32[128,1024]{1,0:T(8,128)S(1)} %get-tuple-element.94.w_ref, f32[8,1024]{1,0:T(8,128)S(1)} %get-tuple-element.95.s_here, ...), custom_call_target="tpu_custom_call" | custom-call | bytes 1000 | tf_op jit(solution)/shard_map/pallas_call | solution.py:594
  77.3 3.6 %all-to-all-start.5 = ((f32[8,96,128]{2,1,0:T(8,128)}), f32[8,96,128]{2,1,0:T(8,128)S(1)}, u32[]{:S(2)}, u32[]{:S(2)}) async-start(f32[8,96,128]{2,1,0:T(8,128)} %bitcast.15), calls=%async_computation.5 | async-start | bytes 786432 | tf_op jit(solution)/shard_map/all_to_all | solution.py:541
  80.9 1.3 collective-permute-start.11
  82.2 2.6 %collective-permute-start.12 = (f32[64,128]{1,0:T(8,128)S(1)}, f32[64,128]{1,0:T(8,128)S(1)}, u32[]{:S(2)}, u32[]{:S(2)}) collective-permute-start(f32[64,128]{1,0:T(8,128)S(1)} %get-tuple-element.105), channel_id=1, source_target_pairs={{0,32},{16,48},{32,0},{48,16},{64,96},{80,112},{96,64},{112,80},{1... | collective-permute-start | bytes 98312 | tf_op jit(solution)/shard_map/ppermute | solution.py:607
  84.9 1.6 %collective-permute-done.12.part_2 = f32[64,128]{1,0:T(8,128)S(1)} collective-permute-done((f32[64,128]{1,0:T(8,128)S(1)}, f32[64,128]{1,0:T(8,128)S(1)}, u32[]{:S(2)}, u32[]{:S(2)}) %collective-permute-start.12) | collective-permute-done | bytes 32800 | tf_op jit(solution)/shard_map/ppermute | solution.py:607
  86.5 2.6 %collective-permute-done.13.part_3 = f32[64,128]{1,0:T(8,128)S(1)} collective-permute-done((f32[64,128]{1,0:T(8,128)S(1)}, f32[64,128]{1,0:T(8,128)S(1)}, u32[]{:S(2)}, u32[]{:S(2)}) %collective-permute-start.13) | collective-permute-done | bytes 32800 | tf_op jit(solution)/shard_map/ppermute | solution.py:607
  89.1 0.1 shard_map.110
  89.2 10.4 %all_to_all.102 = f32[8,64,128]{2,1,0:T(8,128)S(1)} all-to-all(f32[8,64,128]{2,1,0:T(8,128)S(1)} %bitcast.46), channel_id=1, replica_groups=mesh['chan'=8,'st'=8,'core'=2] {'st'}, dimensions={0} | all-to-all | bytes 524288 | tf_op jit(solution)/shard_map/all_to_all | solution.py:541
  99.6 1.1 shard_map.111
  100.7 3.9 %collective-permute-start.15 = (f32[8,1024]{1,0:T(8,128)S(1)}, f32[8,1024]{1,0:T(8,128)S(1)}, u32[]{:S(2)}, u32[]{:S(2)}) collective-permute-start(f32[8,1024]{1,0:T(8,128)S(1)} %get-tuple-element.110.s_here), channel_id=1, source_target_pairs={{0,1},{1,0},{2,3},{3,2},{4,5},{5,4},{6,7},{7,6},{8,9},{9,8},{10,11... | collective-permute-start | bytes 98312 | tf_op jit(solution)/shard_map/ppermute | solution.py:538
  104.6 1.0 shard_map.112
  105.6 0.3 collective-permute-start.14
  106.0 1.1 shard_map.113.before
  107.0 0.1 collective-permute-done.14.s_there
  107.2 1.2 shard_map.114
  108.4 10.2 %all_to_all.103 = f32[8,96,128]{2,1,0:T(8,128)S(1)} all-to-all(f32[8,96,128]{2,1,0:T(8,128)S(1)} %bitcast.29), channel_id=1, replica_groups=mesh['chan'=8,'st'=8,'core'=2] {'st'}, dimensions={0} | all-to-all | bytes 786432 | tf_op jit(solution)/shard_map/all_to_all | solution.py:541
  118.5 0.2 shard_map.115
  118.7 2.0 %collective-permute-start.16 = (f32[1024,128]{1,0:T(8,128)S(1)}, f32[1024,128]{1,0:T(8,128)S(1)}, u32[]{:S(2)}, u32[]{:S(2)}) collective-permute-start(f32[1024,128]{1,0:T(8,128)S(1)} %get-tuple-element.120), channel_id=1, source_target_pairs={{0,1},{1,0},{2,3},{3,2},{4,5},{5,4},{6,7},{7,6},{8,9},{9,8},{10,11... | collective-permute-start | bytes 1572872 | tf_op jit(solution)/shard_map/ppermute | solution.py:538
  120.7 13.2 %all_to_all.104 = f32[16,32,128]{2,1,0:T(8,128)S(1)} all-to-all(f32[16,32,128]{2,1,0:T(8,128)S(1)} %bitcast.45), channel_id=1, replica_groups=mesh['chan'=8,'st'=8,'core'=2] {'chan','core'}, dimensions={0} | all-to-all | bytes 524288 | tf_op jit(solution)/shard_map/all_to_all | solution.py:541
  133.8 1.3 shard_map.116
  (22 shorter events, 0.1 us)
Async XLA Ops:
  0.6 9.1 %copy-start.1 = (bf16[1,32,8,1024]{3,2,1,0:T(8,128)(2,1)S(1)}, bf16[1,32,8,1024]{3,2,1,0:T(8,128)(2,1)}, u32[]{:S(2)}) copy-start(bf16[1,32,8,1024]{3,2,1,0:T(8,128)(2,1)} %param.7) | copy-start | bytes 1572868
  0.6 1.0 copy-start.4
  1.6 8.1 %copy-start.7 = (f32[32]{0:T(128)S(1)}, f32[32]{0:T(128)}, u32[]{:S(2)}) copy-start(f32[32]{0:T(128)} %param.13) | copy-start | bytes 388
  2.4 7.3 %copy-start = (s32[2,1024]{1,0:T(2,128)S(1)}, s32[2,1024]{1,0:T(2,128)}, u32[]{:S(2)}) copy-start(s32[2,1024]{1,0:T(2,128)} %pairs.17) | copy-start | bytes 24580
  2.4 7.3 %copy-start.5 = (f32[1,32,8,32]{3,2,1,0:T(8,128)S(1)}, f32[1,32,8,32]{3,2,1,0:T(8,128)}, u32[]{:S(2)}) copy-start(f32[1,32,8,32]{3,2,1,0:T(8,128)} %param.10) | copy-start | bytes 98308
  2.4 14.7 %all-to-all-start = ((f32[16,32,128]{2,1,0:T(8,128)}), f32[16,32,128]{2,1,0:T(8,128)S(1)}, u32[]{:S(2)}, u32[]{:S(2)}) async-start(f32[16,32,128]{2,1,0:T(8,128)} %bitcast.1), calls=%async_computation | async-start | bytes 524288 | tf_op jit(solution)/shard_map/all_to_all | solution.py:541
  9.8 1.0 copy-start.2
  10.8 0.9 copy-start.6
  11.7 5.4 %copy-start.3 = (f32[1,8,1024]{2,1,0:T(8,128)S(1)}, f32[1,8,1024]{2,1,0:T(8,128)}, u32[]{:S(2)}) copy-start(f32[1,8,1024]{2,1,0:T(8,128)} %param.8) | copy-start | bytes 98308
  13.4 5.4 %collective-permute-start = (f32[40,1024]{1,0:T(8,128)S(1)}, f32[40,1024]{1,0:T(8,128)S(1)}, u32[]{:S(2)}, u32[]{:S(2)}) collective-permute-start(f32[40,1024]{1,0:T(8,128)S(1)} %get-tuple-element.71), channel_id=1, source_target_pairs={{0,1},{1,0},{2,3},{3,2},{4,5},{5,4},{6,7},{7,6},{8,9},{9,8},{10,11... | collective-permute-start | bytes 491528 | tf_op jit(solution)/shard_map/ppermute | solution.py:538
  13.6 5.3 %collective-permute-start.1 = (f32[40,1024]{1,0:T(8,128)S(1)}, f32[40,1024]{1,0:T(8,128)S(1)}, u32[]{:S(2)}, u32[]{:S(2)}) collective-permute-start(f32[40,1024]{1,0:T(8,128)S(1)} %get-tuple-element.72), channel_id=1, source_target_pairs={{0,1},{1,0},{2,3},{3,2},{4,5},{5,4},{6,7},{7,6},{8,9},{9,8},{10,11... | collective-permute-start | bytes 491528 | tf_op jit(solution)/shard_map/ppermute | solution.py:538
  14.0 4.9 %collective-permute-start.2 = (f32[40,1024]{1,0:T(8,128)S(1)}, f32[40,1024]{1,0:T(8,128)S(1)}, u32[]{:S(2)}, u32[]{:S(2)}) collective-permute-start(f32[40,1024]{1,0:T(8,128)S(1)} %get-tuple-element.73), channel_id=1, source_target_pairs={{0,1},{1,0},{2,3},{3,2},{4,5},{5,4},{6,7},{7,6},{8,9},{9,8},{10,11... | collective-permute-start | bytes 491528 | tf_op jit(solution)/shard_map/ppermute | solution.py:538
  14.1 4.8 %collective-permute-start.3 = (f32[40,1024]{1,0:T(8,128)S(1)}, f32[40,1024]{1,0:T(8,128)S(1)}, u32[]{:S(2)}, u32[]{:S(2)}) collective-permute-start(f32[40,1024]{1,0:T(8,128)S(1)} %get-tuple-element.74), channel_id=1, source_target_pairs={{0,1},{1,0},{2,3},{3,2},{4,5},{5,4},{6,7},{7,6},{8,9},{9,8},{10,11... | collective-permute-start | bytes 491528 | tf_op jit(solution)/shard_map/ppermute | solution.py:538
  18.4 1.7 %collective-permute-start.5 = (f32[8,1024]{1,0:T(8,128)S(1)}, f32[8,1024]{1,0:T(8,128)S(1)}, u32[]{:S(2)}, u32[]{:S(2)}) collective-permute-start(f32[8,1024]{1,0:T(8,128)S(1)} %get-tuple-element.69.s_here), channel_id=1, source_target_pairs={{0,1},{1,0},{2,3},{3,2},{4,5},{5,4},{6,7},{7,6},{8,9},{9,8},{10,11... | collective-permute-start | bytes 98312 | tf_op jit(solution)/shard_map/ppermute | solution.py:538
  19.9 1.3 collective-permute-start.4
  42.2 4.1 %collective-permute-start.7 = (f32[8,1024]{1,0:T(8,128)S(1)}, f32[8,1024]{1,0:T(8,128)S(1)}, u32[]{:S(2)}, u32[]{:S(2)}) collective-permute-start(f32[8,1024]{1,0:T(8,128)S(1)} %get-tuple-element.85.s_here), channel_id=1, source_target_pairs={{0,1},{1,0},{2,3},{3,2},{4,5},{5,4},{6,7},{7,6},{8,9},{9,8},{10,11... | collective-permute-start | bytes 98312 | tf_op jit(solution)/shard_map/ppermute | solution.py:538
  46.1 1.5 %collective-permute-start.6 = (f32[8,1024]{1,0:T(8,128)S(1)}, f32[8,1024]{1,0:T(8,128)S(1)}, u32[]{:S(2)}, u32[]{:S(2)}) collective-permute-start(f32[8,1024]{1,0:T(8,128)S(1)} %get-tuple-element.87.s_here), channel_id=1, source_target_pairs={{0,1},{1,0},{2,3},{3,2},{4,5},{5,4},{6,7},{7,6},{8,9},{9,8},{10,11... | collective-permute-start | bytes 98312 | tf_op jit(solution)/shard_map/ppermute | solution.py:538
  59.7 9.2 %all-to-all-start.4 = ((f32[8,64,128]{2,1,0:T(8,128)}), f32[8,64,128]{2,1,0:T(8,128)S(1)}, u32[]{:S(2)}, u32[]{:S(2)}) async-start(f32[8,64,128]{2,1,0:T(8,128)} %bitcast.13), calls=%async_computation.4 | async-start | bytes 524288 | tf_op jit(solution)/shard_map/all_to_all | solution.py:541
  63.1 9.9 %collective-permute-start.8 = (f32[64,128]{1,0:T(8,128)S(1)}, f32[64,128]{1,0:T(8,128)S(1)}, u32[]{:S(2)}, u32[]{:S(2)}) collective-permute-start(f32[64,128]{1,0:T(8,128)S(1)} %get-tuple-element.97.moment), channel_id=1, source_target_pairs={{0,64},{16,80},{32,96},{48,112},{64,0},{80,16},{96,32},{112,48},{1... | collective-permute-start | bytes 98312 | tf_op jit(solution)/shard_map/ppermute | solution.py:607
  70.0 4.2 %collective-permute-start.10 = (f32[8,1024]{1,0:T(8,128)S(1)}, f32[8,1024]{1,0:T(8,128)S(1)}, u32[]{:S(2)}, u32[]{:S(2)}) collective-permute-start(f32[8,1024]{1,0:T(8,128)S(1)} %get-tuple-element.95.s_here), channel_id=1, source_target_pairs={{0,1},{1,0},{2,3},{3,2},{4,5},{5,4},{6,7},{7,6},{8,9},{9,8},{10,11... | collective-permute-start | bytes 98312 | tf_op jit(solution)/shard_map/ppermute | solution.py:538
  74.1 1.3 collective-permute-start.9
  77.3 11.8 %all-to-all-start.5 = ((f32[8,96,128]{2,1,0:T(8,128)}), f32[8,96,128]{2,1,0:T(8,128)S(1)}, u32[]{:S(2)}, u32[]{:S(2)}) async-start(f32[8,96,128]{2,1,0:T(8,128)} %bitcast.15), calls=%async_computation.5 | async-start | bytes 786432 | tf_op jit(solution)/shard_map/all_to_all | solution.py:541
  80.9 3.9 %collective-permute-start.11 = (f32[64,128]{1,0:T(8,128)S(1)}, f32[64,128]{1,0:T(8,128)S(1)}, u32[]{:S(2)}, u32[]{:S(2)}) collective-permute-start(f32[64,128]{1,0:T(8,128)S(1)} %get-tuple-element.104), channel_id=1, source_target_pairs={{0,16},{16,0},{32,48},{48,32},{64,80},{80,64},{96,112},{112,96},{1... | collective-permute-start | bytes 98312 | tf_op jit(solution)/shard_map/ppermute | solution.py:607
  82.2 4.3 %collective-permute-start.12 = (f32[64,128]{1,0:T(8,128)S(1)}, f32[64,128]{1,0:T(8,128)S(1)}, u32[]{:S(2)}, u32[]{:S(2)}) collective-permute-start(f32[64,128]{1,0:T(8,128)S(1)} %get-tuple-element.105), channel_id=1, source_target_pairs={{0,32},{16,48},{32,0},{48,16},{64,96},{80,112},{96,64},{112,80},{1... | collective-permute-start | bytes 98312 | tf_op jit(solution)/shard_map/ppermute | solution.py:607
  84.9 4.3 %collective-permute-start.13 = (f32[64,128]{1,0:T(8,128)S(1)}, f32[64,128]{1,0:T(8,128)S(1)}, u32[]{:S(2)}, u32[]{:S(2)}) collective-permute-start(f32[64,128]{1,0:T(8,128)S(1)} %get-tuple-element.106), channel_id=1, source_target_pairs={{0,48},{16,32},{32,16},{48,0},{64,112},{80,96},{96,80},{112,64},{1... | collective-permute-start | bytes 98312 | tf_op jit(solution)/shard_map/ppermute | solution.py:607
  100.7 5.3 %collective-permute-start.15 = (f32[8,1024]{1,0:T(8,128)S(1)}, f32[8,1024]{1,0:T(8,128)S(1)}, u32[]{:S(2)}, u32[]{:S(2)}) collective-permute-start(f32[8,1024]{1,0:T(8,128)S(1)} %get-tuple-element.110.s_here), channel_id=1, source_target_pairs={{0,1},{1,0},{2,3},{3,2},{4,5},{5,4},{6,7},{7,6},{8,9},{9,8},{10,11... | collective-permute-start | bytes 98312 | tf_op jit(solution)/shard_map/ppermute | solution.py:538
  105.6 1.5 %collective-permute-start.14 = (f32[8,1024]{1,0:T(8,128)S(1)}, f32[8,1024]{1,0:T(8,128)S(1)}, u32[]{:S(2)}, u32[]{:S(2)}) collective-permute-start(f32[8,1024]{1,0:T(8,128)S(1)} %get-tuple-element.112.s_here), channel_id=1, source_target_pairs={{0,1},{1,0},{2,3},{3,2},{4,5},{5,4},{6,7},{7,6},{8,9},{9,8},{10,11... | collective-permute-start | bytes 98312 | tf_op jit(solution)/shard_map/ppermute | solution.py:538
  118.7 15.1 %collective-permute-start.16 = (f32[1024,128]{1,0:T(8,128)S(1)}, f32[1024,128]{1,0:T(8,128)S(1)}, u32[]{:S(2)}, u32[]{:S(2)}) collective-permute-start(f32[1024,128]{1,0:T(8,128)S(1)} %get-tuple-element.120), channel_id=1, source_target_pairs={{0,1},{1,0},{2,3},{3,2},{4,5},{5,4},{6,7},{7,6},{8,9},{9,8},{10,11... | collective-permute-start | bytes 1572872 | tf_op jit(solution)/shard_map/ppermute | solution.py:538

commit v8 on v7

--- a/solution.py
+++ b/solution.py
@@ -610,7 +610,7 @@
     parts, *messages = step_sums(
         *step_model(spread, moment_z), message_sums_kernel, [packed] * 4, (moment, moment_z)
     )
-    shares = [messages[0]] + [from_channel(messages[d], d) for d in (1, 2, 3)]
+    shares = [messages[0]] + [from_channel(messages[d], d) for d in (2, 1, 3)]
     gain, spread, dual, target = call(update_consensus_kernel, [packed, wide, packed, packed], n_in=8)(
         exchange(parts, "st"), gain, *shares, dual, rho_a
     )

time: 136 us -> 135 us (level)
  transfers between devices with their start and end apart: 20 -> 20, of which waited for: 7 -> 9; matrix products, arithmetic and copies ran while one was open for 0% -> 0% of each run, Pallas kernels for 9% -> 9%
where the time goes in v8:
time: 135 us
  blocking collectives  62.3 us (46%)
  starting transfers between devices  35.7 us (26%)
  Pallas kernels  23 us (17%)
  waiting for transfers between devices  9.75 us (7%)
  local copies, waits for them, and re-layouts  2.92 us (2%)
    all_to_all x6, blocking collectives, exchange(): return lax.all_to_all(x, axis, 0, 0, tiled=True)  62.3 us
    all_to_all x3, starting transfers between devices, exchange(): return lax.all_to_all(x, axis, 0, 0, tiled=True)  14.3 us
    ppermute x13, starting transfers between devices, swap(): return lax.ppermute(x, 'core', CORE_SWAP)  14.3 us
    ppermute x4, starting transfers between devices, from_channel(): return lax.ppermute(x, 'chan', [(f, f ^ distance) for f in range(CHANNELS)])  7.08 us
    pallas_call x4, Pallas kernels, step_sums(): call(kernel, [sums_out, *outs], [left, total, hot], n_in=6 + len(extra))  5.53 us
    all_to_all x3, waiting for transfers between devices, exchange(): return lax.all_to_all(x, axis, 0, 0, tiled=True)  5.42 us
    pallas_call x4, Pallas kernels, step_sums(): call(sums_other_kernel, [((384, STATIONS), F32)], [left, hot], n_in=5)  4.2 us
    ppermute x4, waiting for transfers between devices, from_channel(): return lax.ppermute(x, 'chan', [(f, f ^ distance) for f in range(CHANNELS)])  3.9 us
  transfers between devices with their start and end apart: 20, of which 9 were waited for; matrix products, arithmetic and copies ran while one was open for 0% of the time, Pallas kernels for 9%

profile of v8, /device:TPU:1, one launch (start us, length us, event | category | flops | bytes accessed | tf_op | source)
XLA Modules:
  0.0 134.8 jit_solution(1568446840343711775)
XLA Ops:
  0.6 0.0 copy-start.4
  0.7 1.0 copy-done.4
  1.6 0.8 shard_map.94
  2.4 7.3 %all-to-all-start = ((f32[16,32,128]{2,1,0:T(8,128)}), f32[16,32,128]{2,1,0:T(8,128)S(1)}, u32[]{:S(2)}, u32[]{:S(2)}) async-start(f32[16,32,128]{2,1,0:T(8,128)} %bitcast.1), calls=%async_computation | async-start | bytes 524288 | tf_op jit(solution)/shard_map/all_to_all | solution.py:541
  9.8 0.0 copy-start.2
  9.8 1.0 copy-done.2
  10.8 0.9 copy-done.6
  11.7 1.6 %shard_map.95 = (f32[128,1024]{1,0:T(8,128)S(1)}, f32[192,128]{1,0:T(8,128)S(1)}, f32[8,128]{1,0:T(8,128)S(1)}, f32[8,128]{1,0:T(8,128)S(1)}, f32[40,1024]{1,0:T...) custom-call(f32[8,128]{1,0:T(8,128)S(1)} %get-tuple-element.65.mark, ...), custom_call_target="tpu_custom_call" | custom-call | bytes 1000 | tf_op jit(solution)/shard_map/pallas_call | solution.py:552
  13.4 0.2 collective-permute-start
  13.6 0.4 collective-permute-start.1
  14.0 0.1 collective-permute-start.2
  14.1 0.4 collective-permute-start.3
  14.5 2.6 %all-to-all-done = f32[16,32,128]{2,1,0:T(8,128)S(1)} async-done(((f32[16,32,128]{2,1,0:T(8,128)}), f32[16,32,128]{2,1,0:T(8,128)S(1)}, u32[]{:S(2)}, u32[]{:S(2)}) %all-to-all-start) | async-done | bytes 262176 | tf_op jit(solution)/shard_map/all_to_all | solution.py:541
  17.1 1.2 shard_map.96
  18.4 0.5 collective-permute-start.5
  18.9 1.0 shard_map.97
  19.9 0.2 collective-permute-start.4
  20.1 1.1 shard_map.98.before
  21.1 0.0 collective-permute-done.4.s_there
  21.2 1.2 shard_map.99
  22.4 10.2 %all_to_all.99 = f32[8,96,128]{2,1,0:T(8,128)S(1)} all-to-all(f32[8,96,128]{2,1,0:T(8,128)S(1)} %bitcast.27), channel_id=1, replica_groups=mesh['chan'=8,'st'=8,'core'=2] {'st'}, dimensions={0} | all-to-all | bytes 786432 | tf_op jit(solution)/shard_map/all_to_all | solution.py:541
  32.6 0.1 shard_map.100
  32.6 8.5 %all_to_all.100 = f32[8,64,128]{2,1,0:T(8,128)S(1)} all-to-all(f32[8,64,128]{2,1,0:T(8,128)S(1)} %bitcast.47), channel_id=1, replica_groups=mesh['chan'=8,'st'=8,'core'=2] {'st'}, dimensions={0} | all-to-all | bytes 524288 | tf_op jit(solution)/shard_map/all_to_all | solution.py:541
  41.2 1.1 shard_map.101
  42.2 2.8 %collective-permute-start.7 = (f32[8,1024]{1,0:T(8,128)S(1)}, f32[8,1024]{1,0:T(8,128)S(1)}, u32[]{:S(2)}, u32[]{:S(2)}) collective-permute-start(f32[8,1024]{1,0:T(8,128)S(1)} %get-tuple-element.85.s_here), channel_id=1, source_target_pairs={{0,1},{1,0},{2,3},{3,2},{4,5},{5,4},{6,7},{7,6},{8,9},{9,8},{10,11... | collective-permute-start | bytes 98312 | tf_op jit(solution)/shard_map/ppermute | solution.py:538
  45.1 1.0 shard_map.102
  46.1 0.3 collective-permute-start.6
  46.4 1.0 shard_map.103.before
  47.4 0.1 collective-permute-done.6.s_there
  47.6 1.2 shard_map.104
  48.8 10.2 %all_to_all.101 = f32[8,96,128]{2,1,0:T(8,128)S(1)} all-to-all(f32[8,96,128]{2,1,0:T(8,128)S(1)} %bitcast.28), channel_id=1, replica_groups=mesh['chan'=8,'st'=8,'core'=2] {'st'}, dimensions={0} | all-to-all | bytes 786432 | tf_op jit(solution)/shard_map/all_to_all | solution.py:541
  59.0 0.8 shard_map.105
  59.7 3.4 %all-to-all-start.4 = ((f32[8,64,128]{2,1,0:T(8,128)}), f32[8,64,128]{2,1,0:T(8,128)S(1)}, u32[]{:S(2)}, u32[]{:S(2)}) async-start(f32[8,64,128]{2,1,0:T(8,128)} %bitcast.13), calls=%async_computation.4 | async-start | bytes 524288 | tf_op jit(solution)/shard_map/all_to_all | solution.py:541
  63.1 3.4 %collective-permute-start.8 = (f32[64,128]{1,0:T(8,128)S(1)}, f32[64,128]{1,0:T(8,128)S(1)}, u32[]{:S(2)}, u32[]{:S(2)}) collective-permute-start(f32[64,128]{1,0:T(8,128)S(1)} %get-tuple-element.97.moment), channel_id=1, source_target_pairs={{0,64},{16,80},{32,96},{48,112},{64,0},{80,16},{96,32},{112,48},{1... | collective-permute-start | bytes 98312 | tf_op jit(solution)/shard_map/ppermute | solution.py:607
  66.5 2.4 %all-to-all-done.4 = f32[8,64,128]{2,1,0:T(8,128)S(1)} async-done(((f32[8,64,128]{2,1,0:T(8,128)}), f32[8,64,128]{2,1,0:T(8,128)S(1)}, u32[]{:S(2)}, u32[]{:S(2)}) %all-to-all-start.4) | async-done | bytes 262176 | tf_op jit(solution)/shard_map/all_to_all | solution.py:541
  68.9 1.1 shard_map.106
  70.0 3.1 %collective-permute-start.10 = (f32[8,1024]{1,0:T(8,128)S(1)}, f32[8,1024]{1,0:T(8,128)S(1)}, u32[]{:S(2)}, u32[]{:S(2)}) collective-permute-start(f32[8,1024]{1,0:T(8,128)S(1)} %get-tuple-element.95.s_here), channel_id=1, source_target_pairs={{0,1},{1,0},{2,3},{3,2},{4,5},{5,4},{6,7},{7,6},{8,9},{9,8},{10,11... | collective-permute-start | bytes 98312 | tf_op jit(solution)/shard_map/ppermute | solution.py:538
  73.1 1.0 shard_map.107
  74.1 0.1 collective-permute-start.9
  74.2 1.0 shard_map.108.before
  75.2 0.1 collective-permute-done.9.s_there
  75.4 2.0 %shard_map.109 = (f32[768,128]{1,0:T(8,128)}, f32[64,128]{1,0:T(8,128)S(1)}, f32[64,128]{1,0:T(8,128)S(1)}, f32[64,128]{1,0:T(8,128)S(1)}, f32[64,128]{1,0:T(8,128)S(1)}) custom-call(f32[128,1024]{1,0:T(8,128)S(1)} %get-tuple-element.93.z_ref, f32[128,1024]{1,0:T(8,128)S(1)} %get-tuple-element.94.w_ref, f32[8,1024]{1,0:T(8,128)S(1)} %get-tuple-element.95.s_here, ...), custom_call_target="tpu_custom_call" | custom-call | bytes 1000 | tf_op jit(solution)/shard_map/pallas_call | solution.py:594
  77.3 3.6 %all-to-all-start.5 = ((f32[8,96,128]{2,1,0:T(8,128)}), f32[8,96,128]{2,1,0:T(8,128)S(1)}, u32[]{:S(2)}, u32[]{:S(2)}) async-start(f32[8,96,128]{2,1,0:T(8,128)} %bitcast.15), calls=%async_computation.5 | async-start | bytes 786432 | tf_op jit(solution)/shard_map/all_to_all | solution.py:541
  80.9 2.9 %collective-permute-start.11 = (f32[64,128]{1,0:T(8,128)S(1)}, f32[64,128]{1,0:T(8,128)S(1)}, u32[]{:S(2)}, u32[]{:S(2)}) collective-permute-start(f32[64,128]{1,0:T(8,128)S(1)} %get-tuple-element.104), channel_id=1, source_target_pairs={{0,32},{16,48},{32,0},{48,16},{64,96},{80,112},{96,64},{112,80},{1... | collective-permute-start | bytes 98312 | tf_op jit(solution)/shard_map/ppermute | solution.py:607
  83.9 0.4 collective-permute-start.12
  84.2 0.4 collective-permute-start.13
  84.6 0.6 collective-permute-done.11.part_1
  85.2 1.9 %collective-permute-done.12.part_2 = f32[64,128]{1,0:T(8,128)S(1)} collective-permute-done((f32[64,128]{1,0:T(8,128)S(1)}, f32[64,128]{1,0:T(8,128)S(1)}, u32[]{:S(2)}, u32[]{:S(2)}) %collective-permute-start.12) | collective-permute-done | bytes 32800 | tf_op jit(solution)/shard_map/ppermute | solution.py:607
  87.1 1.4 %collective-permute-done.13.part_3 = f32[64,128]{1,0:T(8,128)S(1)} collective-permute-done((f32[64,128]{1,0:T(8,128)S(1)}, f32[64,128]{1,0:T(8,128)S(1)}, u32[]{:S(2)}, u32[]{:S(2)}) %collective-permute-start.13) | collective-permute-done | bytes 32800 | tf_op jit(solution)/shard_map/ppermute | solution.py:607
  88.5 0.4 all-to-all-done.5
  88.9 0.1 shard_map.110
  89.0 10.0 %all_to_all.102 = f32[8,64,128]{2,1,0:T(8,128)S(1)} all-to-all(f32[8,64,128]{2,1,0:T(8,128)S(1)} %bitcast.46), channel_id=1, replica_groups=mesh['chan'=8,'st'=8,'core'=2] {'st'}, dimensions={0} | all-to-all | bytes 524288 | tf_op jit(solution)/shard_map/all_to_all | solution.py:541
  99.0 1.1 shard_map.111
  100.1 3.9 %collective-permute-start.15 = (f32[8,1024]{1,0:T(8,128)S(1)}, f32[8,1024]{1,0:T(8,128)S(1)}, u32[]{:S(2)}, u32[]{:S(2)}) collective-permute-start(f32[8,1024]{1,0:T(8,128)S(1)} %get-tuple-element.110.s_here), channel_id=1, source_target_pairs={{0,1},{1,0},{2,3},{3,2},{4,5},{5,4},{6,7},{7,6},{8,9},{9,8},{10,11... | collective-permute-start | bytes 98312 | tf_op jit(solution)/shard_map/ppermute | solution.py:538
  104.0 1.0 shard_map.112
  105.0 0.3 collective-permute-start.14
  105.4 1.0 shard_map.113.before
  106.4 0.1 collective-permute-done.14.s_there
  106.5 1.2 shard_map.114
  107.7 10.2 %all_to_all.103 = f32[8,96,128]{2,1,0:T(8,128)S(1)} all-to-all(f32[8,96,128]{2,1,0:T(8,128)S(1)} %bitcast.29), channel_id=1, replica_groups=mesh['chan'=8,'st'=8,'core'=2] {'st'}, dimensions={0} | all-to-all | bytes 786432 | tf_op jit(solution)/shard_map/all_to_all | solution.py:541
  117.9 0.2 shard_map.115
  118.1 1.9 %collective-permute-start.16 = (f32[1024,128]{1,0:T(8,128)S(1)}, f32[1024,128]{1,0:T(8,128)S(1)}, u32[]{:S(2)}, u32[]{:S(2)}) collective-permute-start(f32[1024,128]{1,0:T(8,128)S(1)} %get-tuple-element.120), channel_id=1, source_target_pairs={{0,1},{1,0},{2,3},{3,2},{4,5},{5,4},{6,7},{7,6},{8,9},{9,8},{10,11... | collective-permute-start | bytes 1572872 | tf_op jit(solution)/shard_map/ppermute | solution.py:538
  120.1 13.2 %all_to_all.104 = f32[16,32,128]{2,1,0:T(8,128)S(1)} all-to-all(f32[16,32,128]{2,1,0:T(8,128)S(1)} %bitcast.45), channel_id=1, replica_groups=mesh['chan'=8,'st'=8,'core'=2] {'chan','core'}, dimensions={0} | all-to-all | bytes 524288 | tf_op jit(solution)/shard_map/all_to_all | solution.py:541
  133.3 1.3 shard_map.116
  (22 shorter events, 0.1 us)
Async XLA Ops:
  0.6 9.1 %copy-start.1 = (bf16[1,32,8,1024]{3,2,1,0:T(8,128)(2,1)S(1)}, bf16[1,32,8,1024]{3,2,1,0:T(8,128)(2,1)}, u32[]{:S(2)}) copy-start(bf16[1,32,8,1024]{3,2,1,0:T(8,128)(2,1)} %param.7) | copy-start | bytes 1572868
  0.6 1.0 copy-start.4
  1.6 8.1 %copy-start.7 = (f32[32]{0:T(128)S(1)}, f32[32]{0:T(128)}, u32[]{:S(2)}) copy-start(f32[32]{0:T(128)} %param.13) | copy-start | bytes 388
  2.4 7.3 %copy-start = (s32[2,1024]{1,0:T(2,128)S(1)}, s32[2,1024]{1,0:T(2,128)}, u32[]{:S(2)}) copy-start(s32[2,1024]{1,0:T(2,128)} %pairs.17) | copy-start | bytes 24580
  2.4 7.3 %copy-start.5 = (f32[1,32,8,32]{3,2,1,0:T(8,128)S(1)}, f32[1,32,8,32]{3,2,1,0:T(8,128)}, u32[]{:S(2)}) copy-start(f32[1,32,8,32]{3,2,1,0:T(8,128)} %param.10) | copy-start | bytes 98308
  2.4 14.7 %all-to-all-start = ((f32[16,32,128]{2,1,0:T(8,128)}), f32[16,32,128]{2,1,0:T(8,128)S(1)}, u32[]{:S(2)}, u32[]{:S(2)}) async-start(f32[16,32,128]{2,1,0:T(8,128)} %bitcast.1), calls=%async_computation | async-start | bytes 524288 | tf_op jit(solution)/shard_map/all_to_all | solution.py:541
  9.8 1.0 copy-start.2
  10.8 0.9 copy-start.6
  11.7 5.4 %copy-start.3 = (f32[1,8,1024]{2,1,0:T(8,128)S(1)}, f32[1,8,1024]{2,1,0:T(8,128)}, u32[]{:S(2)}) copy-start(f32[1,8,1024]{2,1,0:T(8,128)} %param.8) | copy-start | bytes 98308
  13.4 5.4 %collective-permute-start = (f32[40,1024]{1,0:T(8,128)S(1)}, f32[40,1024]{1,0:T(8,128)S(1)}, u32[]{:S(2)}, u32[]{:S(2)}) collective-permute-start(f32[40,1024]{1,0:T(8,128)S(1)} %get-tuple-element.71), channel_id=1, source_target_pairs={{0,1},{1,0},{2,3},{3,2},{4,5},{5,4},{6,7},{7,6},{8,9},{9,8},{10,11... | collective-permute-start | bytes 491528 | tf_op jit(solution)/shard_map/ppermute | solution.py:538
  13.6 5.3 %collective-permute-start.1 = (f32[40,1024]{1,0:T(8,128)S(1)}, f32[40,1024]{1,0:T(8,128)S(1)}, u32[]{:S(2)}, u32[]{:S(2)}) collective-permute-start(f32[40,1024]{1,0:T(8,128)S(1)} %get-tuple-element.72), channel_id=1, source_target_pairs={{0,1},{1,0},{2,3},{3,2},{4,5},{5,4},{6,7},{7,6},{8,9},{9,8},{10,11... | collective-permute-start | bytes 491528 | tf_op jit(solution)/shard_map/ppermute | solution.py:538
  14.0 4.9 %collective-permute-start.2 = (f32[40,1024]{1,0:T(8,128)S(1)}, f32[40,1024]{1,0:T(8,128)S(1)}, u32[]{:S(2)}, u32[]{:S(2)}) collective-permute-start(f32[40,1024]{1,0:T(8,128)S(1)} %get-tuple-element.73), channel_id=1, source_target_pairs={{0,1},{1,0},{2,3},{3,2},{4,5},{5,4},{6,7},{7,6},{8,9},{9,8},{10,11... | collective-permute-start | bytes 491528 | tf_op jit(solution)/shard_map/ppermute | solution.py:538
  14.1 4.8 %collective-permute-start.3 = (f32[40,1024]{1,0:T(8,128)S(1)}, f32[40,1024]{1,0:T(8,128)S(1)}, u32[]{:S(2)}, u32[]{:S(2)}) collective-permute-start(f32[40,1024]{1,0:T(8,128)S(1)} %get-tuple-element.74), channel_id=1, source_target_pairs={{0,1},{1,0},{2,3},{3,2},{4,5},{5,4},{6,7},{7,6},{8,9},{9,8},{10,11... | collective-permute-start | bytes 491528 | tf_op jit(solution)/shard_map/ppermute | solution.py:538
  18.4 1.7 %collective-permute-start.5 = (f32[8,1024]{1,0:T(8,128)S(1)}, f32[8,1024]{1,0:T(8,128)S(1)}, u32[]{:S(2)}, u32[]{:S(2)}) collective-permute-start(f32[8,1024]{1,0:T(8,128)S(1)} %get-tuple-element.69.s_here), channel_id=1, source_target_pairs={{0,1},{1,0},{2,3},{3,2},{4,5},{5,4},{6,7},{7,6},{8,9},{9,8},{10,11... | collective-permute-start | bytes 98312 | tf_op jit(solution)/shard_map/ppermute | solution.py:538
  19.9 1.3 collective-permute-start.4
  42.2 4.1 %collective-permute-start.7 = (f32[8,1024]{1,0:T(8,128)S(1)}, f32[8,1024]{1,0:T(8,128)S(1)}, u32[]{:S(2)}, u32[]{:S(2)}) collective-permute-start(f32[8,1024]{1,0:T(8,128)S(1)} %get-tuple-element.85.s_here), channel_id=1, source_target_pairs={{0,1},{1,0},{2,3},{3,2},{4,5},{5,4},{6,7},{7,6},{8,9},{9,8},{10,11... | collective-permute-start | bytes 98312 | tf_op jit(solution)/shard_map/ppermute | solution.py:538
  46.1 1.5 %collective-permute-start.6 = (f32[8,1024]{1,0:T(8,128)S(1)}, f32[8,1024]{1,0:T(8,128)S(1)}, u32[]{:S(2)}, u32[]{:S(2)}) collective-permute-start(f32[8,1024]{1,0:T(8,128)S(1)} %get-tuple-element.87.s_here), channel_id=1, source_target_pairs={{0,1},{1,0},{2,3},{3,2},{4,5},{5,4},{6,7},{7,6},{8,9},{9,8},{10,11... | collective-permute-start | bytes 98312 | tf_op jit(solution)/shard_map/ppermute | solution.py:538
  59.7 9.2 %all-to-all-start.4 = ((f32[8,64,128]{2,1,0:T(8,128)}), f32[8,64,128]{2,1,0:T(8,128)S(1)}, u32[]{:S(2)}, u32[]{:S(2)}) async-start(f32[8,64,128]{2,1,0:T(8,128)} %bitcast.13), calls=%async_computation.4 | async-start | bytes 524288 | tf_op jit(solution)/shard_map/all_to_all | solution.py:541
  63.1 9.9 %collective-permute-start.8 = (f32[64,128]{1,0:T(8,128)S(1)}, f32[64,128]{1,0:T(8,128)S(1)}, u32[]{:S(2)}, u32[]{:S(2)}) collective-permute-start(f32[64,128]{1,0:T(8,128)S(1)} %get-tuple-element.97.moment), channel_id=1, source_target_pairs={{0,64},{16,80},{32,96},{48,112},{64,0},{80,16},{96,32},{112,48},{1... | collective-permute-start | bytes 98312 | tf_op jit(solution)/shard_map/ppermute | solution.py:607
  70.0 4.2 %collective-permute-start.10 = (f32[8,1024]{1,0:T(8,128)S(1)}, f32[8,1024]{1,0:T(8,128)S(1)}, u32[]{:S(2)}, u32[]{:S(2)}) collective-permute-start(f32[8,1024]{1,0:T(8,128)S(1)} %get-tuple-element.95.s_here), channel_id=1, source_target_pairs={{0,1},{1,0},{2,3},{3,2},{4,5},{5,4},{6,7},{7,6},{8,9},{9,8},{10,11... | collective-permute-start | bytes 98312 | tf_op jit(solution)/shard_map/ppermute | solution.py:538
  74.1 1.3 collective-permute-start.9
  77.3 11.6 %all-to-all-start.5 = ((f32[8,96,128]{2,1,0:T(8,128)}), f32[8,96,128]{2,1,0:T(8,128)S(1)}, u32[]{:S(2)}, u32[]{:S(2)}) async-start(f32[8,96,128]{2,1,0:T(8,128)} %bitcast.15), calls=%async_computation.5 | async-start | bytes 786432 | tf_op jit(solution)/shard_map/all_to_all | solution.py:541
  80.9 4.3 %collective-permute-start.11 = (f32[64,128]{1,0:T(8,128)S(1)}, f32[64,128]{1,0:T(8,128)S(1)}, u32[]{:S(2)}, u32[]{:S(2)}) collective-permute-start(f32[64,128]{1,0:T(8,128)S(1)} %get-tuple-element.104), channel_id=1, source_target_pairs={{0,32},{16,48},{32,0},{48,16},{64,96},{80,112},{96,64},{112,80},{1... | collective-permute-start | bytes 98312 | tf_op jit(solution)/shard_map/ppermute | solution.py:607
  83.9 3.2 %collective-permute-start.12 = (f32[64,128]{1,0:T(8,128)S(1)}, f32[64,128]{1,0:T(8,128)S(1)}, u32[]{:S(2)}, u32[]{:S(2)}) collective-permute-start(f32[64,128]{1,0:T(8,128)S(1)} %get-tuple-element.105), channel_id=1, source_target_pairs={{0,16},{16,0},{32,48},{48,32},{64,80},{80,64},{96,112},{112,96},{1... | collective-permute-start | bytes 98312 | tf_op jit(solution)/shard_map/ppermute | solution.py:607
  84.2 4.3 %collective-permute-start.13 = (f32[64,128]{1,0:T(8,128)S(1)}, f32[64,128]{1,0:T(8,128)S(1)}, u32[]{:S(2)}, u32[]{:S(2)}) collective-permute-start(f32[64,128]{1,0:T(8,128)S(1)} %get-tuple-element.106), channel_id=1, source_target_pairs={{0,48},{16,32},{32,16},{48,0},{64,112},{80,96},{96,80},{112,64},{1... | collective-permute-start | bytes 98312 | tf_op jit(solution)/shard_map/ppermute | solution.py:607
  100.1 5.3 %collective-permute-start.15 = (f32[8,1024]{1,0:T(8,128)S(1)}, f32[8,1024]{1,0:T(8,128)S(1)}, u32[]{:S(2)}, u32[]{:S(2)}) collective-permute-start(f32[8,1024]{1,0:T(8,128)S(1)} %get-tuple-element.110.s_here), channel_id=1, source_target_pairs={{0,1},{1,0},{2,3},{3,2},{4,5},{5,4},{6,7},{7,6},{8,9},{9,8},{10,11... | collective-permute-start | bytes 98312 | tf_op jit(solution)/shard_map/ppermute | solution.py:538
  105.0 1.5 %collective-permute-start.14 = (f32[8,1024]{1,0:T(8,128)S(1)}, f32[8,1024]{1,0:T(8,128)S(1)}, u32[]{:S(2)}, u32[]{:S(2)}) collective-permute-start(f32[8,1024]{1,0:T(8,128)S(1)} %get-tuple-element.112.s_here), channel_id=1, source_target_pairs={{0,1},{1,0},{2,3},{3,2},{4,5},{5,4},{6,7},{7,6},{8,9},{9,8},{10,11... | collective-permute-start | bytes 98312 | tf_op jit(solution)/shard_map/ppermute | solution.py:538
  118.1 15.2 %collective-permute-start.16 = (f32[1024,128]{1,0:T(8,128)S(1)}, f32[1024,128]{1,0:T(8,128)S(1)}, u32[]{:S(2)}, u32[]{:S(2)}) collective-permute-start(f32[1024,128]{1,0:T(8,128)S(1)} %get-tuple-element.120), channel_id=1, source_target_pairs={{0,1},{1,0},{2,3},{3,2},{4,5},{5,4},{6,7},{7,6},{8,9},{9,8},{10,11... | collective-permute-start | bytes 1572872 | tf_op jit(solution)/shard_map/ppermute | solution.py:538

commit v9 on v8

--- a/solution.py
+++ b/solution.py
@@ -610,7 +610,7 @@
     parts, *messages = step_sums(
         *step_model(spread, moment_z), message_sums_kernel, [packed] * 4, (moment, moment_z)
     )
-    shares = [messages[0]] + [from_channel(messages[d], d) for d in (2, 1, 3)]
+    shares = [messages[0]] + [from_channel(messages[d], d) for d in (2, 3, 1)]
     gain, spread, dual, target = call(update_consensus_kernel, [packed, wide, packed, packed], n_in=8)(
         exchange(parts, "st"), gain, *shares, dual, rho_a
     )

time: 135 us -> 136 us (level)
  transfers between devices with their start and end apart: 20 -> 20, of which waited for: 9 -> 8; matrix products, arithmetic and copies ran while one was open for 0% -> 0% of each run, Pallas kernels for 9% -> 9%
where the time goes in v9:
time: 136 us
  blocking collectives  63.4 us (47%)
  starting transfers between devices  35.4 us (26%)
  Pallas kernels  23 us (17%)
  waiting for transfers between devices  9.75 us (7%)
  local copies, waits for them, and re-layouts  2.92 us (2%)
    all_to_all x6, blocking collectives, exchange(): return lax.all_to_all(x, axis, 0, 0, tiled=True)  63.4 us
    all_to_all x3, starting transfers between devices, exchange(): return lax.all_to_all(x, axis, 0, 0, tiled=True)  14.3 us
    ppermute x13, starting transfers between devices, swap(): return lax.ppermute(x, 'core', CORE_SWAP)  14 us
    ppermute x4, starting transfers between devices, from_channel(): return lax.ppermute(x, 'chan', [(f, f ^ distance) for f in range(CHANNELS)])  7.08 us
    all_to_all x3, waiting for transfers between devices, exchange(): return lax.all_to_all(x, axis, 0, 0, tiled=True)  5.81 us
    pallas_call x4, Pallas kernels, step_sums(): call(kernel, [sums_out, *outs], [left, total, hot], n_in=6 + len(extra))  5.53 us
    pallas_call x4, Pallas kernels, step_sums(): call(sums_other_kernel, [((384, STATIONS), F32)], [left, hot], n_in=5)  4.2 us
    ppermute x4, waiting for transfers between devices, from_channel(): return lax.ppermute(x, 'chan', [(f, f ^ distance) for f in range(CHANNELS)])  3.5 us
  transfers between devices with their start and end apart: 20, of which 8 were waited for; matrix products, arithmetic and copies ran while one was open for 0% of the time, Pallas kernels for 9%

profile of v9, /device:TPU:1, one launch (start us, length us, event | category | flops | bytes accessed | tf_op | source)
XLA Modules:
  0.0 135.5 jit_solution(16381543086045030838)
XLA Ops:
  0.6 0.0 copy-start.4
  0.7 1.0 copy-done.4
  1.6 0.8 shard_map.94
  2.4 7.3 %all-to-all-start = ((f32[16,32,128]{2,1,0:T(8,128)}), f32[16,32,128]{2,1,0:T(8,128)S(1)}, u32[]{:S(2)}, u32[]{:S(2)}) async-start(f32[16,32,128]{2,1,0:T(8,128)} %bitcast.1), calls=%async_computation | async-start | bytes 524288 | tf_op jit(solution)/shard_map/all_to_all | solution.py:541
  9.8 0.0 copy-start.2
  9.8 1.0 copy-done.2
  10.8 0.9 copy-done.6
  11.7 1.6 %shard_map.95 = (f32[128,1024]{1,0:T(8,128)S(1)}, f32[192,128]{1,0:T(8,128)S(1)}, f32[8,128]{1,0:T(8,128)S(1)}, f32[8,128]{1,0:T(8,128)S(1)}, f32[40,1024]{1,0:T...) custom-call(f32[8,128]{1,0:T(8,128)S(1)} %get-tuple-element.65.mark, ...), custom_call_target="tpu_custom_call" | custom-call | bytes 1000 | tf_op jit(solution)/shard_map/pallas_call | solution.py:552
  13.4 0.2 collective-permute-start
  13.6 0.4 collective-permute-start.1
  14.0 0.1 collective-permute-start.2
  14.1 0.4 collective-permute-start.3
  14.5 2.6 %all-to-all-done = f32[16,32,128]{2,1,0:T(8,128)S(1)} async-done(((f32[16,32,128]{2,1,0:T(8,128)}), f32[16,32,128]{2,1,0:T(8,128)S(1)}, u32[]{:S(2)}, u32[]{:S(2)}) %all-to-all-start) | async-done | bytes 262176 | tf_op jit(solution)/shard_map/all_to_all | solution.py:541
  17.1 1.2 shard_map.96
  18.4 0.5 collective-permute-start.5
  18.8 0.0 collective-permute-done.recv_0
  18.8 0.0 collective-permute-done.1.recv_1
  18.9 1.0 shard_map.97
  19.9 0.2 collective-permute-start.4
  20.1 1.1 shard_map.98.before
  21.1 0.0 collective-permute-done.4.s_there
  21.2 1.2 shard_map.99
  22.4 10.2 %all_to_all.99 = f32[8,96,128]{2,1,0:T(8,128)S(1)} all-to-all(f32[8,96,128]{2,1,0:T(8,128)S(1)} %bitcast.27), channel_id=1, replica_groups=mesh['chan'=8,'st'=8,'core'=2] {'st'}, dimensions={0} | all-to-all | bytes 786432 | tf_op jit(solution)/shard_map/all_to_all | solution.py:541
  32.6 0.1 shard_map.100
  32.6 8.5 %all_to_all.100 = f32[8,64,128]{2,1,0:T(8,128)S(1)} all-to-all(f32[8,64,128]{2,1,0:T(8,128)S(1)} %bitcast.47), channel_id=1, replica_groups=mesh['chan'=8,'st'=8,'core'=2] {'st'}, dimensions={0} | all-to-all | bytes 524288 | tf_op jit(solution)/shard_map/all_to_all | solution.py:541
  41.2 1.1 shard_map.101
  42.2 2.8 %collective-permute-start.7 = (f32[8,1024]{1,0:T(8,128)S(1)}, f32[8,1024]{1,0:T(8,128)S(1)}, u32[]{:S(2)}, u32[]{:S(2)}) collective-permute-start(f32[8,1024]{1,0:T(8,128)S(1)} %get-tuple-element.85.s_here), channel_id=1, source_target_pairs={{0,1},{1,0},{2,3},{3,2},{4,5},{5,4},{6,7},{7,6},{8,9},{9,8},{10,11... | collective-permute-start | bytes 98312 | tf_op jit(solution)/shard_map/ppermute | solution.py:538
  45.1 1.0 shard_map.102
  46.1 0.3 collective-permute-start.6
  46.4 1.0 shard_map.103.before
  47.4 0.1 collective-permute-done.6.s_there
  47.6 1.2 shard_map.104
  48.8 10.2 %all_to_all.101 = f32[8,96,128]{2,1,0:T(8,128)S(1)} all-to-all(f32[8,96,128]{2,1,0:T(8,128)S(1)} %bitcast.28), channel_id=1, replica_groups=mesh['chan'=8,'st'=8,'core'=2] {'st'}, dimensions={0} | all-to-all | bytes 786432 | tf_op jit(solution)/shard_map/all_to_all | solution.py:541
  59.0 0.8 shard_map.105
  59.7 3.4 %all-to-all-start.4 = ((f32[8,64,128]{2,1,0:T(8,128)}), f32[8,64,128]{2,1,0:T(8,128)S(1)}, u32[]{:S(2)}, u32[]{:S(2)}) async-start(f32[8,64,128]{2,1,0:T(8,128)} %bitcast.13), calls=%async_computation.4 | async-start | bytes 524288 | tf_op jit(solution)/shard_map/all_to_all | solution.py:541
  63.1 3.4 %collective-permute-start.8 = (f32[64,128]{1,0:T(8,128)S(1)}, f32[64,128]{1,0:T(8,128)S(1)}, u32[]{:S(2)}, u32[]{:S(2)}) collective-permute-start(f32[64,128]{1,0:T(8,128)S(1)} %get-tuple-element.97.moment), channel_id=1, source_target_pairs={{0,64},{16,80},{32,96},{48,112},{64,0},{80,16},{96,32},{112,48},{1... | collective-permute-start | bytes 98312 | tf_op jit(solution)/shard_map/ppermute | solution.py:607
  66.5 2.4 %all-to-all-done.4 = f32[8,64,128]{2,1,0:T(8,128)S(1)} async-done(((f32[8,64,128]{2,1,0:T(8,128)}), f32[8,64,128]{2,1,0:T(8,128)S(1)}, u32[]{:S(2)}, u32[]{:S(2)}) %all-to-all-start.4) | async-done | bytes 262176 | tf_op jit(solution)/shard_map/all_to_all | solution.py:541
  68.9 1.1 shard_map.106
  70.0 3.1 %collective-permute-start.10 = (f32[8,1024]{1,0:T(8,128)S(1)}, f32[8,1024]{1,0:T(8,128)S(1)}, u32[]{:S(2)}, u32[]{:S(2)}) collective-permute-start(f32[8,1024]{1,0:T(8,128)S(1)} %get-tuple-element.95.s_here), channel_id=1, source_target_pairs={{0,1},{1,0},{2,3},{3,2},{4,5},{5,4},{6,7},{7,6},{8,9},{9,8},{10,11... | collective-permute-start | bytes 98312 | tf_op jit(solution)/shard_map/ppermute | solution.py:538
  73.1 1.0 shard_map.107
  74.1 0.1 collective-permute-start.9
  74.2 1.0 shard_map.108.before
  75.2 0.1 collective-permute-done.9.s_there
  75.4 2.0 %shard_map.109 = (f32[768,128]{1,0:T(8,128)}, f32[64,128]{1,0:T(8,128)S(1)}, f32[64,128]{1,0:T(8,128)S(1)}, f32[64,128]{1,0:T(8,128)S(1)}, f32[64,128]{1,0:T(8,128)S(1)}) custom-call(f32[128,1024]{1,0:T(8,128)S(1)} %get-tuple-element.93.z_ref, f32[128,1024]{1,0:T(8,128)S(1)} %get-tuple-element.94.w_ref, f32[8,1024]{1,0:T(8,128)S(1)} %get-tuple-element.95.s_here, ...), custom_call_target="tpu_custom_call" | custom-call | bytes 1000 | tf_op jit(solution)/shard_map/pallas_call | solution.py:594
  77.3 3.6 %all-to-all-start.5 = ((f32[8,96,128]{2,1,0:T(8,128)}), f32[8,96,128]{2,1,0:T(8,128)S(1)}, u32[]{:S(2)}, u32[]{:S(2)}) async-start(f32[8,96,128]{2,1,0:T(8,128)} %bitcast.15), calls=%async_computation.5 | async-start | bytes 786432 | tf_op jit(solution)/shard_map/all_to_all | solution.py:541
  80.9 2.9 %collective-permute-start.11 = (f32[64,128]{1,0:T(8,128)S(1)}, f32[64,128]{1,0:T(8,128)S(1)}, u32[]{:S(2)}, u32[]{:S(2)}) collective-permute-start(f32[64,128]{1,0:T(8,128)S(1)} %get-tuple-element.104), channel_id=1, source_target_pairs={{0,32},{16,48},{32,0},{48,16},{64,96},{80,112},{96,64},{112,80},{1... | collective-permute-start | bytes 98312 | tf_op jit(solution)/shard_map/ppermute | solution.py:607
  83.9 0.8 collective-permute-start.12
  84.6 0.6 collective-permute-done.11.part_1
  85.2 2.9 %collective-permute-done.12.part_2 = f32[64,128]{1,0:T(8,128)S(1)} collective-permute-done((f32[64,128]{1,0:T(8,128)S(1)}, f32[64,128]{1,0:T(8,128)S(1)}, u32[]{:S(2)}, u32[]{:S(2)}) %collective-permute-start.12) | collective-permute-done | bytes 32800 | tf_op jit(solution)/shard_map/ppermute | solution.py:607
  88.1 0.8 all-to-all-done.5
  88.9 0.1 shard_map.110
  89.0 9.7 %all_to_all.102 = f32[8,64,128]{2,1,0:T(8,128)S(1)} all-to-all(f32[8,64,128]{2,1,0:T(8,128)S(1)} %bitcast.46), channel_id=1, replica_groups=mesh['chan'=8,'st'=8,'core'=2] {'st'}, dimensions={0} | all-to-all | bytes 524288 | tf_op jit(solution)/shard_map/all_to_all | solution.py:541
  98.7 1.1 shard_map.111
  99.7 3.6 %collective-permute-start.15 = (f32[8,1024]{1,0:T(8,128)S(1)}, f32[8,1024]{1,0:T(8,128)S(1)}, u32[]{:S(2)}, u32[]{:S(2)}) collective-permute-start(f32[8,1024]{1,0:T(8,128)S(1)} %get-tuple-element.110.s_here), channel_id=1, source_target_pairs={{0,1},{1,0},{2,3},{3,2},{4,5},{5,4},{6,7},{7,6},{8,9},{9,8},{10,11... | collective-permute-start | bytes 98312 | tf_op jit(solution)/shard_map/ppermute | solution.py:538
  103.3 1.0 shard_map.112
  104.4 0.3 collective-permute-start.14
  104.7 1.0 shard_map.113.before
  105.7 0.1 collective-permute-done.14.s_there
  105.9 1.2 shard_map.114
  107.1 10.2 %all_to_all.103 = f32[8,96,128]{2,1,0:T(8,128)S(1)} all-to-all(f32[8,96,128]{2,1,0:T(8,128)S(1)} %bitcast.29), channel_id=1, replica_groups=mesh['chan'=8,'st'=8,'core'=2] {'st'}, dimensions={0} | all-to-all | bytes 786432 | tf_op jit(solution)/shard_map/all_to_all | solution.py:541
  117.3 0.2 shard_map.115
  117.5 1.9 %collective-permute-start.16 = (f32[1024,128]{1,0:T(8,128)S(1)}, f32[1024,128]{1,0:T(8,128)S(1)}, u32[]{:S(2)}, u32[]{:S(2)}) collective-permute-start(f32[1024,128]{1,0:T(8,128)S(1)} %get-tuple-element.120), channel_id=1, source_target_pairs={{0,1},{1,0},{2,3},{3,2},{4,5},{5,4},{6,7},{7,6},{8,9},{9,8},{10,11... | collective-permute-start | bytes 1572872 | tf_op jit(solution)/shard_map/ppermute | solution.py:538
  119.4 14.6 %all_to_all.104 = f32[16,32,128]{2,1,0:T(8,128)S(1)} all-to-all(f32[16,32,128]{2,1,0:T(8,128)S(1)} %bitcast.45), channel_id=1, replica_groups=mesh['chan'=8,'st'=8,'core'=2] {'chan','core'}, dimensions={0} | all-to-all | bytes 524288 | tf_op jit(solution)/shard_map/all_to_all | solution.py:541
  134.0 1.3 shard_map.116
  (22 shorter events, 0.1 us)
Async XLA Ops:
  0.6 9.1 %copy-start.1 = (bf16[1,32,8,1024]{3,2,1,0:T(8,128)(2,1)S(1)}, bf16[1,32,8,1024]{3,2,1,0:T(8,128)(2,1)}, u32[]{:S(2)}) copy-start(bf16[1,32,8,1024]{3,2,1,0:T(8,128)(2,1)} %param.7) | copy-start | bytes 1572868
  0.6 1.0 copy-start.4
  1.6 8.1 %copy-start.7 = (f32[32]{0:T(128)S(1)}, f32[32]{0:T(128)}, u32[]{:S(2)}) copy-start(f32[32]{0:T(128)} %param.13) | copy-start | bytes 388
  2.4 7.3 %copy-start = (s32[2,1024]{1,0:T(2,128)S(1)}, s32[2,1024]{1,0:T(2,128)}, u32[]{:S(2)}) copy-start(s32[2,1024]{1,0:T(2,128)} %pairs.17) | copy-start | bytes 24580
  2.4 7.3 %copy-start.5 = (f32[1,32,8,32]{3,2,1,0:T(8,128)S(1)}, f32[1,32,8,32]{3,2,1,0:T(8,128)}, u32[]{:S(2)}) copy-start(f32[1,32,8,32]{3,2,1,0:T(8,128)} %param.10) | copy-start | bytes 98308
  2.4 14.7 %all-to-all-start = ((f32[16,32,128]{2,1,0:T(8,128)}), f32[16,32,128]{2,1,0:T(8,128)S(1)}, u32[]{:S(2)}, u32[]{:S(2)}) async-start(f32[16,32,128]{2,1,0:T(8,128)} %bitcast.1), calls=%async_computation | async-start | bytes 524288 | tf_op jit(solution)/shard_map/all_to_all | solution.py:541
  9.8 1.0 copy-start.2
  10.8 0.9 copy-start.6
  11.7 5.4 %copy-start.3 = (f32[1,8,1024]{2,1,0:T(8,128)S(1)}, f32[1,8,1024]{2,1,0:T(8,128)}, u32[]{:S(2)}) copy-start(f32[1,8,1024]{2,1,0:T(8,128)} %param.8) | copy-start | bytes 98308
  13.4 5.4 %collective-permute-start = (f32[40,1024]{1,0:T(8,128)S(1)}, f32[40,1024]{1,0:T(8,128)S(1)}, u32[]{:S(2)}, u32[]{:S(2)}) collective-permute-start(f32[40,1024]{1,0:T(8,128)S(1)} %get-tuple-element.71), channel_id=1, source_target_pairs={{0,1},{1,0},{2,3},{3,2},{4,5},{5,4},{6,7},{7,6},{8,9},{9,8},{10,11... | collective-permute-start | bytes 491528 | tf_op jit(solution)/shard_map/ppermute | solution.py:538
  13.6 5.3 %collective-permute-start.1 = (f32[40,1024]{1,0:T(8,128)S(1)}, f32[40,1024]{1,0:T(8,128)S(1)}, u32[]{:S(2)}, u32[]{:S(2)}) collective-permute-start(f32[40,1024]{1,0:T(8,128)S(1)} %get-tuple-element.72), channel_id=1, source_target_pairs={{0,1},{1,0},{2,3},{3,2},{4,5},{5,4},{6,7},{7,6},{8,9},{9,8},{10,11... | collective-permute-start | bytes 491528 | tf_op jit(solution)/shard_map/ppermute | solution.py:538
  14.0 4.9 %collective-permute-start.2 = (f32[40,1024]{1,0:T(8,128)S(1)}, f32[40,1024]{1,0:T(8,128)S(1)}, u32[]{:S(2)}, u32[]{:S(2)}) collective-permute-start(f32[40,1024]{1,0:T(8,128)S(1)} %get-tuple-element.73), channel_id=1, source_target_pairs={{0,1},{1,0},{2,3},{3,2},{4,5},{5,4},{6,7},{7,6},{8,9},{9,8},{10,11... | collective-permute-start | bytes 491528 | tf_op jit(solution)/shard_map/ppermute | solution.py:538
  14.1 4.8 %collective-permute-start.3 = (f32[40,1024]{1,0:T(8,128)S(1)}, f32[40,1024]{1,0:T(8,128)S(1)}, u32[]{:S(2)}, u32[]{:S(2)}) collective-permute-start(f32[40,1024]{1,0:T(8,128)S(1)} %get-tuple-element.74), channel_id=1, source_target_pairs={{0,1},{1,0},{2,3},{3,2},{4,5},{5,4},{6,7},{7,6},{8,9},{9,8},{10,11... | collective-permute-start | bytes 491528 | tf_op jit(solution)/shard_map/ppermute | solution.py:538
  18.4 1.7 %collective-permute-start.5 = (f32[8,1024]{1,0:T(8,128)S(1)}, f32[8,1024]{1,0:T(8,128)S(1)}, u32[]{:S(2)}, u32[]{:S(2)}) collective-permute-start(f32[8,1024]{1,0:T(8,128)S(1)} %get-tuple-element.69.s_here), channel_id=1, source_target_pairs={{0,1},{1,0},{2,3},{3,2},{4,5},{5,4},{6,7},{7,6},{8,9},{9,8},{10,11... | collective-permute-start | bytes 98312 | tf_op jit(solution)/shard_map/ppermute | solution.py:538
  19.9 1.3 collective-permute-start.4
  42.2 4.1 %collective-permute-start.7 = (f32[8,1024]{1,0:T(8,128)S(1)}, f32[8,1024]{1,0:T(8,128)S(1)}, u32[]{:S(2)}, u32[]{:S(2)}) collective-permute-start(f32[8,1024]{1,0:T(8,128)S(1)} %get-tuple-element.85.s_here), channel_id=1, source_target_pairs={{0,1},{1,0},{2,3},{3,2},{4,5},{5,4},{6,7},{7,6},{8,9},{9,8},{10,11... | collective-permute-start | bytes 98312 | tf_op jit(solution)/shard_map/ppermute | solution.py:538
  46.1 1.5 %collective-permute-start.6 = (f32[8,1024]{1,0:T(8,128)S(1)}, f32[8,1024]{1,0:T(8,128)S(1)}, u32[]{:S(2)}, u32[]{:S(2)}) collective-permute-start(f32[8,1024]{1,0:T(8,128)S(1)} %get-tuple-element.87.s_here), channel_id=1, source_target_pairs={{0,1},{1,0},{2,3},{3,2},{4,5},{5,4},{6,7},{7,6},{8,9},{9,8},{10,11... | collective-permute-start | bytes 98312 | tf_op jit(solution)/shard_map/ppermute | solution.py:538
  59.7 9.2 %all-to-all-start.4 = ((f32[8,64,128]{2,1,0:T(8,128)}), f32[8,64,128]{2,1,0:T(8,128)S(1)}, u32[]{:S(2)}, u32[]{:S(2)}) async-start(f32[8,64,128]{2,1,0:T(8,128)} %bitcast.13), calls=%async_computation.4 | async-start | bytes 524288 | tf_op jit(solution)/shard_map/all_to_all | solution.py:541
  63.1 9.9 %collective-permute-start.8 = (f32[64,128]{1,0:T(8,128)S(1)}, f32[64,128]{1,0:T(8,128)S(1)}, u32[]{:S(2)}, u32[]{:S(2)}) collective-permute-start(f32[64,128]{1,0:T(8,128)S(1)} %get-tuple-element.97.moment), channel_id=1, source_target_pairs={{0,64},{16,80},{32,96},{48,112},{64,0},{80,16},{96,32},{112,48},{1... | collective-permute-start | bytes 98312 | tf_op jit(solution)/shard_map/ppermute | solution.py:607
  70.0 4.2 %collective-permute-start.10 = (f32[8,1024]{1,0:T(8,128)S(1)}, f32[8,1024]{1,0:T(8,128)S(1)}, u32[]{:S(2)}, u32[]{:S(2)}) collective-permute-start(f32[8,1024]{1,0:T(8,128)S(1)} %get-tuple-element.95.s_here), channel_id=1, source_target_pairs={{0,1},{1,0},{2,3},{3,2},{4,5},{5,4},{6,7},{7,6},{8,9},{9,8},{10,11... | collective-permute-start | bytes 98312 | tf_op jit(solution)/shard_map/ppermute | solution.py:538
  74.1 1.3 collective-permute-start.9
  77.3 11.6 %all-to-all-start.5 = ((f32[8,96,128]{2,1,0:T(8,128)}), f32[8,96,128]{2,1,0:T(8,128)S(1)}, u32[]{:S(2)}, u32[]{:S(2)}) async-start(f32[8,96,128]{2,1,0:T(8,128)} %bitcast.15), calls=%async_computation.5 | async-start | bytes 786432 | tf_op jit(solution)/shard_map/all_to_all | solution.py:541
  80.9 4.3 %collective-permute-start.11 = (f32[64,128]{1,0:T(8,128)S(1)}, f32[64,128]{1,0:T(8,128)S(1)}, u32[]{:S(2)}, u32[]{:S(2)}) collective-permute-start(f32[64,128]{1,0:T(8,128)S(1)} %get-tuple-element.104), channel_id=1, source_target_pairs={{0,32},{16,48},{32,0},{48,16},{64,96},{80,112},{96,64},{112,80},{1... | collective-permute-start | bytes 98312 | tf_op jit(solution)/shard_map/ppermute | solution.py:607
  83.9 4.3 %collective-permute-start.12 = (f32[64,128]{1,0:T(8,128)S(1)}, f32[64,128]{1,0:T(8,128)S(1)}, u32[]{:S(2)}, u32[]{:S(2)}) collective-permute-start(f32[64,128]{1,0:T(8,128)S(1)} %get-tuple-element.105), channel_id=1, source_target_pairs={{0,48},{16,32},{32,16},{48,0},{64,112},{80,96},{96,80},{112,64},{1... | collective-permute-start | bytes 98312 | tf_op jit(solution)/shard_map/ppermute | solution.py:607
  84.6 3.5 %collective-permute-start.13 = (f32[64,128]{1,0:T(8,128)S(1)}, f32[64,128]{1,0:T(8,128)S(1)}, u32[]{:S(2)}, u32[]{:S(2)}) collective-permute-start(f32[64,128]{1,0:T(8,128)S(1)} %get-tuple-element.106), channel_id=1, source_target_pairs={{0,16},{16,0},{32,48},{48,32},{64,80},{80,64},{96,112},{112,96},{1... | collective-permute-start | bytes 98312 | tf_op jit(solution)/shard_map/ppermute | solution.py:607
  99.7 4.9 %collective-permute-start.15 = (f32[8,1024]{1,0:T(8,128)S(1)}, f32[8,1024]{1,0:T(8,128)S(1)}, u32[]{:S(2)}, u32[]{:S(2)}) collective-permute-start(f32[8,1024]{1,0:T(8,128)S(1)} %get-tuple-element.110.s_here), channel_id=1, source_target_pairs={{0,1},{1,0},{2,3},{3,2},{4,5},{5,4},{6,7},{7,6},{8,9},{9,8},{10,11... | collective-permute-start | bytes 98312 | tf_op jit(solution)/shard_map/ppermute | solution.py:538
  104.4 1.5 %collective-permute-start.14 = (f32[8,1024]{1,0:T(8,128)S(1)}, f32[8,1024]{1,0:T(8,128)S(1)}, u32[]{:S(2)}, u32[]{:S(2)}) collective-permute-start(f32[8,1024]{1,0:T(8,128)S(1)} %get-tuple-element.112.s_here), channel_id=1, source_target_pairs={{0,1},{1,0},{2,3},{3,2},{4,5},{5,4},{6,7},{7,6},{8,9},{9,8},{10,11... | collective-permute-start | bytes 98312 | tf_op jit(solution)/shard_map/ppermute | solution.py:538
  117.5 16.6 %collective-permute-start.16 = (f32[1024,128]{1,0:T(8,128)S(1)}, f32[1024,128]{1,0:T(8,128)S(1)}, u32[]{:S(2)}, u32[]{:S(2)}) collective-permute-start(f32[1024,128]{1,0:T(8,128)S(1)} %get-tuple-element.120), channel_id=1, source_target_pairs={{0,1},{1,0},{2,3},{3,2},{4,5},{5,4},{6,7},{7,6},{8,9},{9,8},{10,11... | collective-permute-start | bytes 1572872 | tf_op jit(solution)/shard_map/ppermute | solution.py:538
